TPU v7x, 32 devices: a whole 2x2x4 slice. The times are simulated.
32 devices in a mesh: test: 2 (over core), slab: 16 (over z, y, x).
Axes of the slice: x: 2, y: 2, z: 4, core: 2. Of those that a mesh axis runs over, the one named last changes fastest.
Arguments:
- log_conductivity: float32 [32, 512, 128], P('slab'), may hold values from -4 to 4
- storage: float32 [32, 512, 128], P('slab'), may hold values from 0.1 to 1
- active_mask: int32 [32, 512, 128], P('slab'), may hold values 0 or 1
- heads: float32 [2, 32, 512, 128], P('test', 'slab'), may hold values from -6 to 6
- adjoint_next: float32 [2, 32, 512, 128], P('test', 'slab'), may hold values from -6 to 6
- pump_cells: int32 [2], P('test'), may hold values from 0 to 2097151
- obs_cells: int32 [64], replicated, may hold values from 0 to 2097151
- obs_data: float32 [2, 64], P('test'), may hold values from -6 to 6
Outputs:
- adjoint: float32 [2, 32, 512, 128], P('test', 'slab')
- gradient: float32 [32, 512, 128], P('slab')
All inputs are finite; a program needn't handle non-finite values. No bound on the sum of `active_mask` on one device may be relied on, other than what follows from the above.
Results may differ from a plain program's by a relative error of at most 0.0003.
Values sent between devices are 32-bit elements; how exact they have to be, the bound alone decides.
No kernel may reach another device: no remote copies, remote signals or barrier semaphores. Data moves between devices by JAX's collectives and lax.ppermute only.
A program may use at most 64 MiB of HBM per device.

v0:
```python
import jax
import jax.numpy as jnp
from jax import lax
from jax.sharding import PartitionSpec as P

ITERS = 3


WELL_TERM = 4.0


def padded_2(cells, sides, width):
    for axis, dim in sides:
        count = lax.axis_size(axis)
        ends = count - 1
        head = lax.slice_in_dim(cells, 0, width, axis=dim)
        tail = lax.slice_in_dim(cells, cells.shape[dim] - width, cells.shape[dim], axis=dim)
        cells = jnp.concatenate(
            [
                lax.ppermute(tail, axis, [(i, (i + 1) % count) for i in range(ends)]),
                cells,
                lax.ppermute(head, axis, [((i + 1) % count, i) for i in range(ends)]),
            ],
            axis=dim,
        )
    return cells


def part_of(v, axis_num, start, length):
    return lax.slice_in_dim(v, start, start + length, axis=axis_num)


def pad_axis(v, axis_num):
    widths = [(0, 0)] * v.ndim
    widths[axis_num] = (1, 1)
    return jnp.pad(v, widths)


def face_values(cond_pad, axis_num):
    count = cond_pad.shape[axis_num] - 1
    left = part_of(cond_pad, axis_num, 0, count)
    right = part_of(cond_pad, axis_num, 1, count)
    return 2.0 * left * right / (left + right)


def flux_axis(padded, faces, axis_num):
    count = padded.shape[axis_num] - 1
    terms = faces * (part_of(padded, axis_num, 0, count) - part_of(padded, axis_num, 1, count))
    return part_of(terms, axis_num, 1, count - 1) - part_of(terms, axis_num, 0, count - 1)


def face_total(faces, axis_num):
    count = faces.shape[axis_num] - 1
    return part_of(faces, axis_num, 1, count) + part_of(faces, axis_num, 0, count)


def slope(own, other):
    total = own + other
    return 2.0 * own * other * other / (total * total)


def side_terms(cond_pad, adj_pad, head_pad, axis_num):
    count = cond_pad.shape[axis_num] - 2
    cond_c = part_of(cond_pad, axis_num, 1, count)
    adj_c = part_of(adj_pad, axis_num, 1, count)
    head_c = part_of(head_pad, axis_num, 1, count)
    total = jnp.zeros(cond_c.shape, jnp.float32)
    for start in (0, 2):
        cond_n = part_of(cond_pad, axis_num, start, count)
        adj_n = part_of(adj_pad, axis_num, start, count)
        head_n = part_of(head_pad, axis_num, start, count)
        total = total + slope(cond_c, cond_n) * (adj_c - adj_n) * (head_c - head_n)
    return total


def operate(field, faces, self_term, active):
    field_x = padded_2(field, (("slab", 0),), 1)
    flux = flux_axis(field_x, faces[0], 0)
    flux = flux + flux_axis(pad_axis(field, 1), faces[1], 1)
    flux = flux + flux_axis(pad_axis(field, 2), faces[2], 2)
    return (active * (self_term * field + flux) + (1.0 - active) * field, field_x)


def precond_inner(resid, precond):
    return lax.psum(jnp.sum(resid * precond), "slab")


def on_device(
    log_conductivity, storage, active_mask, heads, adjoint_next, pump_cells, obs_cells, obs_data
):
    width, rows, depth = log_conductivity.shape
    conduct = jnp.exp(log_conductivity)
    active = active_mask.astype(jnp.float32)
    heads_here = heads[0]
    later = adjoint_next[0]
    stacked = padded_2(jnp.stack([conduct, heads_here]), (("slab", 1),), 1)
    cond_x = stacked[0]
    heads_x = stacked[1]
    cond_y = pad_axis(conduct, 1)
    cond_z = pad_axis(conduct, 2)
    faces = (face_values(cond_x, 0), face_values(cond_y, 1), face_values(cond_z, 2))
    face_sum = face_total(faces[0], 0) + face_total(faces[1], 1) + face_total(faces[2], 2)
    shape = (width, rows, depth)
    cells_here = width * rows * depth
    offset = lax.axis_index("slab") * cells_here
    local_index = (
        lax.broadcasted_iota(jnp.int32, shape, 0) * (rows * depth)
        + lax.broadcasted_iota(jnp.int32, shape, 1) * depth
        + lax.broadcasted_iota(jnp.int32, shape, 2)
    )
    well = jnp.where(local_index == pump_cells[0] - offset, WELL_TERM, 0.0).astype(jnp.float32)
    self_term = storage + well
    diag = active * (self_term + face_sum) + (1.0 - active)
    obs_local = obs_cells - offset
    inside = (obs_local >= 0) & (obs_local < cells_here)
    safe_index = jnp.where(inside, obs_local, 0)
    picked = heads_here.reshape(-1)[safe_index]
    values = jnp.where(inside, picked - obs_data[0], 0.0)
    misfit = jnp.zeros((cells_here,), jnp.float32).at[safe_index].add(values).reshape(shape)
    rhs = active * (storage * later + misfit)
    solution = jnp.zeros_like(rhs)
    resid = rhs
    low_rim = jnp.zeros((rows, depth), jnp.float32)
    high_rim = jnp.zeros((rows, depth), jnp.float32)
    precond = resid / diag
    direction = precond
    rz_now = precond_inner(resid, precond)
    for step in range(ITERS):
        image, dir_x = operate(direction, faces, self_term, active)
        alpha = rz_now / lax.psum(jnp.sum(direction * image), "slab")
        solution = solution + alpha * direction
        low_rim = low_rim + alpha * dir_x[0]
        high_rim = high_rim + alpha * dir_x[-1]
        resid = resid - alpha * image
        if step + 1 < ITERS:
            precond = resid / diag
            rz_next = precond_inner(resid, precond)
            direction = precond + rz_next / rz_now * direction
            rz_now = rz_next
    solution_x = padded_2(solution, (("slab", 0),), 1)
    terms = side_terms(cond_x, solution_x, heads_x, 0)
    terms = terms + side_terms(cond_y, pad_axis(solution, 1), pad_axis(heads_here, 1), 1)
    terms = terms + side_terms(cond_z, pad_axis(solution, 2), pad_axis(heads_here, 2), 2)
    gradient = lax.psum(-terms, "test")
    return (solution[None], gradient)


def solution(mesh):
    return jax.shard_map(
        on_device,
        mesh=mesh,
        in_specs=(
            P("slab", None, None),
            P("slab", None, None),
            P("slab", None, None),
            P("test", "slab", None, None),
            P("test", "slab", None, None),
            P("test"),
            P(),
            P("test", None),
        ),
        out_specs=(P("test", "slab", None, None), P("slab", None, None)),
        check_vma=False,
    )
```

profile of v0, /device:TPU:1, one launch (start us, length us, event | category | flops | bytes accessed | tf_op | source)
XLA Modules:
  0.0 330.2 jit_solution(15330560122750045655)
XLA Ops:
  7.2 1.2 exponential_bitcast_fusion
  9.3 4.0 %collective-permute-start = (f32[2,1,512,128]{3,2,1,0:T(8,128)}, f32[2,1,512,128]{3,2,1,0:T(8,128)S(1)}, u32[]{:S(2)}, u32[]{:S(2)}) collective-permute-start(f32[2,1,512,128]{3,2,1,0:T(8,128)} %get-tuple-element.17), channel_id=1, source_target_pairs={{0,1},{1,2},{2,3},{3,4},{4,5},{5,6},{6,7},{7,8},{8,9},{9,10},{10,1... | collective-permute-start | bytes 1572872 | tf_op jit(solution)/shard_map/ppermute | solution.py:20
  13.3 1.3 collective-permute-start.1
  16.0 1.8 scatter_custom_fusion
  18.3 17.0 %collective-permute-done = f32[2,1,512,128]{3,2,1,0:T(8,128)S(1)} collective-permute-done((f32[2,1,512,128]{3,2,1,0:T(8,128)}, f32[2,1,512,128]{3,2,1,0:T(8,128)S(1)}, u32[]{:S(2)}, u32[]{:S(2)}) %collective-permute-start) | collective-permute-done | bytes 524320 | tf_op jit(solution)/shard_map/ppermute | solution.py:20
  35.3 1.8 collective-permute-done.1
  40.6 1.3 collective-permute-start.3
  41.9 4.0 %collective-permute-start.2 = (f32[1,512,128]{2,1,0:T(8,128)S(1)}, f32[1,512,128]{2,1,0:T(8,128)S(1)}, u32[]{:S(2)}, u32[]{:S(2)}) collective-permute-start(f32[1,512,128]{2,1,0:T(8,128)S(1)} %get-tuple-element.26), channel_id=1, source_target_pairs={{0,1},{1,2},{2,3},{3,4},{4,5},{5,6},{6,7},{7,8},{8,9},{9,10},{10,1... | collective-permute-start | bytes 786440 | tf_op jit(solution)/shard_map/ppermute | solution.py:20
  46.8 2.0 collective-permute-done.3
  48.8 6.4 %collective-permute-done.2 = f32[1,512,128]{2,1,0:T(8,128)S(1)} collective-permute-done((f32[1,512,128]{2,1,0:T(8,128)S(1)}, f32[1,512,128]{2,1,0:T(8,128)S(1)}, u32[]{:S(2)}, u32[]{:S(2)}) %collective-permute-start.2) | collective-permute-done | bytes 262176 | tf_op jit(solution)/shard_map/ppermute | solution.py:20
  55.4 2.0 multiply_reduce_fusion.3
  57.3 34.8 %all-reduce.12 = (f32[]{:T(128)}, f32[]{:T(128)}) all-reduce(f32[]{:T(128)} %get-tuple-element.3, f32[]{:T(128)} %get-tuple-element.2), channel_id=1, replica_groups=mesh['test'=2,'slab'=16] {'slab'}, use_global_device_ids=true, to_apply=%region_2.3 | all-reduce | flops 2 | bytes 16 | tf_op jit(solution)/shard_map/psum | solution.py:85
  93.5 2.7 multiply_reduce_fusion.2
  96.2 30.3 %psum.51 = f32[]{:T(128)} all-reduce(f32[]{:T(128)} %get-tuple-element.8), channel_id=1, replica_groups=mesh['test'=2,'slab'=16] {'slab'}, use_global_device_ids=true, to_apply=%region_6.7 | all-reduce | flops 1 | bytes 8 | tf_op jit(solution)/shard_map/psum | solution.py:85
  129.0 1.3 collective-permute-start.5
  130.3 4.0 %collective-permute-start.4 = (f32[1,512,128]{2,1,0:T(8,128)S(1)}, f32[1,512,128]{2,1,0:T(8,128)S(1)}, u32[]{:S(2)}, u32[]{:S(2)}) collective-permute-start(f32[1,512,128]{2,1,0:T(8,128)S(1)} %get-tuple-element.24), channel_id=1, source_target_pairs={{0,1},{1,2},{2,3},{3,4},{4,5},{5,6},{6,7},{7,8},{8,9},{9,10},{10,1... | collective-permute-start | bytes 786440 | tf_op jit(solution)/shard_map/ppermute | solution.py:20
  136.1 1.5 collective-permute-done.4
  137.8 1.9 multiply_reduce_fusion.1
  139.7 32.7 %psum.52 = f32[]{:T(128)} all-reduce(f32[]{:T(128)} %get-tuple-element.6), channel_id=1, replica_groups=mesh['test'=2,'slab'=16] {'slab'}, use_global_device_ids=true, to_apply=%region_8.9 | all-reduce | flops 1 | bytes 8 | tf_op jit(solution)/shard_map/psum | solution.py:130
  173.6 2.0 multiply_reduce_fusion
  175.6 30.3 %psum.53 = f32[]{:T(128)} all-reduce(f32[]{:T(128)} %multiply_reduce_fusion), channel_id=1, replica_groups=mesh['test'=2,'slab'=16] {'slab'}, use_global_device_ids=true, to_apply=%region_10.11 | all-reduce | flops 1 | bytes 8 | tf_op jit(solution)/shard_map/psum | solution.py:85
  207.3 1.5 multiply_add_fusion.1
  208.8 1.3 collective-permute-start.7
  210.1 4.0 %collective-permute-start.6 = (f32[1,512,128]{2,1,0:T(8,128)S(1)}, f32[1,512,128]{2,1,0:T(8,128)S(1)}, u32[]{:S(2)}, u32[]{:S(2)}) collective-permute-start(f32[1,512,128]{2,1,0:T(8,128)S(1)} %get-tuple-element.22), channel_id=1, source_target_pairs={{0,1},{1,2},{2,3},{3,4},{4,5},{5,6},{6,7},{7,8},{8,9},{9,10},{10,1... | collective-permute-start | bytes 786440 | tf_op jit(solution)/shard_map/ppermute | solution.py:20
  214.9 1.4 collective-permute-done.7
  218.6 32.6 %psum.54 = f32[]{:T(128)} all-reduce(f32[]{:T(128)} %fusion.46), channel_id=1, replica_groups=mesh['test'=2,'slab'=16] {'slab'}, use_global_device_ids=true, to_apply=%region_12.13 | all-reduce | flops 1 | bytes 8 | tf_op jit(solution)/shard_map/psum | solution.py:130
  252.8 1.9 collective-permute-start.8
  254.7 1.3 collective-permute-start.9
  256.0 4.9 %collective-permute-done.8 = f32[1,512,128]{2,1,0:T(8,128)S(1)} collective-permute-done((f32[1,512,128]{2,1,0:T(8,128)S(1)}, f32[1,512,128]{2,1,0:T(8,128)S(1)}, u32[]{:S(2)}, u32[]{:S(2)}) %collective-permute-start.8) | collective-permute-done | bytes 262176 | tf_op jit(solution)/shard_map/ppermute | solution.py:20
  261.9 2.3 fusion.65
  264.3 57.2 %all-reduce.15.cloned.1.call-done = f32[2,512,128]{2,1,0:T(8,128)} async-done(((f32[2,512,128]{2,1,0:T(8,128)}), f32[2,512,128]{2,1,0:T(8,128)}) %all-reduce.15.cloned.1.call-update) | async-done | bytes 524304 | tf_op jit(solution)/shard_map/psum | solution.py:144
  321.5 1.9 copy.12
  (67 shorter events, 13.8 us)
Async XLA Ops:
  7.2 1.2 copy-start
  7.2 7.4 %copy-start.15 = (s32[64]{0:T(128)S(1)}, s32[64]{0:T(128)}, u32[]{:S(2)}) copy-start(s32[64]{0:T(128)} %param.14) | copy-start | bytes 772
  7.2 314.3 %all-reduce.15.cloned.1.call-start = ((), (), s32[]{:S(2)}) async-start(), calls=%async_computation | async-start | bytes 1048576 | tf_op jit(solution)/shard_map/psum | solution.py:144
  8.4 7.0 %copy-start.16 = (f32[1,64]{1,0:T(1,128)S(1)}, f32[1,64]{1,0:T(1,128)}, u32[]{:S(2)}) copy-start(f32[1,64]{1,0:T(1,128)} %param.15) | copy-start | bytes 772
  9.3 26.1 %collective-permute-start = (f32[2,1,512,128]{3,2,1,0:T(8,128)}, f32[2,1,512,128]{3,2,1,0:T(8,128)S(1)}, u32[]{:S(2)}, u32[]{:S(2)}) collective-permute-start(f32[2,1,512,128]{3,2,1,0:T(8,128)} %get-tuple-element.17), channel_id=1, source_target_pairs={{0,1},{1,2},{2,3},{3,4},{4,5},{5,6},{6,7},{7,8},{8,9},{9,10},{10,1... | collective-permute-start | bytes 1572872 | tf_op jit(solution)/shard_map/ppermute | solution.py:20
  13.3 23.9 %collective-permute-start.1 = (f32[2,1,512,128]{3,2,1,0:T(8,128)S(1)}, f32[2,1,512,128]{3,2,1,0:T(8,128)S(1)}, u32[]{:S(2)}, u32[]{:S(2)}) collective-permute-start(f32[2,1,512,128]{3,2,1,0:T(8,128)S(1)} %get-tuple-element.18), channel_id=1, source_target_pairs={{1,0},{2,1},{3,2},{4,3},{5,4},{6,5},{7,6},{8,7},{9,8},{10,9},{11,1... | collective-permute-start | bytes 1572872 | tf_op jit(solution)/shard_map/ppermute | solution.py:22
  37.4 1.2 copy-start.8
  37.4 3.2 copy-start.10
  37.4 1.4 copy-start.2
  37.4 2.0 copy-start.5
  37.4 2.5 copy-start.13
  37.5 2.6 copy-start.14
  40.6 133.0 %copy-start.1 = (f32[2,512,128]{2,1,0:T(8,128)}, f32[2,512,128]{2,1,0:T(8,128)S(1)}, u32[]{:S(2)}) copy-start(f32[2,512,128]{2,1,0:T(8,128)S(1)} %get-tuple-element.13) | copy-start | bytes 1572868
  40.6 8.1 %collective-permute-start.3 = (f32[1,512,128]{2,1,0:T(8,128)S(1)}, f32[1,512,128]{2,1,0:T(8,128)S(1)}, u32[]{:S(2)}, u32[]{:S(2)}) collective-permute-start(f32[1,512,128]{2,1,0:T(8,128)S(1)} %get-tuple-element.25), channel_id=1, source_target_pairs={{1,0},{2,1},{3,2},{4,3},{5,4},{6,5},{7,6},{8,7},{9,8},{10,9},{11,1... | collective-permute-start | bytes 786440 | tf_op jit(solution)/shard_map/ppermute | solution.py:22
  41.9 13.3 %collective-permute-start.2 = (f32[1,512,128]{2,1,0:T(8,128)S(1)}, f32[1,512,128]{2,1,0:T(8,128)S(1)}, u32[]{:S(2)}, u32[]{:S(2)}) collective-permute-start(f32[1,512,128]{2,1,0:T(8,128)S(1)} %get-tuple-element.26), channel_id=1, source_target_pairs={{0,1},{1,2},{2,3},{3,4},{4,5},{5,6},{6,7},{7,8},{8,9},{9,10},{10,1... | collective-permute-start | bytes 786440 | tf_op jit(solution)/shard_map/ppermute | solution.py:20
  129.0 7.1 %collective-permute-start.5 = (f32[1,512,128]{2,1,0:T(8,128)S(1)}, f32[1,512,128]{2,1,0:T(8,128)S(1)}, u32[]{:S(2)}, u32[]{:S(2)}) collective-permute-start(f32[1,512,128]{2,1,0:T(8,128)S(1)} %get-tuple-element.23), channel_id=1, source_target_pairs={{1,0},{2,1},{3,2},{4,3},{5,4},{6,5},{7,6},{8,7},{9,8},{10,9},{11,1... | collective-permute-start | bytes 786440 | tf_op jit(solution)/shard_map/ppermute | solution.py:22
  130.3 7.3 %collective-permute-start.4 = (f32[1,512,128]{2,1,0:T(8,128)S(1)}, f32[1,512,128]{2,1,0:T(8,128)S(1)}, u32[]{:S(2)}, u32[]{:S(2)}) collective-permute-start(f32[1,512,128]{2,1,0:T(8,128)S(1)} %get-tuple-element.24), channel_id=1, source_target_pairs={{0,1},{1,2},{2,3},{3,4},{4,5},{5,6},{6,7},{7,8},{8,9},{9,10},{10,1... | collective-permute-start | bytes 786440 | tf_op jit(solution)/shard_map/ppermute | solution.py:20
  135.1 2.6 copy-start.3
  135.1 2.6 copy-start.6
  208.8 7.6 %collective-permute-start.7 = (f32[1,512,128]{2,1,0:T(8,128)S(1)}, f32[1,512,128]{2,1,0:T(8,128)S(1)}, u32[]{:S(2)}, u32[]{:S(2)}) collective-permute-start(f32[1,512,128]{2,1,0:T(8,128)S(1)} %get-tuple-element.21), channel_id=1, source_target_pairs={{1,0},{2,1},{3,2},{4,3},{5,4},{6,5},{7,6},{8,7},{9,8},{10,9},{11,1... | collective-permute-start | bytes 786440 | tf_op jit(solution)/shard_map/ppermute | solution.py:22
  210.1 7.3 %collective-permute-start.6 = (f32[1,512,128]{2,1,0:T(8,128)S(1)}, f32[1,512,128]{2,1,0:T(8,128)S(1)}, u32[]{:S(2)}, u32[]{:S(2)}) collective-permute-start(f32[1,512,128]{2,1,0:T(8,128)S(1)} %get-tuple-element.22), channel_id=1, source_target_pairs={{0,1},{1,2},{2,3},{3,4},{4,5},{5,6},{6,7},{7,8},{8,9},{9,10},{10,1... | collective-permute-start | bytes 786440 | tf_op jit(solution)/shard_map/ppermute | solution.py:20
  214.9 2.7 copy-start.4
  214.9 2.7 copy-start.7
  252.6 9.3 %copy-start.9 = (f32[2,3,512,128]{3,2,1,0:T(8,128)S(1)}, f32[2,3,512,128]{3,2,1,0:T(8,128)}, u32[]{:S(2)}) copy-start(f32[2,3,512,128]{3,2,1,0:T(8,128)} %copy-done.8) | copy-start | bytes 4718596
  252.6 9.3 %copy-start.11 = (f32[2,3,512,128]{3,2,1,0:T(8,128)S(1)}, f32[2,3,512,128]{3,2,1,0:T(8,128)}, u32[]{:S(2)}) copy-start(f32[2,3,512,128]{3,2,1,0:T(8,128)} %copy-done.10) | copy-start | bytes 4718596
  252.7 11.5 %copy-start.12 = (f32[2,512,128]{2,1,0:T(8,128)}, f32[2,512,128]{2,1,0:T(8,128)S(1)}, u32[]{:S(2)}) copy-start(f32[2,512,128]{2,1,0:T(8,128)S(1)} %multiply_add_fusion) | copy-start | bytes 1572868
  252.8 8.1 %collective-permute-start.8 = (f32[1,512,128]{2,1,0:T(8,128)S(1)}, f32[1,512,128]{2,1,0:T(8,128)S(1)}, u32[]{:S(2)}, u32[]{:S(2)}) collective-permute-start(f32[1,512,128]{2,1,0:T(8,128)S(1)} %get-tuple-element.19), channel_id=1, source_target_pairs={{0,1},{1,2},{2,3},{3,4},{4,5},{5,6},{6,7},{7,8},{8,9},{9,10},{10,1... | collective-permute-start | bytes 786440 | tf_op jit(solution)/shard_map/ppermute | solution.py:20
  254.7 7.2 %collective-permute-start.9 = (f32[1,512,128]{2,1,0:T(8,128)S(1)}, f32[1,512,128]{2,1,0:T(8,128)S(1)}, u32[]{:S(2)}, u32[]{:S(2)}) collective-permute-start(f32[1,512,128]{2,1,0:T(8,128)S(1)} %get-tuple-element.20), channel_id=1, source_target_pairs={{1,0},{2,1},{3,2},{4,3},{5,4},{6,5},{7,6},{8,7},{9,8},{10,9},{11,1... | collective-permute-start | bytes 786440 | tf_op jit(solution)/shard_map/ppermute | solution.py:22
Sparse Core Ops, SparseCore 0:
  264.4 57.0 all-reduce.14
where the time goes:
time: 331 us; the launch traced here: 330 us
  blocking collectives  161 us (49%)
  waiting for transfers between devices  95.4 us (29%)
  starting transfers between devices  24.4 us (7%)
  between operations  21.8 us (7%)
  other arithmetic  21.5 us (6%)
  local copies, waits for them, and re-layouts  6.49 us (2%)
    psum x3, blocking collectives, precond_inner(): return lax.psum(jnp.sum(resid * precond), 'slab')  95.4 us
    psum x2, blocking collectives, on_device(): alpha = rz_now / lax.psum(jnp.sum(direction * image), 'slab')  65.3 us
    psum x1, waiting for transfers between devices, on_device(): gradient = lax.psum(-terms, 'test')  57.2 us
    ppermute x5, waiting for transfers between devices, padded_2(): lax.ppermute(tail, axis, [(i, (i + 1) % count) for i in range(ends)])  30.8 us
    ppermute x5, starting transfers between devices, padded_2(): lax.ppermute(tail, axis, [(i, (i + 1) % count) for i in range(ends)])  17.9 us
    ppermute x5, waiting for transfers between devices, padded_2(): lax.ppermute(head, axis, [((i + 1) % count, i) for i in range(ends)])  7.29 us
  transfers between devices with their start and end apart: 11, of which 11 were waited for; matrix products, arithmetic and copies ran while one was open for 2% of the time, Pallas kernels for 0%

commit v1 on v0

v1 whole, which is shorter than its diff:
```python
import jax
import jax.numpy as jnp
from jax import lax
from jax.sharding import PartitionSpec as P

WELL_TERM = 4.0


def face_value(a, b):
    return 2.0 * a * b / (a + b)


def slope(own, other):
    total = own + other
    return 2.0 * own * other * other / (total * total)


def shift_down(v, axis):
    widths = [(0, 0)] * v.ndim
    widths[axis] = (1, 0)
    return lax.slice_in_dim(jnp.pad(v, widths), 0, v.shape[axis], axis=axis)


def shift_up(v, axis):
    widths = [(0, 0)] * v.ndim
    widths[axis] = (0, 1)
    return lax.slice_in_dim(jnp.pad(v, widths), 1, v.shape[axis] + 1, axis=axis)


def to_neighbours(low, high):
    count = lax.axis_size("slab")
    before = lax.ppermute(high, "slab", [(i, i + 1) for i in range(count - 1)])
    after = lax.ppermute(low, "slab", [(i + 1, i) for i in range(count - 1)])
    return before, after


def combine(moments, least):
    m0, m1, m2, m3, m4, m5 = moments
    most = 2.0 - least
    alpha_low, alpha_high = 1.0 / most, 1.0 / least
    beta_high = (1.0 - least) * (1.0 - least) / (least * most)

    def alpha_of(rz, curve):
        return jnp.clip(jnp.where(curve > 0.0, rz / curve, alpha_low), alpha_low, alpha_high)

    def beta_of(rz_new, rz):
        return jnp.clip(jnp.where(rz > 0.0, rz_new / rz, 0.0), 0.0, beta_high)

    a0 = alpha_of(m0, m1)
    rz1 = m0 - 2.0 * a0 * m1 + a0 * a0 * m2
    b0 = beta_of(rz1, m0)
    u = 1.0 + b0
    curve1 = u * u * m1 - 2.0 * a0 * u * m2 + a0 * a0 * m3
    a1 = alpha_of(rz1, curve1)
    c1 = -a0 - a1 * u
    c2 = a0 * a1
    rz2 = m0 + 2.0 * c1 * m1 + (2.0 * c2 + c1 * c1) * m2 + 2.0 * c1 * c2 * m3 + c2 * c2 * m4
    b1 = beta_of(rz2, rz1)
    q0 = 1.0 + b1 * u
    q1 = c1 - b1 * a0
    q2 = c2
    curve2 = q0 * q0 * m1 + 2.0 * q0 * q1 * m2 + (2.0 * q0 * q2 + q1 * q1) * m3 + 2.0 * q1 * q2 * m4 + q2 * q2 * m5
    a2 = alpha_of(rz2, curve2)
    return a0 + a1 * u + a2 * q0, a2 * q1 - a1 * a0, a2 * q2


def on_device(
    log_conductivity, storage, active_mask, heads, adjoint_next, pump_cells, obs_cells, obs_data
):
    width, rows, depth = log_conductivity.shape
    slabs = lax.axis_size("slab")
    place = lax.axis_index("slab")
    has_before = place > 0
    has_after = place < slabs - 1
    logs = [log_conductivity[i] for i in range(width)]
    log_before, log_after = to_neighbours(logs[0], logs[-1])
    head = [heads[0, i] for i in range(width)]
    head_before, head_after = to_neighbours(head[0], head[-1])

    cond = [jnp.exp(v) for v in logs]
    cond_before = jnp.where(has_before, jnp.exp(log_before), 0.0)
    cond_after = jnp.where(has_after, jnp.exp(log_after), 0.0)
    active = [active_mask[i].astype(jnp.float32) for i in range(width)]

    row_ids = lax.broadcasted_iota(jnp.int32, (rows, depth), 0)
    lane_ids = lax.broadcasted_iota(jnp.int32, (rows, depth), 1)
    cond_pad = [cond_before, *cond, cond_after]
    face_x = [face_value(cond_pad[i], cond_pad[i + 1]) for i in range(width + 1)]
    face_y = [jnp.where(row_ids > 0, face_value(shift_down(c, 0), c), 0.0) for c in cond]
    face_z = [jnp.where(lane_ids > 0, face_value(shift_down(c, 1), c), 0.0) for c in cond]
    face_sum = [
        face_x[i] + face_x[i + 1] + face_y[i] + shift_up(face_y[i], 0) + face_z[i] + shift_up(face_z[i], 1)
        for i in range(width)
    ]

    cells_here = width * rows * depth
    offset = place * cells_here
    pump_local = pump_cells[0] - offset
    cell_ids = row_ids * depth + lane_ids
    self_term = [
        storage[i] + jnp.where(cell_ids + i * rows * depth == pump_local, WELL_TERM, 0.0).astype(jnp.float32)
        for i in range(width)
    ]
    diag = [active[i] * (self_term[i] + face_sum[i]) + (1.0 - active[i]) for i in range(width)]
    ratio = [jnp.where(active[i] > 0.0, self_term[i] / diag[i], 1.0) for i in range(width)]

    obs_local = obs_cells - offset
    inside = (obs_local >= 0) & (obs_local < cells_here)
    safe_index = jnp.where(inside, obs_local, 0)
    picked = heads[0].reshape(-1)[safe_index]
    values = jnp.where(inside, picked - obs_data[0], 0.0)
    misfit = jnp.zeros((cells_here,), jnp.float32).at[safe_index].add(values).reshape(width, rows, depth)
    rhs = [active[i] * (storage[i] * adjoint_next[0, i] + misfit[i]) for i in range(width)]

    def apply(field, before, after):
        pad = [before, *field, after]
        flux_x = [face_x[i] * (pad[i] - pad[i + 1]) for i in range(width + 1)]
        image = []
        for i in range(width):
            v = field[i]
            flux_y = face_y[i] * (shift_down(v, 0) - v)
            flux_z = face_z[i] * (shift_down(v, 1) - v)
            flux = flux_x[i + 1] - flux_x[i] + shift_up(flux_y, 0) - flux_y + shift_up(flux_z, 1) - flux_z
            image.append(active[i] * (self_term[i] * v + flux))
        return image

    def dot(xs, ys):
        return sum(jnp.sum(x * y, axis=0) for x, y in zip(xs, ys))

    field = [rhs[i] / diag[i] for i in range(width)]
    weighted = rhs
    fields, sums = [], []
    for step in range(3):
        before, after = to_neighbours(field[0], field[-1])
        fields.append([before, *field, after])
        sums.append(dot(field, weighted))
        image = apply(field, before, after)
        sums.append(dot(field, image))
        weighted = image
        field = [image[i] / diag[i] for i in range(width)]
    least = jnp.min(jnp.stack(ratio), axis=(0, 1))
    payload = jnp.stack([*sums, least, least])
    gathered = lax.all_to_all(
        jnp.broadcast_to(payload[None], (slabs, *payload.shape)), "slab", 0, 0, tiled=True
    )
    totals = jnp.sum(jnp.sum(gathered, axis=0), axis=1)
    coefs = combine([totals[i] for i in range(6)], jnp.min(gathered[:, 6]))
    adjoint = [sum(c * f[i] for c, f in zip(coefs, fields)) for i in range(width + 2)]

    head_pad = [head_before, *head, head_after]
    terms = []
    for i in range(width):
        c, a, h = cond[i], adjoint[i + 1], head[i]
        total = jnp.zeros_like(c)
        for j in (i, i + 2):
            total = total + slope(c, cond_pad[j]) * (a - adjoint[j]) * (h - head_pad[j])
        for axis in (0, 1):
            for shift in (shift_down, shift_up):
                total = total + slope(c, shift(c, axis)) * (a - shift(a, axis)) * (h - shift(h, axis))
        terms.append(total)
    terms = -jnp.stack(terms)
    if lax.axis_size("test") == 2:
        gradient = terms + lax.ppermute(terms, "test", [(0, 1), (1, 0)])
    else:
        gradient = lax.psum(terms, "test")
    return jnp.stack(adjoint[1:-1])[None], gradient


def solution(mesh):
    return jax.shard_map(
        on_device,
        mesh=mesh,
        in_specs=(
            P("slab", None, None),
            P("slab", None, None),
            P("slab", None, None),
            P("test", "slab", None, None),
            P("test", "slab", None, None),
            P("test"),
            P(),
            P("test", None),
        ),
        out_specs=(P("test", "slab", None, None), P("slab", None, None)),
        check_vma=False,
    )
```

time: 331 us -> 106 us (0.32)
  blocking collectives: 161 us -> 0 us
  waiting for transfers between devices: 95.4 us -> 20.2 us
  starting transfers between devices: 24.4 us -> 45.4 us
  other arithmetic: 21.5 us -> 12.9 us
  between operations: 21.8 us -> 17 us
    psum x5 -> x0, blocking collectives: 161 us -> none  [the longest x3 95.4 us: precond_inner(): return lax.psum(jnp.sum(resid * precond), 'slab')]
    psum x1 -> x0, waiting for transfers between devices: 57.2 us -> none  [on_device(): gradient = lax.psum(-terms, 'test')]
    ppermute x10 -> x11, waiting for transfers between devices: 38.1 us -> 19.8 us  [the longest x5 10.2 us: to_neighbours(): after = lax.ppermute(low, 'slab', [(i + 1, i) for i in range(count - 1)])]
    ppermute x10 -> x11, starting transfers between devices: 24.4 us -> 36 us  [the longest x5 19.8 us: to_neighbours(): before = lax.ppermute(high, 'slab', [(i, i + 1) for i in range(count - 1)])]
    all_to_all x0 -> x1, starting transfers between devices: none -> 9.41 us  [on_device(): lax.all_to_all(jnp.broadcast_to(payload[None], (slabs, *payload.shape)),...]
    reduce_sum x5 -> x3, other arithmetic: 9.65 us -> 0.86 us  [the longest x2 0.73 us: dot(): return sum((jnp.sum(x * y, axis=0) for x, y in zip(xs, ys)))]
    another operation x1 -> x2, other arithmetic: 0.86 us -> 4.33 us  [on_device(): terms = -jnp.stack(terms)]
  transfers between devices with their start and end apart: 11 -> 12, of which waited for: 11 -> 8; matrix products, arithmetic and copies ran while one was open for 2% -> 10% of each run, Pallas kernels for 0% -> 0%
where the time goes in v1:
time: 106 us; the launch traced here: 105 us
  starting transfers between devices  45.4 us (43%)
  waiting for transfers between devices  20.2 us (19%)
  between operations  17 us (16%)
  other arithmetic  12.9 us (12%)
  local copies, waits for them, and re-layouts  9.66 us (9%)
    ppermute x5, starting transfers between devices, to_neighbours(): before = lax.ppermute(high, 'slab', [(i, i + 1) for i in range(count - 1)])  19.8 us
    ppermute x5, waiting for transfers between devices, to_neighbours(): after = lax.ppermute(low, 'slab', [(i + 1, i) for i in range(count - 1)])  10.2 us
    ppermute x1, starting transfers between devices, on_device(): gradient = terms + lax.ppermute(terms, 'test', [(0, 1), (1, 0)])  9.61 us
    all_to_all x1, starting transfers between devices, on_device(): lax.all_to_all(jnp.broadcast_to(payload[None], (slabs, *payload.shape)),...  9.41 us
    ppermute x5, waiting for transfers between devices, to_neighbours(): before = lax.ppermute(high, 'slab', [(i, i + 1) for i in range(count - 1)])  8.83 us
    ppermute x5, starting transfers between devices, to_neighbours(): after = lax.ppermute(low, 'slab', [(i + 1, i) for i in range(count - 1)])  6.57 us
    unnamed x50, local copies, waits for them, and re-layouts  4.94 us
    another operation x2, other arithmetic, on_device(): terms = -jnp.stack(terms)  4.33 us
  transfers between devices with their start and end apart: 12, of which 8 were waited for; matrix products, arithmetic and copies ran while one was open for 10% of the time, Pallas kernels for 0%

profile of v1, /device:TPU:1, one launch (start us, length us, event | category | flops | bytes accessed | tf_op | source)
XLA Modules:
  0.0 105.1 jit_solution(4632121804880993028)
XLA Ops:
  0.6 1.8 %slice_bitcast_fusion.4 = (f32[512,128]{1,0:T(8,128)}, f32[512,128]{1,0:T(8,128)S(1)}) fusion(f32[2,512,128]{2,1,0:T(8,128)} %param.8), kind=kLoop, calls=%fused_computation.238 | loop fusion | bytes 1048576 | tf_op jit(solution)/shard_map/squeeze | solution.py:75
  2.5 4.1 %collective-permute-start = (f32[512,128]{1,0:T(8,128)S(1)}, f32[512,128]{1,0:T(8,128)S(1)}, u32[]{:S(2)}, u32[]{:S(2)}) collective-permute-start(f32[512,128]{1,0:T(8,128)S(1)} %get-tuple-element.37), channel_id=1, source_target_pairs={{0,1},{1,2},{2,3},{3,4},{4,5},{5,6},{6,7},{7,8},{8,9},{9,10},{10,1... | collective-permute-start | bytes 786440 | tf_op jit(solution)/shard_map/ppermute | solution.py:32
  6.6 1.3 %collective-permute-start.1 = (f32[512,128]{1,0:T(8,128)}, f32[512,128]{1,0:T(8,128)S(1)}, u32[]{:S(2)}, u32[]{:S(2)}) collective-permute-start(f32[512,128]{1,0:T(8,128)} %get-tuple-element.36), channel_id=1, source_target_pairs={{1,0},{2,1},{3,2},{4,3},{5,4},{6,5},{7,6},{8,7},{9,8},{10,9},{11,1... | collective-permute-start | bytes 786440 | tf_op jit(solution)/shard_map/ppermute | solution.py:33
  8.0 0.6 copy-done.23
  8.6 0.8 gather_fusion
  10.1 1.1 %scatter_custom_fusion = f32[131072]{0:T(1024)S(1)} fusion(s32[64]{0:T(128)S(1)} %compare_select_fusion, f32[64]{0:T(128)S(1)} %fusion.147, f32[]{:T(128)} %constant.12.clone.1), kind=kCustom, calls=%fused_computation.243 | custom fusion | flops 64 | bytes 524292 | tf_op jit(solution)/shard_map/scatter-add | solution.py:112
  11.5 0.8 copy-done
  12.3 1.3 %fusion.158 = (f32[512,128]{1,0:T(8,128)S(1)}, f32[512,128]{1,0:T(8,128)S(1)}, f32[512,128]{1,0:T(8,128)S(1)}, f32[512,128]{1,0:T(8,128)S(1)}, f32[512,128]{1,0:T(8,128)S(1)}, /*index=5*/f32[512,128]{1,0:T(8,128)S(1)}) fusion(f32[512,128]{1,0:T(8,128)S(1)} %get-tuple-element.52, f32[512,128]{1,0:T(8,128)S(1)} %get-tuple-element.51, s32[]{:T(128)S(6)} %sub.232, ...), kind=kLoop, calls=%fused_computation.276 | loop fusion | flops 1769472 | bytes 3934213 | tf_op jit(solution)/shard_map/div | solution.py:130
  13.7 1.4 %collective-permute-start.3 = (f32[512,128]{1,0:T(8,128)S(1)}, f32[512,128]{1,0:T(8,128)S(1)}, u32[]{:S(2)}, u32[]{:S(2)}) collective-permute-start(f32[512,128]{1,0:T(8,128)S(1)} %get-tuple-element.25), channel_id=1, source_target_pairs={{1,0},{2,1},{3,2},{4,3},{5,4},{6,5},{7,6},{8,7},{9,8},{10,9},{11,1... | collective-permute-start | bytes 786440 | tf_op jit(solution)/shard_map/ppermute | solution.py:33
  15.3 3.7 %collective-permute-done.1 = f32[512,128]{1,0:T(8,128)S(1)} collective-permute-done((f32[512,128]{1,0:T(8,128)}, f32[512,128]{1,0:T(8,128)S(1)}, u32[]{:S(2)}, u32[]{:S(2)}) %collective-permute-start.1) | collective-permute-done | bytes 262176 | tf_op jit(solution)/shard_map/ppermute | solution.py:33
  19.8 3.1 %collective-permute-start.2 = (f32[512,128]{1,0:T(8,128)S(1)}, f32[512,128]{1,0:T(8,128)S(1)}, u32[]{:S(2)}, u32[]{:S(2)}) collective-permute-start(f32[512,128]{1,0:T(8,128)S(1)} %get-tuple-element.30), channel_id=1, source_target_pairs={{0,1},{1,2},{2,3},{3,4},{4,5},{5,6},{6,7},{7,8},{8,9},{9,10},{10,1... | collective-permute-start | bytes 786440 | tf_op jit(solution)/shard_map/ppermute | solution.py:32
  23.7 6.0 %collective-permute-done.2 = f32[512,128]{1,0:T(8,128)S(1)} collective-permute-done((f32[512,128]{1,0:T(8,128)S(1)}, f32[512,128]{1,0:T(8,128)S(1)}, u32[]{:S(2)}, u32[]{:S(2)}) %collective-permute-start.2) | collective-permute-done | bytes 262176 | tf_op jit(solution)/shard_map/ppermute | solution.py:32
  30.4 1.3 %collective-permute-start.5 = (f32[512,128]{1,0:T(8,128)S(1)}, f32[512,128]{1,0:T(8,128)S(1)}, u32[]{:S(2)}, u32[]{:S(2)}) collective-permute-start(f32[512,128]{1,0:T(8,128)S(1)} %get-tuple-element.21), channel_id=1, source_target_pairs={{1,0},{2,1},{3,2},{4,3},{5,4},{6,5},{7,6},{8,7},{9,8},{10,9},{11,1... | collective-permute-start | bytes 786440 | tf_op jit(solution)/shard_map/ppermute | solution.py:33
  31.8 4.7 %collective-permute-start.4 = (f32[512,128]{1,0:T(8,128)S(1)}, f32[512,128]{1,0:T(8,128)S(1)}, u32[]{:S(2)}, u32[]{:S(2)}) collective-permute-start(f32[512,128]{1,0:T(8,128)S(1)} %get-tuple-element.23), channel_id=1, source_target_pairs={{0,1},{1,2},{2,3},{3,4},{4,5},{5,6},{6,7},{7,8},{8,9},{9,10},{10,1... | collective-permute-start | bytes 786440 | tf_op jit(solution)/shard_map/ppermute | solution.py:32
  36.8 1.9 %collective-permute-done.5 = f32[512,128]{1,0:T(8,128)S(1)} collective-permute-done((f32[512,128]{1,0:T(8,128)S(1)}, f32[512,128]{1,0:T(8,128)S(1)}, u32[]{:S(2)}, u32[]{:S(2)}) %collective-permute-start.5) | collective-permute-done | bytes 262176 | tf_op jit(solution)/shard_map/ppermute | solution.py:33
  39.4 3.9 %collective-permute-start.6 = (f32[512,128]{1,0:T(8,128)S(1)}, f32[512,128]{1,0:T(8,128)S(1)}, u32[]{:S(2)}, u32[]{:S(2)}) collective-permute-start(f32[512,128]{1,0:T(8,128)S(1)} %div.117), channel_id=1, source_target_pairs={{0,1},{1,2},{2,3},{3,4},{4,5},{5,6},{6,7},{7,8},{8,9},{9,10},{10,1... | collective-permute-start | bytes 786440 | tf_op jit(solution)/shard_map/ppermute | solution.py:32
  44.2 1.3 %collective-permute-start.7 = (f32[512,128]{1,0:T(8,128)S(1)}, f32[512,128]{1,0:T(8,128)S(1)}, u32[]{:S(2)}, u32[]{:S(2)}) collective-permute-start(f32[512,128]{1,0:T(8,128)S(1)} %get-tuple-element.19), channel_id=1, source_target_pairs={{1,0},{2,1},{3,2},{4,3},{5,4},{6,5},{7,6},{8,7},{9,8},{10,9},{11,1... | collective-permute-start | bytes 786440 | tf_op jit(solution)/shard_map/ppermute | solution.py:33
  45.7 2.6 %collective-permute-done.6 = f32[512,128]{1,0:T(8,128)S(1)} collective-permute-done((f32[512,128]{1,0:T(8,128)S(1)}, f32[512,128]{1,0:T(8,128)S(1)}, u32[]{:S(2)}, u32[]{:S(2)}) %collective-permute-start.6) | collective-permute-done | bytes 262176 | tf_op jit(solution)/shard_map/ppermute | solution.py:32
  49.0 4.6 %collective-permute-done.7 = f32[512,128]{1,0:T(8,128)S(1)} collective-permute-done((f32[512,128]{1,0:T(8,128)S(1)}, f32[512,128]{1,0:T(8,128)S(1)}, u32[]{:S(2)}, u32[]{:S(2)}) %collective-permute-start.7) | collective-permute-done | bytes 262176 | tf_op jit(solution)/shard_map/ppermute | solution.py:33
  54.3 0.6 broadcast_in_dim.47
  55.0 9.4 %all-to-all-start = ((f32[16,8,128]{2,1,0:T(8,128)}), f32[16,8,128]{2,1,0:T(8,128)S(1)}, u32[]{:S(2)}, u32[]{:S(2)}) async-start(f32[16,8,128]{2,1,0:T(8,128)} %broadcast_in_dim.47), calls=%async_computation | async-start | bytes 131072 | tf_op jit(solution)/shard_map/all_to_all | solution.py:143
  64.4 0.7 slice_bitcast_fusion.2
  65.1 4.0 %collective-permute-start.8 = (f32[512,128]{1,0:T(8,128)}, f32[512,128]{1,0:T(8,128)}, u32[]{:S(2)}, u32[]{:S(2)}) collective-permute-start(f32[512,128]{1,0:T(8,128)} %get-tuple-element.34), channel_id=1, source_target_pairs={{0,1},{1,2},{2,3},{3,4},{4,5},{5,6},{6,7},{7,8},{8,9},{9,10},{10,1... | collective-permute-start | bytes 786440 | tf_op jit(solution)/shard_map/ppermute | solution.py:32
  69.1 1.3 %collective-permute-start.9 = (f32[512,128]{1,0:T(8,128)S(1)}, f32[512,128]{1,0:T(8,128)}, u32[]{:S(2)}, u32[]{:S(2)}) collective-permute-start(f32[512,128]{1,0:T(8,128)S(1)} %get-tuple-element.35), channel_id=1, source_target_pairs={{1,0},{2,1},{3,2},{4,3},{5,4},{6,5},{7,6},{8,7},{9,8},{10,9},{11,1... | collective-permute-start | bytes 786440 | tf_op jit(solution)/shard_map/ppermute | solution.py:33
  70.9 0.7 fusion.164
  87.6 0.8 copy-done.7
  88.6 1.8 %fusion.69 = (f32[1,512,128]{2,1,0:T(8,128)S(1)}, f32[512,128]{1,0:T(8,128)S(1)}) fusion(f32[512,128]{1,0:T(8,128)S(1)} %multiply_add_fusion.1, f32[512,128]{1,0:T(8,128)S(1)} %get-tuple-element.35, f32[512,128]{1,0:T(8,128)S(1)} %fusion.149, f32[512,128]{1,0:T(8,128)} %collective-permute-done.8, f32[512,128]{1,0:T(8,128)S(1)} %copy-done.13, ...), kind=kLoop, calls=%fused_computation.135 | loop fusion | flops 4653056 | bytes 3932173 | tf_op jit(solution)/shard_map/stack | solution.py:161
  90.5 2.5 %fusion.82 = f32[1,512,128]{2,1,0:T(8,128)S(1)} fusion(f32[512,128]{1,0:T(8,128)S(1)} %get-tuple-element.17, f32[512,128]{1,0:T(8,128)} %get-tuple-element.34, f32[512,128]{1,0:T(8,128)S(1)} %copy-done.5, f32[512,128]{1,0:T(8,128)} %collective-permute-done.9, f32[512,128]{1,0:T(8,128)S(1)} %copy-done.19, f32[512,128]{1,0:T(8,128)S(1)} %copy-done.17, ...), kind=kLoop, calls=%fused_computation.148 | loop fusion | flops 4325376 | bytes 3145741 | tf_op jit(solution)/shard_map/stack | solution.py:161
  93.1 9.6 %collective-permute-start.10 = (f32[2,512,128]{2,1,0:T(8,128)S(1)}, f32[2,512,128]{2,1,0:T(8,128)S(1)}, u32[]{:S(2)}, u32[]{:S(2)}) collective-permute-start(f32[2,512,128]{2,1,0:T(8,128)S(1)} %maximum_negate_fusion), channel_id=1, source_target_pairs={{0,16},{16,0},{1,17},{17,1},{2,18},{18,2},{3,19},{19,3},{4,20},{20... | collective-permute-start | bytes 1572872 | tf_op jit(solution)/shard_map/ppermute | solution.py:163
  102.7 0.8 maximum_bitcast_fusion
  103.5 0.7 collective-permute-done.10
  104.2 0.9 fusion.150
  (85 shorter events, 7.8 us)
Async XLA Ops:
  0.6 7.2 %copy-start.2 = (f32[2,512,128]{2,1,0:T(8,128)S(1)}, f32[2,512,128]{2,1,0:T(8,128)}, u32[]{:S(2)}) copy-start(f32[2,512,128]{2,1,0:T(8,128)} %param.8) | copy-start | bytes 1572868
  2.5 6.2 %copy-start.3 = (f32[1,2,512,128]{3,2,1,0:T(8,128)S(1)}, f32[1,2,512,128]{3,2,1,0:T(8,128)}, u32[]{:S(2)}) copy-start(f32[1,2,512,128]{3,2,1,0:T(8,128)} %param.11) | copy-start | bytes 1572868
  2.5 9.0 %collective-permute-start = (f32[512,128]{1,0:T(8,128)S(1)}, f32[512,128]{1,0:T(8,128)S(1)}, u32[]{:S(2)}, u32[]{:S(2)}) collective-permute-start(f32[512,128]{1,0:T(8,128)S(1)} %get-tuple-element.37), channel_id=1, source_target_pairs={{0,1},{1,2},{2,3},{3,4},{4,5},{5,6},{6,7},{7,8},{8,9},{9,10},{10,1... | collective-permute-start | bytes 786440 | tf_op jit(solution)/shard_map/ppermute | solution.py:32
  6.6 12.5 %collective-permute-start.1 = (f32[512,128]{1,0:T(8,128)}, f32[512,128]{1,0:T(8,128)S(1)}, u32[]{:S(2)}, u32[]{:S(2)}) collective-permute-start(f32[512,128]{1,0:T(8,128)} %get-tuple-element.36), channel_id=1, source_target_pairs={{1,0},{2,1},{3,2},{4,3},{5,4},{6,5},{7,6},{8,7},{9,8},{10,9},{11,1... | collective-permute-start | bytes 786440 | tf_op jit(solution)/shard_map/ppermute | solution.py:33
  8.6 0.8 copy-start.24
  10.1 1.4 %copy-start.1 = (s32[2,512,128]{2,1,0:T(8,128)S(1)}, s32[2,512,128]{2,1,0:T(8,128)}, u32[]{:S(2)}) copy-start(s32[2,512,128]{2,1,0:T(8,128)} %param.10) | copy-start | bytes 1572868
  11.2 1.0 copy-start
  11.5 2.1 %copy-start.6 = (f32[512,128]{1,0:T(8,128)}, f32[512,128]{1,0:T(8,128)S(1)}, u32[]{:S(2)}) copy-start(f32[512,128]{1,0:T(8,128)S(1)} %collective-permute-done) | copy-start | bytes 786436
  13.6 1.7 %copy-start.4 = (f32[512,128]{1,0:T(8,128)}, f32[512,128]{1,0:T(8,128)S(1)}, u32[]{:S(2)}) copy-start(f32[512,128]{1,0:T(8,128)S(1)} %get-tuple-element.38) | copy-start | bytes 786436
  13.6 5.4 %copy-start.22 = (f32[1,2,512,128]{3,2,1,0:T(8,128)S(1)}, f32[1,2,512,128]{3,2,1,0:T(8,128)}, u32[]{:S(2)}) copy-start(f32[1,2,512,128]{3,2,1,0:T(8,128)} %param.12) | copy-start | bytes 1572868
  13.7 9.4 %collective-permute-start.3 = (f32[512,128]{1,0:T(8,128)S(1)}, f32[512,128]{1,0:T(8,128)S(1)}, u32[]{:S(2)}, u32[]{:S(2)}) collective-permute-start(f32[512,128]{1,0:T(8,128)S(1)} %get-tuple-element.25), channel_id=1, source_target_pairs={{1,0},{2,1},{3,2},{4,3},{5,4},{6,5},{7,6},{8,7},{9,8},{10,9},{11,1... | collective-permute-start | bytes 786440 | tf_op jit(solution)/shard_map/ppermute | solution.py:33
  19.1 0.7 copy-start.20
  19.8 10.0 %collective-permute-start.2 = (f32[512,128]{1,0:T(8,128)S(1)}, f32[512,128]{1,0:T(8,128)S(1)}, u32[]{:S(2)}, u32[]{:S(2)}) collective-permute-start(f32[512,128]{1,0:T(8,128)S(1)} %get-tuple-element.30), channel_id=1, source_target_pairs={{0,1},{1,2},{2,3},{3,4},{4,5},{5,6},{6,7},{7,8},{8,9},{9,10},{10,1... | collective-permute-start | bytes 786440 | tf_op jit(solution)/shard_map/ppermute | solution.py:32
  29.7 0.7 copy-start.8
  30.4 8.2 %collective-permute-start.5 = (f32[512,128]{1,0:T(8,128)S(1)}, f32[512,128]{1,0:T(8,128)S(1)}, u32[]{:S(2)}, u32[]{:S(2)}) collective-permute-start(f32[512,128]{1,0:T(8,128)S(1)} %get-tuple-element.21), channel_id=1, source_target_pairs={{1,0},{2,1},{3,2},{4,3},{5,4},{6,5},{7,6},{8,7},{9,8},{10,9},{11,1... | collective-permute-start | bytes 786440 | tf_op jit(solution)/shard_map/ppermute | solution.py:33
  31.8 11.7 %collective-permute-start.4 = (f32[512,128]{1,0:T(8,128)S(1)}, f32[512,128]{1,0:T(8,128)S(1)}, u32[]{:S(2)}, u32[]{:S(2)}) collective-permute-start(f32[512,128]{1,0:T(8,128)S(1)} %get-tuple-element.23), channel_id=1, source_target_pairs={{0,1},{1,2},{2,3},{3,4},{4,5},{5,6},{6,7},{7,8},{8,9},{9,10},{10,1... | collective-permute-start | bytes 786440 | tf_op jit(solution)/shard_map/ppermute | solution.py:32
  39.4 8.9 %collective-permute-start.6 = (f32[512,128]{1,0:T(8,128)S(1)}, f32[512,128]{1,0:T(8,128)S(1)}, u32[]{:S(2)}, u32[]{:S(2)}) collective-permute-start(f32[512,128]{1,0:T(8,128)S(1)} %div.117), channel_id=1, source_target_pairs={{0,1},{1,2},{2,3},{3,4},{4,5},{5,6},{6,7},{7,8},{8,9},{9,10},{10,1... | collective-permute-start | bytes 786440 | tf_op jit(solution)/shard_map/ppermute | solution.py:32
  44.2 9.3 %collective-permute-start.7 = (f32[512,128]{1,0:T(8,128)S(1)}, f32[512,128]{1,0:T(8,128)S(1)}, u32[]{:S(2)}, u32[]{:S(2)}) collective-permute-start(f32[512,128]{1,0:T(8,128)S(1)} %get-tuple-element.19), channel_id=1, source_target_pairs={{1,0},{2,1},{3,2},{4,3},{5,4},{6,5},{7,6},{8,7},{9,8},{10,9},{11,1... | collective-permute-start | bytes 786440 | tf_op jit(solution)/shard_map/ppermute | solution.py:33
  48.3 0.7 copy-start.12
  55.0 15.8 %all-to-all-start = ((f32[16,8,128]{2,1,0:T(8,128)}), f32[16,8,128]{2,1,0:T(8,128)S(1)}, u32[]{:S(2)}, u32[]{:S(2)}) async-start(f32[16,8,128]{2,1,0:T(8,128)} %broadcast_in_dim.47), calls=%async_computation | async-start | bytes 131072 | tf_op jit(solution)/shard_map/all_to_all | solution.py:143
  65.1 22.5 %collective-permute-start.8 = (f32[512,128]{1,0:T(8,128)}, f32[512,128]{1,0:T(8,128)}, u32[]{:S(2)}, u32[]{:S(2)}) collective-permute-start(f32[512,128]{1,0:T(8,128)} %get-tuple-element.34), channel_id=1, source_target_pairs={{0,1},{1,2},{2,3},{3,4},{4,5},{5,6},{6,7},{7,8},{8,9},{9,10},{10,1... | collective-permute-start | bytes 786440 | tf_op jit(solution)/shard_map/ppermute | solution.py:32
  69.1 21.4 %collective-permute-start.9 = (f32[512,128]{1,0:T(8,128)S(1)}, f32[512,128]{1,0:T(8,128)}, u32[]{:S(2)}, u32[]{:S(2)}) collective-permute-start(f32[512,128]{1,0:T(8,128)S(1)} %get-tuple-element.35), channel_id=1, source_target_pairs={{1,0},{2,1},{3,2},{4,3},{5,4},{6,5},{7,6},{8,7},{9,8},{10,9},{11,1... | collective-permute-start | bytes 786440 | tf_op jit(solution)/shard_map/ppermute | solution.py:33
  87.4 1.0 copy-start.7
  87.5 1.0 copy-start.9
  87.5 1.1 %copy-start.11 = (f32[512,128]{1,0:T(8,128)S(1)}, f32[512,128]{1,0:T(8,128)}, u32[]{:S(2)}) copy-start(f32[512,128]{1,0:T(8,128)} %copy-done.10) | copy-start | bytes 786436
  87.5 1.2 %copy-start.13 = (f32[512,128]{1,0:T(8,128)S(1)}, f32[512,128]{1,0:T(8,128)}, u32[]{:S(2)}) copy-start(f32[512,128]{1,0:T(8,128)} %copy-done.12) | copy-start | bytes 786436
  87.5 2.9 %copy-start.5 = (f32[512,128]{1,0:T(8,128)S(1)}, f32[512,128]{1,0:T(8,128)}, u32[]{:S(2)}) copy-start(f32[512,128]{1,0:T(8,128)} %copy-done.4) | copy-start | bytes 786436
  87.6 2.9 %copy-start.15 = (f32[512,128]{1,0:T(8,128)S(1)}, f32[512,128]{1,0:T(8,128)}, u32[]{:S(2)}) copy-start(f32[512,128]{1,0:T(8,128)} %copy-done.14) | copy-start | bytes 786436
  87.6 2.9 %copy-start.17 = (f32[512,128]{1,0:T(8,128)S(1)}, f32[512,128]{1,0:T(8,128)}, u32[]{:S(2)}) copy-start(f32[512,128]{1,0:T(8,128)} %copy-done.16) | copy-start | bytes 786436
  87.6 2.9 %copy-start.19 = (f32[512,128]{1,0:T(8,128)S(1)}, f32[512,128]{1,0:T(8,128)}, u32[]{:S(2)}) copy-start(f32[512,128]{1,0:T(8,128)} %copy-done.18) | copy-start | bytes 786436
  87.6 2.9 %copy-start.21 = (f32[512,128]{1,0:T(8,128)S(1)}, f32[512,128]{1,0:T(8,128)}, u32[]{:S(2)}) copy-start(f32[512,128]{1,0:T(8,128)} %copy-done.20) | copy-start | bytes 786436
  93.1 11.2 %collective-permute-start.10 = (f32[2,512,128]{2,1,0:T(8,128)S(1)}, f32[2,512,128]{2,1,0:T(8,128)S(1)}, u32[]{:S(2)}, u32[]{:S(2)}) collective-permute-start(f32[2,512,128]{2,1,0:T(8,128)S(1)} %maximum_negate_fusion), channel_id=1, source_target_pairs={{0,16},{16,0},{1,17},{17,1},{2,18},{18,2},{3,19},{19,3},{4,20},{20... | collective-permute-start | bytes 1572872 | tf_op jit(solution)/shard_map/ppermute | solution.py:163
  (5 other events, 3.4 us)

commit v2 on v1

--- a/solution.py
+++ b/solution.py
@@ -1,6 +1,8 @@
 import jax
 import jax.numpy as jnp
 from jax import lax
+from jax.experimental import pallas as pl
+from jax.experimental.pallas import tpu as pltpu
 from jax.sharding import PartitionSpec as P
 
 WELL_TERM = 4.0
@@ -8,11 +10,6 @@
 
 def face_value(a, b):
     return 2.0 * a * b / (a + b)
-
-
-def slope(own, other):
-    total = own + other
-    return 2.0 * own * other * other / (total * total)
 
 
 def shift_down(v, axis):
@@ -64,6 +61,41 @@
     return a0 + a1 * u + a2 * q0, a2 * q1 - a1 * a0, a2 * q2
 
 
+def coefficient_kernel(parts_ref, coef_ref):
+    sums = parts_ref[0]
+    least = parts_ref[0]
+    for i in range(1, parts_ref.shape[0]):
+        sums = sums + parts_ref[i]
+        least = jnp.minimum(least, parts_ref[i])
+    sums = jnp.sum(sums, axis=1, keepdims=True)
+    least = jnp.min(least, axis=1, keepdims=True)
+    coefs = combine([sums[i : i + 1] for i in range(6)], least[6:7])
+    for i, c in enumerate(coefs):
+        coef_ref[i : i + 1, :] = jnp.broadcast_to(c, (1, coef_ref.shape[1]))
+    coef_ref[3:8, :] = jnp.zeros((5, coef_ref.shape[1]), jnp.float32)
+
+
+def coefficients(parts):
+    return pl.pallas_call(
+        coefficient_kernel,
+        out_shape=jax.ShapeDtypeStruct(parts.shape[1:], jnp.float32),
+        in_specs=[pl.BlockSpec(memory_space=pltpu.VMEM)],
+        out_specs=pl.BlockSpec(memory_space=pltpu.VMEM),
+        cost_estimate=pl.CostEstimate(flops=parts.size, bytes_accessed=4 * parts.size, transcendentals=0),
+    )(parts)
+
+
+def shared_halo(low, high):
+    if lax.axis_size("test") != 2:
+        return to_neighbours(low, high)
+    half = low.shape[0] // 2
+    test = lax.axis_index("test")
+    mine = jnp.stack(to_neighbours(*(lax.dynamic_slice_in_dim(v, test * half, half) for v in (low, high))))
+    other = lax.ppermute(mine, "test", [(0, 1), (1, 0)])
+    both = jnp.where(test == 0, jnp.concatenate([mine, other], axis=1), jnp.concatenate([other, mine], axis=1))
+    return both[0], both[1]
+
+
 def on_device(
     log_conductivity, storage, active_mask, heads, adjoint_next, pump_cells, obs_cells, obs_data
 ):
@@ -73,7 +105,7 @@
     has_before = place > 0
     has_after = place < slabs - 1
     logs = [log_conductivity[i] for i in range(width)]
-    log_before, log_after = to_neighbours(logs[0], logs[-1])
+    log_before, log_after = shared_halo(logs[0], logs[-1])
     head = [heads[0, i] for i in range(width)]
     head_before, head_after = to_neighbours(head[0], head[-1])
 
@@ -92,6 +124,14 @@
         face_x[i] + face_x[i + 1] + face_y[i] + shift_up(face_y[i], 0) + face_z[i] + shift_up(face_z[i], 1)
         for i in range(width)
     ]
+
+    def edge(face, a, b, head_a, head_b):
+        return face * (head_a - head_b) / (a + b)
+
+    head_pad = [head_before, *head, head_after]
+    edge_x = [edge(face_x[i], cond_pad[i], cond_pad[i + 1], head_pad[i], head_pad[i + 1]) for i in range(width + 1)]
+    edge_y = [edge(face_y[i], shift_down(cond[i], 0), cond[i], shift_down(head[i], 0), head[i]) for i in range(width)]
+    edge_z = [edge(face_z[i], shift_down(cond[i], 1), cond[i], shift_down(head[i], 1), head[i]) for i in range(width)]
 
     cells_here = width * rows * depth
     offset = place * cells_here
@@ -143,20 +183,17 @@
     gathered = lax.all_to_all(
         jnp.broadcast_to(payload[None], (slabs, *payload.shape)), "slab", 0, 0, tiled=True
     )
-    totals = jnp.sum(jnp.sum(gathered, axis=0), axis=1)
-    coefs = combine([totals[i] for i in range(6)], jnp.min(gathered[:, 6]))
-    adjoint = [sum(c * f[i] for c, f in zip(coefs, fields)) for i in range(width + 2)]
-
-    head_pad = [head_before, *head, head_after]
+    coefs = coefficients(gathered)
+    adjoint = [sum(coefs[k : k + 1] * fields[k][i] for k in range(3)) for i in range(width + 2)]
+
     terms = []
     for i in range(width):
-        c, a, h = cond[i], adjoint[i + 1], head[i]
-        total = jnp.zeros_like(c)
-        for j in (i, i + 2):
-            total = total + slope(c, cond_pad[j]) * (a - adjoint[j]) * (h - head_pad[j])
-        for axis in (0, 1):
-            for shift in (shift_down, shift_up):
-                total = total + slope(c, shift(c, axis)) * (a - shift(a, axis)) * (h - shift(h, axis))
+        a = adjoint[i + 1]
+        flux_y = edge_y[i] * (shift_down(a, 0) - a)
+        flux_z = edge_z[i] * (shift_down(a, 1) - a)
+        total = edge_x[i] * (adjoint[i] - a) * cond_pad[i] + edge_x[i + 1] * (a - adjoint[i + 2]) * cond_pad[i + 2]
+        total = total + flux_y * shift_down(cond[i], 0) + shift_up(flux_y * cond[i], 0)
+        total = total + flux_z * shift_down(cond[i], 1) + shift_up(flux_z * cond[i], 1)
         terms.append(total)
     terms = -jnp.stack(terms)
     if lax.axis_size("test") == 2:

time: 106 us -> 97.8 us (0.923)
  between operations: 17 us -> 1.81 us
  waiting for transfers between devices: 20.2 us -> 26.4 us
  starting transfers between devices: 45.4 us -> 43.4 us
  Pallas kernels: 0 us -> 1.67 us
    ppermute x5, waiting for transfers between devices: 10.2 us -> 14.5 us  [to_neighbours(): after = lax.ppermute(low, 'slab', [(i + 1, i) for i in range(count - 1)])]
    ppermute x1, starting transfers between devices: 9.61 us -> 5.69 us  [on_device(): gradient = terms + lax.ppermute(terms, 'test', [(0, 1), (1, 0)])]
    mul x0 -> x2, other arithmetic: none -> 3.01 us  [on_device(): flux_z * cond[i]]
    ppermute x5, starting transfers between devices: 19.8 us -> 22 us  [to_neighbours(): before = lax.ppermute(high, 'slab', [(i, i + 1) for i in range(count - 1)])]
    squeeze x1 -> x0, local copies, waits for them, and re-layouts: 1.82 us -> none  [on_device(): logs = [log_conductivity[i] for i in range(width)]]
    pallas_call x0 -> x1, Pallas kernels: none -> 1.67 us  [coefficients(): pl.pallas_call(coefficient_kernel, out_shape=jax.ShapeDtypeStruct(parts.s...]
    ppermute x5, waiting for transfers between devices: 8.83 us -> 10.4 us  [to_neighbours(): before = lax.ppermute(high, 'slab', [(i, i + 1) for i in range(count - 1)])]
    squeeze x1, local copies, waits for them, and re-layouts: 0.74 us -> 1.87 us  [on_device(): head = [heads[0, i] for i in range(width)]]
  transfers between devices with their start and end apart: 12 -> 13, of which waited for: 8 -> 9; matrix products, arithmetic and copies ran while one was open for 10% -> 14% of each run, Pallas kernels for 0% -> 2%
where the time goes in v2:
time: 97.8 us; the launch traced here: 96.8 us
  starting transfers between devices  43.4 us (44%)
  waiting for transfers between devices  26.4 us (27%)
  other arithmetic  13.7 us (14%)
  local copies, waits for them, and re-layouts  9.84 us (10%)
  between operations  1.81 us (2%)
  Pallas kernels  1.67 us (2%)
    ppermute x5, starting transfers between devices, to_neighbours(): before = lax.ppermute(high, 'slab', [(i, i + 1) for i in range(count - 1)])  22 us
    ppermute x5, waiting for transfers between devices, to_neighbours(): after = lax.ppermute(low, 'slab', [(i + 1, i) for i in range(count - 1)])  14.5 us
    ppermute x5, waiting for transfers between devices, to_neighbours(): before = lax.ppermute(high, 'slab', [(i, i + 1) for i in range(count - 1)])  10.4 us
    all_to_all x1, starting transfers between devices, on_device(): lax.all_to_all(jnp.broadcast_to(payload[None], (slabs, *payload.shape)),...  8.58 us
    ppermute x5, starting transfers between devices, to_neighbours(): after = lax.ppermute(low, 'slab', [(i + 1, i) for i in range(count - 1)])  6.57 us
    ppermute x1, starting transfers between devices, on_device(): gradient = terms + lax.ppermute(terms, 'test', [(0, 1), (1, 0)])  5.69 us
    unnamed x62, local copies, waits for them, and re-layouts  4.6 us
    another operation x2, other arithmetic, on_device(): terms = -jnp.stack(terms)  3.79 us
  transfers between devices with their start and end apart: 13, of which 9 were waited for; matrix products, arithmetic and copies ran while one was open for 14% of the time, Pallas kernels for 2%

profile of v2, /device:TPU:1, one launch (start us, length us, event | category | flops | bytes accessed | tf_op | source)
XLA Modules:
  0.0 96.8 jit_solution(16357869846223556999)
XLA Ops:
  0.6 1.1 %exponential_bitcast_fusion = (f32[512,128]{1,0:T(8,128)S(1)}, f32[512,128]{1,0:T(8,128)S(1)}, f32[1,512,128]{2,1,0:T(8,128)S(1)}, f32[1,512,128]{2,1,0:T(8,128)S(1)}) fusion(f32[2,512,128]{2,1,0:T(8,128)} %param.8), kind=kLoop, calls=%fused_computation.199 | loop fusion | bytes 1572864 | tf_op jit(solution)/shard_map/exp | solution.py:112
  1.8 1.4 %collective-permute-start.1 = (f32[256,128]{1,0:T(8,128)S(1)}, f32[256,128]{1,0:T(8,128)S(1)}, u32[]{:S(2)}, u32[]{:S(2)}) collective-permute-start(f32[256,128]{1,0:T(8,128)S(1)} %dynamic-slice_bitcast_fusion), channel_id=1, source_target_pairs={{1,0},{2,1},{3,2},{4,3},{5,4},{6,5},{7,6},{8,7},{9,8},{10,9},{11,1... | collective-permute-start | bytes 393224 | tf_op jit(solution)/shard_map/ppermute | solution.py:30
  3.3 4.6 %collective-permute-start = (f32[256,128]{1,0:T(8,128)S(1)}, f32[256,128]{1,0:T(8,128)S(1)}, u32[]{:S(2)}, u32[]{:S(2)}) collective-permute-start(f32[256,128]{1,0:T(8,128)S(1)} %dynamic-slice_bitcast_fusion.1), channel_id=1, source_target_pairs={{0,1},{1,2},{2,3},{3,4},{4,5},{5,6},{6,7},{7,8},{8,9},{9,10},{10,1... | collective-permute-start | bytes 393224 | tf_op jit(solution)/shard_map/ppermute | solution.py:29
  10.0 1.1 %scatter_custom_fusion = f32[131072]{0:T(1024)S(1)} fusion(s32[64]{0:T(128)S(1)} %compare_select_fusion, f32[64]{0:T(128)S(1)} %fusion.123, f32[]{:T(128)} %constant.15.clone.1), kind=kCustom, calls=%fused_computation.204 | custom fusion | flops 64 | bytes 524292 | tf_op jit(solution)/shard_map/scatter-add | solution.py:152
  11.2 2.6 %collective-permute-done = f32[256,128]{1,0:T(8,128)S(1)} collective-permute-done((f32[256,128]{1,0:T(8,128)S(1)}, f32[256,128]{1,0:T(8,128)S(1)}, u32[]{:S(2)}, u32[]{:S(2)}) %collective-permute-start) | collective-permute-done | bytes 131104 | tf_op jit(solution)/shard_map/ppermute | solution.py:29
  14.7 0.8 collective-permute-done.2
  16.3 1.3 %collective-permute-start.4 = (f32[512,128]{1,0:T(8,128)S(1)}, f32[512,128]{1,0:T(8,128)S(1)}, u32[]{:S(2)}, u32[]{:S(2)}) collective-permute-start(f32[512,128]{1,0:T(8,128)S(1)} %get-tuple-element.25), channel_id=1, source_target_pairs={{1,0},{2,1},{3,2},{4,3},{5,4},{6,5},{7,6},{8,7},{9,8},{10,9},{11,1... | collective-permute-start | bytes 786440 | tf_op jit(solution)/shard_map/ppermute | solution.py:30
  18.0 4.8 %collective-permute-start.3 = (f32[512,128]{1,0:T(8,128)S(1)}, f32[512,128]{1,0:T(8,128)S(1)}, u32[]{:S(2)}, u32[]{:S(2)}) collective-permute-start(f32[512,128]{1,0:T(8,128)S(1)} %get-tuple-element.30), channel_id=1, source_target_pairs={{0,1},{1,2},{2,3},{3,4},{4,5},{5,6},{6,7},{7,8},{8,9},{9,10},{10,1... | collective-permute-start | bytes 786440 | tf_op jit(solution)/shard_map/ppermute | solution.py:29
  22.9 4.2 %collective-permute-done.4 = f32[512,128]{1,0:T(8,128)S(1)} collective-permute-done((f32[512,128]{1,0:T(8,128)S(1)}, f32[512,128]{1,0:T(8,128)S(1)}, u32[]{:S(2)}, u32[]{:S(2)}) %collective-permute-start.4) | collective-permute-done | bytes 262176 | tf_op jit(solution)/shard_map/ppermute | solution.py:30
  27.8 5.4 %collective-permute-done.3 = f32[512,128]{1,0:T(8,128)S(1)} collective-permute-done((f32[512,128]{1,0:T(8,128)S(1)}, f32[512,128]{1,0:T(8,128)S(1)}, u32[]{:S(2)}, u32[]{:S(2)}) %collective-permute-start.3) | collective-permute-done | bytes 262176 | tf_op jit(solution)/shard_map/ppermute | solution.py:29
  33.9 1.3 %collective-permute-start.6 = (f32[512,128]{1,0:T(8,128)S(1)}, f32[512,128]{1,0:T(8,128)S(1)}, u32[]{:S(2)}, u32[]{:S(2)}) collective-permute-start(f32[512,128]{1,0:T(8,128)S(1)} %get-tuple-element.21), channel_id=1, source_target_pairs={{1,0},{2,1},{3,2},{4,3},{5,4},{6,5},{7,6},{8,7},{9,8},{10,9},{11,1... | collective-permute-start | bytes 786440 | tf_op jit(solution)/shard_map/ppermute | solution.py:30
  35.3 4.7 %collective-permute-start.5 = (f32[512,128]{1,0:T(8,128)S(1)}, f32[512,128]{1,0:T(8,128)S(1)}, u32[]{:S(2)}, u32[]{:S(2)}) collective-permute-start(f32[512,128]{1,0:T(8,128)S(1)} %get-tuple-element.23), channel_id=1, source_target_pairs={{0,1},{1,2},{2,3},{3,4},{4,5},{5,6},{6,7},{7,8},{8,9},{9,10},{10,1... | collective-permute-start | bytes 786440 | tf_op jit(solution)/shard_map/ppermute | solution.py:29
  40.2 4.1 %collective-permute-done.6 = f32[512,128]{1,0:T(8,128)S(1)} collective-permute-done((f32[512,128]{1,0:T(8,128)S(1)}, f32[512,128]{1,0:T(8,128)S(1)}, u32[]{:S(2)}, u32[]{:S(2)}) %collective-permute-start.6) | collective-permute-done | bytes 262176 | tf_op jit(solution)/shard_map/ppermute | solution.py:30
  45.0 4.0 %collective-permute-start.7 = (f32[512,128]{1,0:T(8,128)S(1)}, f32[512,128]{1,0:T(8,128)S(1)}, u32[]{:S(2)}, u32[]{:S(2)}) collective-permute-start(f32[512,128]{1,0:T(8,128)S(1)} %div.78), channel_id=1, source_target_pairs={{0,1},{1,2},{2,3},{3,4},{4,5},{5,6},{6,7},{7,8},{8,9},{9,10},{10,1... | collective-permute-start | bytes 786440 | tf_op jit(solution)/shard_map/ppermute | solution.py:29
  49.0 1.0 %collective-permute-done.5 = f32[512,128]{1,0:T(8,128)S(1)} collective-permute-done((f32[512,128]{1,0:T(8,128)S(1)}, f32[512,128]{1,0:T(8,128)S(1)}, u32[]{:S(2)}, u32[]{:S(2)}) %collective-permute-start.5) | collective-permute-done | bytes 262176 | tf_op jit(solution)/shard_map/ppermute | solution.py:29
  50.7 1.3 %collective-permute-start.8 = (f32[512,128]{1,0:T(8,128)S(1)}, f32[512,128]{1,0:T(8,128)S(1)}, u32[]{:S(2)}, u32[]{:S(2)}) collective-permute-start(f32[512,128]{1,0:T(8,128)S(1)} %get-tuple-element.19), channel_id=1, source_target_pairs={{1,0},{2,1},{3,2},{4,3},{5,4},{6,5},{7,6},{8,7},{9,8},{10,9},{11,1... | collective-permute-start | bytes 786440 | tf_op jit(solution)/shard_map/ppermute | solution.py:30
  52.2 1.4 %collective-permute-done.7 = f32[512,128]{1,0:T(8,128)S(1)} collective-permute-done((f32[512,128]{1,0:T(8,128)S(1)}, f32[512,128]{1,0:T(8,128)S(1)}, u32[]{:S(2)}, u32[]{:S(2)}) %collective-permute-start.7) | collective-permute-done | bytes 262176 | tf_op jit(solution)/shard_map/ppermute | solution.py:29
  54.3 6.2 %collective-permute-done.8 = f32[512,128]{1,0:T(8,128)S(1)} collective-permute-done((f32[512,128]{1,0:T(8,128)S(1)}, f32[512,128]{1,0:T(8,128)S(1)}, u32[]{:S(2)}, u32[]{:S(2)}) %collective-permute-start.8) | collective-permute-done | bytes 262176 | tf_op jit(solution)/shard_map/ppermute | solution.py:30
  61.9 8.6 %all-to-all-start = ((f32[16,8,128]{2,1,0:T(8,128)}), f32[16,8,128]{2,1,0:T(8,128)S(1)}, u32[]{:S(2)}, u32[]{:S(2)}) async-start(f32[16,8,128]{2,1,0:T(8,128)} %broadcast_in_dim.50), calls=%async_computation | async-start | bytes 131072 | tf_op jit(solution)/shard_map/all_to_all | solution.py:183
  70.5 1.9 %slice_bitcast_fusion.3 = (f32[512,128]{1,0:T(8,128)}, f32[512,128]{1,0:T(8,128)}) fusion(f32[1,2,512,128]{3,2,1,0:T(8,128)} %param.11), kind=kLoop, calls=%fused_computation.174 | loop fusion | bytes 1048576 | tf_op jit(solution)/shard_map/squeeze | solution.py:109
  72.3 4.0 %collective-permute-start.9 = (f32[512,128]{1,0:T(8,128)}, f32[512,128]{1,0:T(8,128)}, u32[]{:S(2)}, u32[]{:S(2)}) collective-permute-start(f32[512,128]{1,0:T(8,128)} %get-tuple-element.38), channel_id=1, source_target_pairs={{0,1},{1,2},{2,3},{3,4},{4,5},{5,6},{6,7},{7,8},{8,9},{9,10},{10,1... | collective-permute-start | bytes 786440 | tf_op jit(solution)/shard_map/ppermute | solution.py:29
  76.3 1.3 %collective-permute-start.10 = (f32[512,128]{1,0:T(8,128)}, f32[512,128]{1,0:T(8,128)}, u32[]{:S(2)}, u32[]{:S(2)}) collective-permute-start(f32[512,128]{1,0:T(8,128)} %get-tuple-element.39), channel_id=1, source_target_pairs={{1,0},{2,1},{3,2},{4,3},{5,4},{6,5},{7,6},{8,7},{9,8},{10,9},{11,1... | collective-permute-start | bytes 786440 | tf_op jit(solution)/shard_map/ppermute | solution.py:30
  78.2 1.7 %shard_map.95 = f32[8,128]{1,0:T(8,128)} custom-call(f32[16,8,128]{2,1,0:T(8,128)} %copy-done.28), custom_call_target="tpu_custom_call" | custom-call | flops 16384 | bytes 65536 | tf_op jit(solution)/shard_map/pallas_call | solution.py:79
  79.9 0.8 slice_bitcast_fusion.6
  80.7 0.9 copy-done.14
  81.6 1.6 %fusion.120 = (f32[512,128]{1,0:T(8,128)S(1)}, f32[512,128]{1,0:T(8,128)S(1)}) fusion(f32[512,128]{1,0:T(8,128)S(1)} %copy-done.14, f32[512,128]{1,0:T(8,128)S(1)} %multiply_add_fusion.1, f32[512,128]{1,0:T(8,128)S(1)} %get-tuple-element.57, f32[512,128]{1,0:T(8,128)} %get-tuple-element.39, f32[512,128]{1,0:T(8,128)S(1)} %get-tuple-element.56), kind=kLoop, calls=%fused_computation.213 | loop fusion | flops 917504 | bytes 1835008 | tf_op jit(solution)/shard_map/mul | solution.py:196
  83.3 1.9 %fusion.70 = (f32[1,512,128]{2,1,0:T(8,128)S(1)}, f32[512,128]{1,0:T(8,128)S(1)}) fusion(f32[512,128]{1,0:T(8,128)S(1)} %get-tuple-element.37, f32[512,128]{1,0:T(8,128)S(1)} %get-tuple-element.36, f32[512,128]{1,0:T(8,128)S(1)} %multiply_add_fusion.1, f32[512,128]{1,0:T(8,128)S(1)} %copy-done.26, f32[512,128]{1,0:T(8,128)S(1)} %copy-done.24, ...), kind=kLoop, calls=%fused_computation.119 | loop fusion | flops 2883584 | bytes 5768705 | tf_op jit(solution)/shard_map/stack | solution.py:198
  85.3 1.5 %fusion.122 = (f32[512,128]{1,0:T(8,128)S(1)}, f32[512,128]{1,0:T(8,128)S(1)}) fusion(f32[512,128]{1,0:T(8,128)S(1)} %copy-done.12, f32[512,128]{1,0:T(8,128)S(1)} %get-tuple-element.17, f32[512,128]{1,0:T(8,128)S(1)} %get-tuple-element.61, f32[512,128]{1,0:T(8,128)} %get-tuple-element.38, f32[512,128]{1,0:T(8,128)S(1)} %get-tuple-element.62), kind=kLoop, calls=%fused_computation.215 | loop fusion | flops 917504 | bytes 1835008 | tf_op jit(solution)/shard_map/mul | solution.py:196
  86.8 1.8 %fusion.79 = f32[1,512,128]{2,1,0:T(8,128)S(1)} fusion(f32[512,128]{1,0:T(8,128)S(1)} %get-tuple-element.35, f32[512,128]{1,0:T(8,128)S(1)} %get-tuple-element.34, f32[512,128]{1,0:T(8,128)S(1)} %get-tuple-element.17, f32[512,128]{1,0:T(8,128)S(1)} %copy-done.20, f32[512,128]{1,0:T(8,128)S(1)} %copy-done.18, f32[512,128]{1,0:T(8,128)S(1)} %copy-done.16, ...), kind=kLoop, calls=%fused_computation.128 | loop fusion | flops 2555904 | bytes 4982273 | tf_op jit(solution)/shard_map/stack | solution.py:198
  88.7 5.7 %collective-permute-start.11 = (f32[2,512,128]{2,1,0:T(8,128)S(1)}, f32[2,512,128]{2,1,0:T(8,128)S(1)}, u32[]{:S(2)}, u32[]{:S(2)}) collective-permute-start(f32[2,512,128]{2,1,0:T(8,128)S(1)} %maximum_negate_fusion), channel_id=1, source_target_pairs={{0,16},{16,0},{1,17},{17,1},{2,18},{18,2},{3,19},{19,3},{4,20},{20... | collective-permute-start | bytes 1572872 | tf_op jit(solution)/shard_map/ppermute | solution.py:200
  94.4 0.8 maximum_bitcast_fusion
  95.9 0.8 fusion.127
  (101 shorter events, 10.5 us)
Async XLA Ops:
  1.8 12.6 %copy-start.11 = (f32[512,128]{1,0:T(8,128)}, f32[512,128]{1,0:T(8,128)S(1)}, u32[]{:S(2)}) copy-start(f32[512,128]{1,0:T(8,128)S(1)} %get-tuple-element.40) | copy-start | bytes 786436
  1.8 12.6 %copy-start.13 = (f32[512,128]{1,0:T(8,128)}, f32[512,128]{1,0:T(8,128)S(1)}, u32[]{:S(2)}) copy-start(f32[512,128]{1,0:T(8,128)S(1)} %get-tuple-element.41) | copy-start | bytes 786436
  1.8 6.8 %copy-start.7 = (f32[1,2,512,128]{3,2,1,0:T(8,128)S(1)}, f32[1,2,512,128]{3,2,1,0:T(8,128)}, u32[]{:S(2)}) copy-start(f32[1,2,512,128]{3,2,1,0:T(8,128)} %param.11) | copy-start | bytes 1572868
  1.8 9.4 %collective-permute-start.1 = (f32[256,128]{1,0:T(8,128)S(1)}, f32[256,128]{1,0:T(8,128)S(1)}, u32[]{:S(2)}, u32[]{:S(2)}) collective-permute-start(f32[256,128]{1,0:T(8,128)S(1)} %dynamic-slice_bitcast_fusion), channel_id=1, source_target_pairs={{1,0},{2,1},{3,2},{4,3},{5,4},{6,5},{7,6},{8,7},{9,8},{10,9},{11,1... | collective-permute-start | bytes 393224 | tf_op jit(solution)/shard_map/ppermute | solution.py:30
  3.3 10.5 %collective-permute-start = (f32[256,128]{1,0:T(8,128)S(1)}, f32[256,128]{1,0:T(8,128)S(1)}, u32[]{:S(2)}, u32[]{:S(2)}) collective-permute-start(f32[256,128]{1,0:T(8,128)S(1)} %dynamic-slice_bitcast_fusion.1), channel_id=1, source_target_pairs={{0,1},{1,2},{2,3},{3,4},{4,5},{5,6},{6,7},{7,8},{8,9},{9,10},{10,1... | collective-permute-start | bytes 393224 | tf_op jit(solution)/shard_map/ppermute | solution.py:29
  13.8 1.7 %collective-permute-start.2 = (f32[2,256,128]{2,1,0:T(8,128)S(1)}, f32[2,256,128]{2,1,0:T(8,128)S(1)}, u32[]{:S(2)}, u32[]{:S(2)}) collective-permute-start(f32[2,256,128]{2,1,0:T(8,128)S(1)} %pad_maximum_fusion), channel_id=1, source_target_pairs={{0,16},{16,0},{1,17},{17,1},{2,18},{18,2},{3,19},{19,3},{4,20},{20... | collective-permute-start | bytes 786440 | tf_op jit(solution)/shard_map/ppermute | solution.py:94
  14.4 1.2 %copy-start.27 = (f32[1,2,512,128]{3,2,1,0:T(8,128)S(1)}, f32[1,2,512,128]{3,2,1,0:T(8,128)}, u32[]{:S(2)}) copy-start(f32[1,2,512,128]{3,2,1,0:T(8,128)} %param.12) | copy-start | bytes 1572868
  14.7 1.3 %copy-start.1 = (s32[2,512,128]{2,1,0:T(8,128)S(1)}, s32[2,512,128]{2,1,0:T(8,128)}, u32[]{:S(2)}) copy-start(s32[2,512,128]{2,1,0:T(8,128)} %param.10) | copy-start | bytes 1572868
  15.6 2.1 %copy-start.9 = (f32[2,512,128]{2,1,0:T(8,128)}, f32[2,512,128]{2,1,0:T(8,128)S(1)}, u32[]{:S(2)}) copy-start(f32[2,512,128]{2,1,0:T(8,128)S(1)} %maximum_select_fusion) | copy-start | bytes 1572868
  16.3 37.3 %copy-start.5 = (f32[512,128]{1,0:T(8,128)}, f32[512,128]{1,0:T(8,128)S(1)}, u32[]{:S(2)}) copy-start(f32[512,128]{1,0:T(8,128)S(1)} %get-tuple-element.27) | copy-start | bytes 786436
  16.3 10.7 %collective-permute-start.4 = (f32[512,128]{1,0:T(8,128)S(1)}, f32[512,128]{1,0:T(8,128)S(1)}, u32[]{:S(2)}, u32[]{:S(2)}) collective-permute-start(f32[512,128]{1,0:T(8,128)S(1)} %get-tuple-element.25), channel_id=1, source_target_pairs={{1,0},{2,1},{3,2},{4,3},{5,4},{6,5},{7,6},{8,7},{9,8},{10,9},{11,1... | collective-permute-start | bytes 786440 | tf_op jit(solution)/shard_map/ppermute | solution.py:30
  18.0 15.2 %collective-permute-start.3 = (f32[512,128]{1,0:T(8,128)S(1)}, f32[512,128]{1,0:T(8,128)S(1)}, u32[]{:S(2)}, u32[]{:S(2)}) collective-permute-start(f32[512,128]{1,0:T(8,128)S(1)} %get-tuple-element.30), channel_id=1, source_target_pairs={{0,1},{1,2},{2,3},{3,4},{4,5},{5,6},{6,7},{7,8},{8,9},{9,10},{10,1... | collective-permute-start | bytes 786440 | tf_op jit(solution)/shard_map/ppermute | solution.py:29
  33.9 10.4 %collective-permute-start.6 = (f32[512,128]{1,0:T(8,128)S(1)}, f32[512,128]{1,0:T(8,128)S(1)}, u32[]{:S(2)}, u32[]{:S(2)}) collective-permute-start(f32[512,128]{1,0:T(8,128)S(1)} %get-tuple-element.21), channel_id=1, source_target_pairs={{1,0},{2,1},{3,2},{4,3},{5,4},{6,5},{7,6},{8,7},{9,8},{10,9},{11,1... | collective-permute-start | bytes 786440 | tf_op jit(solution)/shard_map/ppermute | solution.py:30
  35.3 14.7 %collective-permute-start.5 = (f32[512,128]{1,0:T(8,128)S(1)}, f32[512,128]{1,0:T(8,128)S(1)}, u32[]{:S(2)}, u32[]{:S(2)}) collective-permute-start(f32[512,128]{1,0:T(8,128)S(1)} %get-tuple-element.23), channel_id=1, source_target_pairs={{0,1},{1,2},{2,3},{3,4},{4,5},{5,6},{6,7},{7,8},{8,9},{9,10},{10,1... | collective-permute-start | bytes 786440 | tf_op jit(solution)/shard_map/ppermute | solution.py:29
  45.0 15.5 %copy-start.3 = (f32[512,128]{1,0:T(8,128)}, f32[512,128]{1,0:T(8,128)S(1)}, u32[]{:S(2)}) copy-start(f32[512,128]{1,0:T(8,128)S(1)} %div.78) | copy-start | bytes 786436
  45.0 8.5 %collective-permute-start.7 = (f32[512,128]{1,0:T(8,128)S(1)}, f32[512,128]{1,0:T(8,128)S(1)}, u32[]{:S(2)}, u32[]{:S(2)}) collective-permute-start(f32[512,128]{1,0:T(8,128)S(1)} %div.78), channel_id=1, source_target_pairs={{0,1},{1,2},{2,3},{3,4},{4,5},{5,6},{6,7},{7,8},{8,9},{9,10},{10,1... | collective-permute-start | bytes 786440 | tf_op jit(solution)/shard_map/ppermute | solution.py:29
  50.7 9.8 %collective-permute-start.8 = (f32[512,128]{1,0:T(8,128)S(1)}, f32[512,128]{1,0:T(8,128)S(1)}, u32[]{:S(2)}, u32[]{:S(2)}) collective-permute-start(f32[512,128]{1,0:T(8,128)S(1)} %get-tuple-element.19), channel_id=1, source_target_pairs={{1,0},{2,1},{3,2},{4,3},{5,4},{6,5},{7,6},{8,7},{9,8},{10,9},{11,1... | collective-permute-start | bytes 786440 | tf_op jit(solution)/shard_map/ppermute | solution.py:30
  61.9 15.7 %all-to-all-start = ((f32[16,8,128]{2,1,0:T(8,128)}), f32[16,8,128]{2,1,0:T(8,128)S(1)}, u32[]{:S(2)}, u32[]{:S(2)}) async-start(f32[16,8,128]{2,1,0:T(8,128)} %broadcast_in_dim.50), calls=%async_computation | async-start | bytes 131072 | tf_op jit(solution)/shard_map/all_to_all | solution.py:183
  72.3 10.9 %collective-permute-start.9 = (f32[512,128]{1,0:T(8,128)}, f32[512,128]{1,0:T(8,128)}, u32[]{:S(2)}, u32[]{:S(2)}) collective-permute-start(f32[512,128]{1,0:T(8,128)} %get-tuple-element.38), channel_id=1, source_target_pairs={{0,1},{1,2},{2,3},{3,4},{4,5},{5,6},{6,7},{7,8},{8,9},{9,10},{10,1... | collective-permute-start | bytes 786440 | tf_op jit(solution)/shard_map/ppermute | solution.py:29
  76.3 10.5 %collective-permute-start.10 = (f32[512,128]{1,0:T(8,128)}, f32[512,128]{1,0:T(8,128)}, u32[]{:S(2)}, u32[]{:S(2)}) collective-permute-start(f32[512,128]{1,0:T(8,128)} %get-tuple-element.39), channel_id=1, source_target_pairs={{1,0},{2,1},{3,2},{4,3},{5,4},{6,5},{7,6},{8,7},{9,8},{10,9},{11,1... | collective-permute-start | bytes 786440 | tf_op jit(solution)/shard_map/ppermute | solution.py:30
  80.7 2.5 %copy-start.24 = (f32[512,128]{1,0:T(8,128)S(1)}, f32[512,128]{1,0:T(8,128)}, u32[]{:S(2)}) copy-start(f32[512,128]{1,0:T(8,128)} %copy-done.23) | copy-start | bytes 786436
  80.7 2.5 %copy-start.26 = (f32[512,128]{1,0:T(8,128)S(1)}, f32[512,128]{1,0:T(8,128)}, u32[]{:S(2)}) copy-start(f32[512,128]{1,0:T(8,128)} %copy-done.25) | copy-start | bytes 786436
  81.6 1.6 %copy-start.4 = (f32[512,128]{1,0:T(8,128)S(1)}, f32[512,128]{1,0:T(8,128)}, u32[]{:S(2)}) copy-start(f32[512,128]{1,0:T(8,128)} %copy-done.3) | copy-start | bytes 786436
  81.6 1.6 %copy-start.6 = (f32[512,128]{1,0:T(8,128)S(1)}, f32[512,128]{1,0:T(8,128)}, u32[]{:S(2)}) copy-start(f32[512,128]{1,0:T(8,128)} %copy-done.5) | copy-start | bytes 786436
  81.6 1.6 %copy-start.8 = (f32[1,2,512,128]{3,2,1,0:T(8,128)S(1)}, f32[1,2,512,128]{3,2,1,0:T(8,128)}, u32[]{:S(2)}) copy-start(f32[1,2,512,128]{3,2,1,0:T(8,128)} %param.11) | copy-start | bytes 1572868
  81.6 1.6 %copy-start.10 = (f32[2,512,128]{2,1,0:T(8,128)S(1)}, f32[2,512,128]{2,1,0:T(8,128)}, u32[]{:S(2)}) copy-start(f32[2,512,128]{2,1,0:T(8,128)} %copy-done.9) | copy-start | bytes 1572868
  81.6 1.7 %copy-start.22 = (f32[512,128]{1,0:T(8,128)S(1)}, f32[512,128]{1,0:T(8,128)}, u32[]{:S(2)}) copy-start(f32[512,128]{1,0:T(8,128)} %copy-done.21) | copy-start | bytes 786436
  83.3 1.9 %copy-start.12 = (f32[512,128]{1,0:T(8,128)S(1)}, f32[512,128]{1,0:T(8,128)}, u32[]{:S(2)}) copy-start(f32[512,128]{1,0:T(8,128)} %copy-done.11) | copy-start | bytes 786436
  85.3 1.5 %copy-start.16 = (f32[512,128]{1,0:T(8,128)S(1)}, f32[512,128]{1,0:T(8,128)}, u32[]{:S(2)}) copy-start(f32[512,128]{1,0:T(8,128)} %copy-done.15) | copy-start | bytes 786436
  85.3 1.5 %copy-start.18 = (f32[512,128]{1,0:T(8,128)S(1)}, f32[512,128]{1,0:T(8,128)}, u32[]{:S(2)}) copy-start(f32[512,128]{1,0:T(8,128)} %copy-done.17) | copy-start | bytes 786436
  85.3 1.5 %copy-start.20 = (f32[512,128]{1,0:T(8,128)S(1)}, f32[512,128]{1,0:T(8,128)}, u32[]{:S(2)}) copy-start(f32[512,128]{1,0:T(8,128)} %copy-done.19) | copy-start | bytes 786436
  88.7 7.2 %collective-permute-start.11 = (f32[2,512,128]{2,1,0:T(8,128)S(1)}, f32[2,512,128]{2,1,0:T(8,128)S(1)}, u32[]{:S(2)}, u32[]{:S(2)}) collective-permute-start(f32[2,512,128]{2,1,0:T(8,128)S(1)} %maximum_negate_fusion), channel_id=1, source_target_pairs={{0,16},{16,0},{1,17},{17,1},{2,18},{18,2},{3,19},{19,3},{4,20},{20... | collective-permute-start | bytes 1572872 | tf_op jit(solution)/shard_map/ppermute | solution.py:200
  (12 other events, 9.5 us)

commit v3 on v1

v3 whole, which is shorter than its diff:
```python
import jax
import jax.numpy as jnp
from jax import lax
from jax.experimental import pallas as pl
from jax.experimental.pallas import tpu as pltpu
from jax.sharding import PartitionSpec as P

WELL_TERM = 4.0
CHUNK = 64
VMEM = pltpu.VMEM
SMEM = pltpu.SMEM


def row_before(ref, start, count):
    if start == 0:
        return pltpu.roll(ref[0:count], 1, 0)
    return ref[start - 1 : start + count - 1]


def row_after(ref, start, count):
    if start + count == ref.shape[0]:
        return pltpu.roll(ref[start : start + count], count - 1, 0)
    return ref[start + 1 : start + count + 1]


def lane_before(v):
    return pltpu.roll(v, 1, 1)


def lane_after(v):
    return pltpu.roll(v, v.shape[1] - 1, 1)


def chunks_of(rows):
    count = min(CHUNK, rows)
    return [(start, count) for start in range(0, rows, count)]


def fold(v):
    return jnp.sum(v.reshape(v.shape[0] // 8, 8, v.shape[1]), axis=0)


def call(kernel, ins, outs, flops, scalars=0, space=VMEM):
    out_shape = [VMEM(o, jnp.float32) if isinstance(o, tuple) else o for o in outs]
    moved = 4 * sum(x.size for x in ins)
    if space is not None:
        ins = [x if i < scalars else pltpu.with_memory_space_constraint(x, space) for i, x in enumerate(ins)]
    return pl.pallas_call(
        kernel,
        out_shape=out_shape,
        in_specs=[pl.BlockSpec(memory_space=SMEM if i < scalars else VMEM) for i in range(len(ins))],
        out_specs=[pl.BlockSpec(memory_space=VMEM)] * len(outs),
        cost_estimate=pl.CostEstimate(flops=flops, bytes_accessed=moved, transcendentals=0),
        compiler_params=pltpu.CompilerParams(vmem_limit_bytes=16 * 1024 * 1024),
    )(*ins)


def plane_at(i, width, flip):
    return i + flip * (width - 1 - 2 * i)


SIDES = ("y0", "y1", "z0", "z1")


def prepare_kernel(width, place_ref, obs_ref, data_ref, log_ref, storage_ref, mask_ref, head_ref, later_ref, *outs):
    names = ["cond", "own", "base", "rhs", "active", "head", *("f" + s for s in SIDES), *("g" + s for s in SIDES)]
    out = {name: outs[k * width : (k + 1) * width] for k, name in enumerate(names)}
    rest = outs[len(names) * width :]
    fx, gx0, gx1 = (rest[k * (width - 1) : (k + 1) * (width - 1)] for k in range(3))
    rows, depth = outs[0].shape
    at = [plane_at(i, width, place_ref[3]) for i in range(width)]
    for i in range(width):
        for r, n in chunks_of(rows):
            part = slice(r, r + n)
            out["cond"][i][part] = jnp.exp(log_ref[at[i], part])
            out["head"][i][part] = head_ref[0, at[i], part]
    lane = lax.broadcasted_iota(jnp.int32, (min(CHUNK, rows), depth), 1)
    row = lax.broadcasted_iota(jnp.int32, (min(CHUNK, rows), depth), 0)
    for i in range(width):
        cond_i, head_i = out["cond"][i], out["head"][i]
        for r, n in chunks_of(rows):
            part = slice(r, r + n)
            c, h = cond_i[part], head_i[part]

            def pair(cond_n, head_n, inside=None):
                inverse = 1.0 / (c + cond_n)
                face = 2.0 * c * cond_n * inverse
                if inside is not None:
                    face = jnp.where(inside, face, 0.0)
                return face, face * inverse * (h - head_n), cond_n

            well = jnp.where(row * depth + lane + (at[i] * rows + r) * depth == place_ref[0], WELL_TERM, 0.0)
            store = storage_ref[at[i], part]
            own = store + well
            active = mask_ref[at[i], part].astype(jnp.float32)
            out["own"][i][part] = own
            out["active"][i][part] = active
            out["rhs"][i][part] = active * (store * later_ref[0, at[i], part])
            around = {
                "y0": pair(row_before(cond_i, r, n), row_before(head_i, r, n), None if r else row > 0),
                "y1": pair(row_after(cond_i, r, n), row_after(head_i, r, n), None if r + n < rows else row < n - 1),
                "z0": pair(lane_before(c), lane_before(h), lane > 0),
                "z1": pair(lane_after(c), lane_after(h), lane < depth - 1),
            }
            base = own
            for side, (face, slope, cond_n) in around.items():
                out["f" + side][i][part] = face
                out["g" + side][i][part] = slope * cond_n
                base = base + face
            if i > 0:
                base = base + fx[i - 1][part]
            if i < width - 1:
                cond_n = out["cond"][i + 1][part]
                face, slope, _ = pair(cond_n, out["head"][i + 1][part])
                fx[i][part] = face
                gx1[i][part] = slope * cond_n
                gx0[i][part] = -slope * c
                base = base + face
            out["base"][i][part] = base
    lanes = lax.broadcasted_iota(jnp.int32, (1, depth), 1)

    def observe(o, _):
        local = obs_ref[o] - place_ref[4]
        for i in range(width):
            cell = local - at[i] * rows * depth

            @pl.when((cell >= 0) & (cell < rows * depth))
            def _():
                line = pl.ds(cell // depth, 1)
                here = (lanes == cell % depth) & (out["active"][i][line] > 0.0)
                out["rhs"][i][line] += jnp.where(here, out["head"][i][line] - data_ref[o], 0.0)

        return 0

    lax.fori_loop(0, obs_ref.shape[0], observe, 0)


def start_kernel(width, place_ref, *refs):
    mine, others = refs[:2], refs[2:4]
    cond, base, own, rhs, active = (refs[4 + k * width : 4 + (k + 1) * width] for k in range(5))
    refs = refs[4 + 5 * width :]
    field, inverse, outer, outer_slope = refs[:width], refs[width : 2 * width], refs[2 * width : 2 * width + 2], refs[2 * width + 2 : 2 * width + 4]
    sums_ref, least_ref = refs[2 * width + 4 :]
    rows, depth = base[0].shape
    half = mine[0].shape[0]
    sums = jnp.zeros((8, depth), jnp.float32)
    least = jnp.ones((8, depth), jnp.float32)
    for r, n in chunks_of(rows):
        part = slice(r, r + n)
        from_half = slice(r % half, r % half + n)
        mine_here = place_ref[5] == r // half
        faces = []
        for k, i in enumerate((0, width - 1)):
            c = cond[i][part]
            log_n = mine[k][from_half]
            if half < rows:
                log_n = jnp.where(mine_here, log_n, others[k][from_half])
            cond_n = jnp.exp(log_n)
            ratio = cond_n / (c + cond_n)
            face = jnp.where(place_ref[1 + k] > 0, 2.0 * c * ratio, 0.0)
            outer[k][part] = face
            outer_slope[k][part] = face * ratio
            faces.append(face)
        for i in range(width):
            total = base[i][part]
            if i == 0:
                total = total + faces[0]
            if i == width - 1:
                total = total + faces[1]
            here = active[i][part] > 0.0
            inv = 1.0 / total
            least_here = jnp.where(here, own[i][part] * inv, 1.0)
            inv = jnp.where(here, inv, 0.0)
            right = rhs[i][part]
            v = right * inv
            field[i][part] = v
            inverse[i][part] = inv
            sums = sums + fold(v * right)
            least = jnp.minimum(least, jnp.min(least_here.reshape(n // 8, 8, depth), axis=0))
    sums_ref[...] = sums
    least_ref[...] = least


def inner_kernel(width, *refs):
    count = 2 + 2 * len(SIDES)
    v, own, *coefs = (refs[k * width : (k + 1) * width] for k in range(count))
    rest = refs[count * width :]
    fx, gx0, gx1 = (rest[k * (width - 1) : (k + 1) * (width - 1)] for k in range(3))
    outs = rest[3 * (width - 1) :]
    image, terms = outs[:width], outs[width:]
    faces, slopes = coefs[: len(SIDES)], coefs[len(SIDES) :]
    rows = v[0].shape[0]
    for i in range(width):
        for r, n in chunks_of(rows):
            part = slice(r, r + n)
            here = v[i][part]
            total = own[i][part] * here
            term = jnp.zeros_like(here)
            around = (row_before(v[i], r, n), row_after(v[i], r, n), lane_before(here), lane_after(here))
            for k, other in enumerate(around):
                step = here - other
                total = total + faces[k][i][part] * step
                term = term + slopes[k][i][part] * step
            if i > 0:
                step = here - v[i - 1][part]
                total = total + fx[i - 1][part] * step
                term = term + gx0[i - 1][part] * step
            if i < width - 1:
                step = here - v[i + 1][part]
                total = total + fx[i][part] * step
                term = term + gx1[i][part] * step
            image[i][part] = total
            terms[i][part] = term


def outer_image(width, refs, part):
    inner, v, outer, halo = refs
    result = []
    for i in range(width):
        w, here = inner[i][part], v[i][part]
        if i == 0:
            w = w + outer[0][part] * (here - halo[0][part])
        if i == width - 1:
            w = w + outer[1][part] * (here - halo[1][part])
        result.append((here, w))
    return result


def edge_kernel(width, *refs):
    slope, head, heads_halo = refs[:2], refs[2 : 2 + width], refs[2 + width : 4 + width]
    refs = refs[4 + width :]
    count = (len(refs) - 2) // (3 * width + 2)
    sets = [refs[k * (2 * width + 2) : (k + 1) * (2 * width + 2)] for k in range(count)]
    weight, outs = refs[count * (2 * width + 2) :][:2], refs[count * (2 * width + 2) + 2 :]
    rows = slope[0].shape[0]
    for r, n in chunks_of(rows):
        part = slice(r, r + n)
        for k, i in enumerate((0, width - 1)):
            weight[k][part] = slope[k][part] * (head[i][part] - heads_halo[k][part])
        for j, (*arrays,) in enumerate(sets):
            v, halo, terms = arrays[:width], arrays[width : width + 2], arrays[width + 2 :]
            for i in range(width):
                outs[j * width + i][part] = outer_term(width, i, terms, v, halo, weight, part)


def outer_term(width, i, terms, v, halo, weight, part):
    term = terms[i][part]
    for k, end in enumerate((0, width - 1)):
        if i == end:
            term = term + weight[k][part] * (v[i][part] - halo[k][part])
    return term


def finish_kernel(width, *refs):
    inner, v, inverse = (refs[k * width : (k + 1) * width] for k in range(3))
    outer, halo = refs[3 * width : 3 * width + 2], refs[3 * width + 2 : 3 * width + 4]
    following = refs[3 * width + 4 : 4 * width + 4]
    odd_ref, even_ref = refs[4 * width + 4 :]
    rows, depth = v[0].shape
    odd = jnp.zeros((8, depth), jnp.float32)
    even = jnp.zeros((8, depth), jnp.float32)
    for r, n in chunks_of(rows):
        part = slice(r, r + n)
        for i, (here, w) in enumerate(outer_image(width, (inner, v, outer, halo), part)):
            new = w * inverse[i][part]
            following[i][part] = new
            odd = odd + fold(here * w)
            even = even + fold(new * w)
    odd_ref[...] = odd
    even_ref[...] = even


def last_kernel(width, *refs):
    inner, v, terms = (refs[k * width : (k + 1) * width] for k in range(3))
    outer, halo, weight = (refs[3 * width + 2 * k : 3 * width + 2 * k + 2] for k in range(3))
    refs = refs[3 * width + 6 :]
    earlier, least_ref, out_ref, whole_terms = refs[:5], refs[5], refs[6], refs[7:]
    rows, depth = v[0].shape
    odd = jnp.zeros((8, depth), jnp.float32)
    for r, n in chunks_of(rows):
        part = slice(r, r + n)
        for i, (here, w) in enumerate(outer_image(width, (inner, v, outer, halo), part)):
            odd = odd + fold(here * w)
            whole_terms[i][part] = outer_term(width, i, terms, v, halo, weight, part)
    sums = [jnp.sum(x, axis=0, keepdims=True) for x in (*(e[...] for e in earlier), odd)]
    least = jnp.min(least_ref[...], axis=0, keepdims=True)
    told = jnp.concatenate([*sums, least, least], axis=0)
    for k in range(out_ref.shape[0]):
        out_ref[k] = told


def combine(moments, least):
    m0, m1, m2, m3, m4, m5 = moments
    most = 2.0 - least
    alpha_low, alpha_high = 1.0 / most, 1.0 / least
    beta_high = (1.0 - least) * (1.0 - least) / (least * most)

    def alpha_of(rz, curve):
        return jnp.clip(jnp.where(curve > 0.0, rz / curve, alpha_low), alpha_low, alpha_high)

    def beta_of(rz_new, rz):
        return jnp.clip(jnp.where(rz > 0.0, rz_new / rz, 0.0), 0.0, beta_high)

    a0 = alpha_of(m0, m1)
    rz1 = m0 - 2.0 * a0 * m1 + a0 * a0 * m2
    b0 = beta_of(rz1, m0)
    u = 1.0 + b0
    curve1 = u * u * m1 - 2.0 * a0 * u * m2 + a0 * a0 * m3
    a1 = alpha_of(rz1, curve1)
    c1 = -a0 - a1 * u
    c2 = a0 * a1
    rz2 = m0 + 2.0 * c1 * m1 + (2.0 * c2 + c1 * c1) * m2 + 2.0 * c1 * c2 * m3 + c2 * c2 * m4
    b1 = beta_of(rz2, rz1)
    q0 = 1.0 + b1 * u
    q1 = c1 - b1 * a0
    q2 = c2
    curve2 = q0 * q0 * m1 + 2.0 * q0 * q1 * m2 + (2.0 * q0 * q2 + q1 * q1) * m3 + 2.0 * q1 * q2 * m4 + q2 * q2 * m5
    a2 = alpha_of(rz2, curve2)
    return a0 + a1 * u + a2 * q0, a2 * q1 - a1 * a0, a2 * q2


def result_kernel(width, place_ref, told_ref, *refs):
    fields = [refs[k * width : (k + 1) * width] for k in range(3)]
    terms = [refs[k * width : (k + 1) * width] for k in range(3, 6)]
    adjoint_ref, gradient_ref = refs[6 * width :]
    sums = told_ref[0]
    least = told_ref[0]
    for k in range(1, told_ref.shape[0]):
        sums = sums + told_ref[k]
        least = jnp.minimum(least, told_ref[k])
    sums = jnp.sum(sums, axis=1, keepdims=True)
    least = jnp.min(least, axis=1, keepdims=True)
    coefs = combine([sums[i : i + 1] for i in range(6)], least[6:7])
    rows, depth = fields[0][0].shape
    wide = [jnp.broadcast_to(c, (8, depth)) for c in coefs]
    for r, n in chunks_of(rows):
        part = slice(r, r + n)
        scale = [jnp.concatenate([c] * (n // 8), axis=0) for c in wide]
        for i in range(width):
            at = plane_at(i, width, place_ref[3])
            adjoint_ref[0, at, part] = sum(c * f[i][part] for c, f in zip(scale, fields))
            gradient_ref[at, part] = -sum(c * t[i][part] for c, t in zip(scale, terms))


def swap_planes(first, last):
    count = lax.axis_size("slab")
    near = [(i, i ^ 1) for i in range(count) if i ^ 1 < count]
    far = [(a, b) for i in range(1, count - 1, 2) for a, b in ((i, i + 1), (i + 1, i))]
    return lax.ppermute(first, "slab", far), lax.ppermute(last, "slab", near)


def on_device(
    log_conductivity, storage, active_mask, heads, adjoint_next, pump_cells, obs_cells, obs_data
):
    width, rows, depth = log_conductivity.shape
    plane = (rows, depth)
    slabs = lax.axis_size("slab")
    place = lax.axis_index("slab")
    test = lax.axis_index("test")
    two_tests = lax.axis_size("test") == 2
    cells_here = width * rows * depth
    offset = place * cells_here
    flip = place % 2
    far_partner = jnp.where(flip == 0, place - 1, place + 1)
    half = rows // 2
    ends = [plane_at(i, width, flip) for i in (0, width - 1)]

    def piece(array, i, start, count):
        return lax.dynamic_slice(array, (ends[i], start, 0), (1, count, depth))[0]

    if two_tests:
        logs = swap_planes(*(piece(log_conductivity, i, test * half, half) for i in range(2)))
    else:
        logs = swap_planes(*(piece(log_conductivity, i, 0, rows) for i in range(2)))
    flags = jnp.stack(
        [
            pump_cells[0] - offset,
            ((far_partner >= 0) & (far_partner < slabs)).astype(jnp.int32),
            (place + 1 - 2 * flip < slabs).astype(jnp.int32),
            flip,
            offset,
            test if two_tests else jnp.int32(0),
        ]
    )
    planes = [plane] * width
    prepared = call(
        lambda *refs: prepare_kernel(width, *refs),
        [flags, obs_cells, obs_data[0], log_conductivity, storage, active_mask, heads, adjoint_next],
        planes * (6 + 2 * len(SIDES)) + [plane] * (3 * (width - 1)),
        100 * cells_here,
        scalars=3,
        space=pltpu.HBM,
    )
    take = lambda k: prepared[k * width : (k + 1) * width]
    cond, own, base, rhs, active, head = (take(k) for k in range(6))
    coefs = prepared[6 * width :]
    if two_tests:
        logs, prepared = lax.optimization_barrier((logs, prepared))
        logs_sent = [lax.ppermute(x, "test", [(0, 1), (1, 0)]) for x in logs]
    else:
        logs_sent = logs
    heads_halo = swap_planes(head[0], head[-1])
    started = call(
        lambda *refs: start_kernel(width, *refs),
        [flags, *logs, *logs_sent, *cond, *base, *own, *rhs, *active],
        planes * 2 + [plane] * 4 + [(8, depth)] * 2,
        20 * cells_here,
        scalars=1,
    )
    field, inverse = started[:width], started[width : 2 * width]
    outer, outer_slope = started[2 * width : 2 * width + 2], started[2 * width + 2 : 2 * width + 4]
    first_sum, least = started[2 * width + 4 :]

    sums, fields, sets = [first_sum], [], []
    for step in range(3):
        halo = swap_planes(field[0], field[-1])
        fields += field
        inner = call(
            lambda *refs: inner_kernel(width, *refs),
            [*field, *own, *coefs],
            planes * 2,
            30 * cells_here,
        )
        image, terms = inner[:width], inner[width:]
        if step == 0:
            halo, heads_halo = lax.optimization_barrier((halo, heads_halo))
        if step < 2:
            sets += [*field, *halo, *terms]
            *field, odd, even = call(
                lambda *refs: finish_kernel(width, *refs),
                [*image, *field, *inverse, *outer, *halo],
                planes + [(8, depth)] * 2,
                10 * cells_here,
            )
            sums += [odd, even]
    stored = jax.ShapeDtypeStruct(plane, jnp.float32)
    weight_0, weight_1, *whole_terms = call(
        lambda *refs: edge_kernel(width, *refs),
        [*outer_slope, *head, *heads_halo, *sets],
        [plane] * 2 + [stored] * (2 * width),
        10 * cells_here,
    )
    told, *last_terms = call(
        lambda *refs: last_kernel(width, *refs),
        [*image, *field, *terms, *outer, *halo, weight_0, weight_1, *sums, least],
        [jax.ShapeDtypeStruct((slabs, 8, depth), jnp.float32)] + [stored] * width,
        5 * cells_here,
    )
    told = lax.all_to_all(told, "slab", 0, 0, tiled=True)
    adjoint, gradient = call(
        lambda *refs: result_kernel(width, *refs),
        [flags, told, *fields, *whole_terms, *last_terms],
        [jax.ShapeDtypeStruct((1, width, rows, depth), jnp.float32), (width, rows, depth)],
        20 * cells_here,
        scalars=1,
        space=None,
    )
    if two_tests:
        gradient = gradient + lax.ppermute(gradient, "test", [(0, 1), (1, 0)])
    else:
        gradient = lax.psum(gradient, "test")
    return adjoint, gradient


def solution(mesh):
    return jax.shard_map(
        on_device,
        mesh=mesh,
        in_specs=(
            P("slab", None, None),
            P("slab", None, None),
            P("slab", None, None),
            P("test", "slab", None, None),
            P("test", "slab", None, None),
            P("test"),
            P(),
            P("test", None),
        ),
        out_specs=(P("test", "slab", None, None), P("slab", None, None)),
        check_vma=False,
    )
```

time: 106 us -> 92.8 us (0.88)
  starting transfers between devices: 45.4 us -> 25.3 us
  waiting for transfers between devices: 20.2 us -> 39.6 us
  between operations: 17 us -> 1.46 us
  blocking collectives: 0 us -> 13.5 us
  other arithmetic: 12.9 us -> 0.85 us
  Pallas kernels: 0 us -> 9.73 us
  local copies, waits for them, and re-layouts: 9.66 us -> 1.75 us
    ppermute x11 -> x13, waiting for transfers between devices: 19.8 us -> 39.6 us  [the longest x10 38 us: swap_planes(): return (lax.ppermute(first, 'slab', far), lax.ppermute(last, 'slab', near))]
    all_to_all x0 -> x1, blocking collectives: none -> 13.5 us  [on_device(): told = lax.all_to_all(told, 'slab', 0, 0, tiled=True)]
    ppermute x11 -> x13, starting transfers between devices: 36 us -> 25.3 us  [the longest x10 21.6 us: swap_planes(): return (lax.ppermute(first, 'slab', far), lax.ppermute(last, 'slab', near))]
    pallas_call x0 -> x10, Pallas kernels: none -> 9.73 us  [call(): pl.pallas_call(kernel, out_shape=out_shape, in_specs=[pl.BlockSpec(memory...]
    all_to_all x1 -> x0, starting transfers between devices: 9.41 us -> none  [on_device(): lax.all_to_all(jnp.broadcast_to(payload[None], (slabs, *payload.shape)),...]
    another operation x2 -> x0, other arithmetic: 4.33 us -> none  [on_device(): terms = -jnp.stack(terms)]
    unnamed x50 -> x4, local copies, waits for them, and re-layouts: 4.94 us -> 0.67 us
    div x6 -> x0, other arithmetic: 2.66 us -> none  [the longest x2 1.66 us: on_device(): field = [rhs[i] / diag[i] for i in range(width)]]
  transfers between devices with their start and end apart: 12 -> 13, of which waited for: 8 -> 5; matrix products, arithmetic and copies ran while one was open for 10% -> 0% of each run, Pallas kernels for 0% -> 8%
where the time goes in v3:
time: 92.8 us; the launch traced here: 92.1 us
  waiting for transfers between devices  39.6 us (43%)
  starting transfers between devices  25.3 us (27%)
  blocking collectives  13.5 us (15%)
  Pallas kernels  9.73 us (10%)
  local copies, waits for them, and re-layouts  1.75 us (2%)
  between operations  1.46 us (2%)
    ppermute x10, waiting for transfers between devices, swap_planes(): return (lax.ppermute(first, 'slab', far), lax.ppermute(last, 'slab', near))  38 us
    ppermute x10, starting transfers between devices, swap_planes(): return (lax.ppermute(first, 'slab', far), lax.ppermute(last, 'slab', near))  21.6 us
    all_to_all x1, blocking collectives, on_device(): told = lax.all_to_all(told, 'slab', 0, 0, tiled=True)  13.5 us
    pallas_call x10, Pallas kernels, call(): pl.pallas_call(kernel, out_shape=out_shape, in_specs=[pl.BlockSpec(memory...  9.73 us
    ppermute x1, starting transfers between devices, on_device(): gradient = gradient + lax.ppermute(gradient, 'test', [(0, 1), (1, 0)])  2.27 us
  transfers between devices with their start and end apart: 13, of which 5 were waited for; matrix products, arithmetic and copies ran while one was open for 0% of the time, Pallas kernels for 8%

profile of v3, /device:TPU:1, one launch (start us, length us, event | category | flops | bytes accessed | tf_op | source)
XLA Modules:
  0.0 92.1 jit_solution(6988040838431014049)
XLA Ops:
  0.7 1.0 %dynamic-slice_bitcast_fusion = (f32[256,128]{1,0:T(8,128)S(1)}, f32[256,128]{1,0:T(8,128)S(1)}) fusion(f32[2,512,128]{2,1,0:T(8,128)} %refs_3_.1, s32[]{:T(128)S(6)} %select_n.24, s32[]{:T(128)S(6)} %select_n.23, s32[]{:T(128)S(6)} %select_n.22), kind=kLoop, calls=%fused_computation | loop fusion | bytes 524300 | tf_op jit(solution)/shard_map/squeeze | solution.py:369
  1.6 0.7 collective-permute-start
  2.3 4.6 %collective-permute-start.1 = (f32[256,128]{1,0:T(8,128)S(1)}, f32[256,128]{1,0:T(8,128)S(1)}, u32[]{:S(2)}, u32[]{:S(2)}) collective-permute-start(f32[256,128]{1,0:T(8,128)S(1)} %get-tuple-element.158), channel_id=1, source_target_pairs={{0,1},{1,0},{2,3},{3,2},{4,5},{5,4},{6,7},{7,6},{8,9},{9,8},{10,11... | collective-permute-start | bytes 393224 | tf_op jit(solution)/shard_map/ppermute | solution.py:349
  7.5 0.1 stack.35.refs_0_
  7.6 0.7 copy-done
  8.3 4.3 %shard_map.95 = (f32[512,128]{1,0:T(8,128)S(1)}, f32[512,128]{1,0:T(8,128)S(1)}, f32[512,128]{1,0:T(8,128)S(1)}, f32[512,128]{1,0:T(8,128)S(1)}, f32[512,128]{1,...) custom-call(s32[6]{0:T(128)S(1)} %stack.35.refs_0_, ...), custom_call_target="tpu_custom_call" | custom-call | flops 13107200 | bytes 2621976 | tf_op jit(solution)/shard_map/pallas_call | solution.py:48
  12.7 1.4 %collective-permute-start.2 = (f32[256,128]{1,0:T(8,128)S(1)}, f32[256,128]{1,0:T(8,128)S(1)}, u32[]{:S(2)}, u32[]{:S(2)}) collective-permute-start(f32[256,128]{1,0:T(8,128)S(1)} %collective-permute-done.refs_1_), channel_id=1, source_target_pairs={{0,16},{16,0},{1,17},{17,1},{2,18},{18,2},{3,19},{19,3},{4,20},{20... | collective-permute-start | bytes 393224 | tf_op jit(solution)/shard_map/ppermute | solution.py:399
  14.1 0.7 collective-permute-start.6
  14.7 3.7 %collective-permute-start.7 = (f32[512,128]{1,0:T(8,128)S(1)}, f32[512,128]{1,0:T(8,128)S(1)}, u32[]{:S(2)}, u32[]{:S(2)}) collective-permute-start(f32[512,128]{1,0:T(8,128)S(1)} %get-tuple-element.91.refs_3_), channel_id=1, source_target_pairs={{0,1},{1,0},{2,3},{3,2},{4,5},{5,4},{6,7},{7,6},{8,9},{9,8},{10,11... | collective-permute-start | bytes 786440 | tf_op jit(solution)/shard_map/ppermute | solution.py:349
  18.5 0.9 %shard_map.96 = (f32[512,128]{1,0:T(8,128)S(1)}, f32[512,128]{1,0:T(8,128)S(1)}, f32[512,128]{1,0:T(8,128)S(1)}, f32[512,128]{1,0:T(8,128)S(1)}, f32[512,128]{1,...) custom-call(s32[6]{0:T(128)S(1)} %stack.35.refs_0_, ...), custom_call_target="tpu_custom_call" | custom-call | flops 2621440 | bytes 3145752 | tf_op jit(solution)/shard_map/pallas_call | solution.py:48
  19.4 0.7 collective-permute-start.4
  20.1 3.7 %collective-permute-start.5 = (f32[512,128]{1,0:T(8,128)S(1)}, f32[512,128]{1,0:T(8,128)S(1)}, u32[]{:S(2)}, u32[]{:S(2)}) collective-permute-start(f32[512,128]{1,0:T(8,128)S(1)} %get-tuple-element.114.refs_1_.refs_3_.refs_7_), channel_id=1, source_target_pairs={{0,1},{1,0},{2,3},{3,2},{4,5},{5,4},{6,7},{7,6},{8,9},{9,8},{10,11... | collective-permute-start | bytes 786440 | tf_op jit(solution)/shard_map/ppermute | solution.py:349
  23.8 0.6 shard_map.97
  24.5 10.8 %collective-permute-done.7.refs_5_ = f32[512,128]{1,0:T(8,128)S(1)} collective-permute-done((f32[512,128]{1,0:T(8,128)S(1)}, f32[512,128]{1,0:T(8,128)S(1)}, u32[]{:S(2)}, u32[]{:S(2)}) %collective-permute-start.7) | collective-permute-done | bytes 262176 | tf_op jit(solution)/shard_map/ppermute | solution.py:349
  35.3 5.9 %collective-permute-done.5.refs_9_ = f32[512,128]{1,0:T(8,128)S(1)} collective-permute-done((f32[512,128]{1,0:T(8,128)S(1)}, f32[512,128]{1,0:T(8,128)S(1)}, u32[]{:S(2)}, u32[]{:S(2)}) %collective-permute-start.5) | collective-permute-done | bytes 262176 | tf_op jit(solution)/shard_map/ppermute | solution.py:349
  41.2 0.2 shard_map.98
  41.4 0.7 collective-permute-start.8
  42.1 3.2 %collective-permute-start.9 = (f32[512,128]{1,0:T(8,128)S(1)}, f32[512,128]{1,0:T(8,128)S(1)}, u32[]{:S(2)}, u32[]{:S(2)}) collective-permute-start(f32[512,128]{1,0:T(8,128)S(1)} %get-tuple-element.124.refs_1_.refs_3_.refs_13_.refs_5_), channel_id=1, source_target_pairs={{0,1},{1,0},{2,3},{3,2},{4,5},{5,4},{6,7},{7,6},{8,9},{9,8},{10,11... | collective-permute-start | bytes 786440 | tf_op jit(solution)/shard_map/ppermute | solution.py:349
  45.3 0.6 shard_map.99
  45.9 11.1 %collective-permute-done.9.refs_9_.refs_15_ = f32[512,128]{1,0:T(8,128)S(1)} collective-permute-done((f32[512,128]{1,0:T(8,128)S(1)}, f32[512,128]{1,0:T(8,128)S(1)}, u32[]{:S(2)}, u32[]{:S(2)}) %collective-permute-start.9) | collective-permute-done | bytes 262176 | tf_op jit(solution)/shard_map/ppermute | solution.py:349
  57.0 0.2 shard_map.100
  57.2 0.7 collective-permute-start.10
  57.9 3.1 %collective-permute-start.11 = (f32[512,128]{1,0:T(8,128)S(1)}, f32[512,128]{1,0:T(8,128)S(1)}, u32[]{:S(2)}, u32[]{:S(2)}) collective-permute-start(f32[512,128]{1,0:T(8,128)S(1)} %get-tuple-element.128.refs_1_.refs_3_.refs_7_), channel_id=1, source_target_pairs={{0,1},{1,0},{2,3},{3,2},{4,5},{5,4},{6,7},{7,6},{8,9},{9,8},{10,11... | collective-permute-start | bytes 786440 | tf_op jit(solution)/shard_map/ppermute | solution.py:349
  61.0 0.2 shard_map.102
  61.2 0.6 shard_map.101
  61.8 10.2 %collective-permute-done.11.refs_9_ = f32[512,128]{1,0:T(8,128)S(1)} collective-permute-done((f32[512,128]{1,0:T(8,128)S(1)}, f32[512,128]{1,0:T(8,128)S(1)}, u32[]{:S(2)}, u32[]{:S(2)}) %collective-permute-start.11) | collective-permute-done | bytes 262176 | tf_op jit(solution)/shard_map/ppermute | solution.py:349
  72.0 0.2 shard_map.103
  72.2 13.5 %all_to_all.5.refs_1_ = f32[16,8,128]{2,1,0:T(8,128)S(1)} all-to-all(f32[16,8,128]{2,1,0:T(8,128)S(1)} %get-tuple-element.149), channel_id=1, replica_groups=mesh['test'=2,'slab'=16] {'slab'}, dimensions={0} | all-to-all | bytes 131072 | tf_op jit(solution)/shard_map/all_to_all | solution.py:449
  85.7 1.7 %shard_map.104 = (f32[1,2,512,128]{3,2,1,0:T(8,128)}, f32[2,512,128]{2,1,0:T(8,128)S(1)}) custom-call(s32[6]{0:T(128)S(1)} %stack.35.refs_0_, f32[16,8,128]{2,1,0:T(8,128)S(1)} %all_to_all.5.refs_1_, f32[512,128]{1,0:T(8,128)S(1)} %get-tuple-element.113.refs_0_.refs_2_.refs_6_, f32[512,128]{1,0:T(8,128)S(1)} %get-tuple-element.114.refs_1_.refs_3_.refs_7_, ...), custom_call_target="tpu_custom_call" | custom-call | flops 2621440 | bytes 3211288 | tf_op jit(solution)/shard_map/pallas_call | solution.py:48
  87.5 2.3 %collective-permute-start.12 = (f32[2,512,128]{2,1,0:T(8,128)S(1)}, f32[2,512,128]{2,1,0:T(8,128)S(1)}, u32[]{:S(2)}, u32[]{:S(2)}) collective-permute-start(f32[2,512,128]{2,1,0:T(8,128)S(1)} %get-tuple-element.157), channel_id=1, source_target_pairs={{0,16},{16,0},{1,17},{17,1},{2,18},{18,2},{3,19},{19,3},{4,20},{20... | collective-permute-start | bytes 1572872 | tf_op jit(solution)/shard_map/ppermute | solution.py:459
  89.7 1.5 %collective-permute-done.12 = f32[2,512,128]{2,1,0:T(8,128)S(1)} collective-permute-done((f32[2,512,128]{2,1,0:T(8,128)S(1)}, f32[2,512,128]{2,1,0:T(8,128)S(1)}, u32[]{:S(2)}, u32[]{:S(2)}) %collective-permute-start.12) | collective-permute-done | bytes 524320 | tf_op jit(solution)/shard_map/ppermute | solution.py:459
  91.3 0.8 add.33
  (12 shorter events, 0.0 us)
Async XLA Ops:
  1.6 11.0 %collective-permute-start = (f32[256,128]{1,0:T(8,128)S(1)}, f32[256,128]{1,0:T(8,128)S(1)}, u32[]{:S(2)}, u32[]{:S(2)}) collective-permute-start(f32[256,128]{1,0:T(8,128)S(1)} %get-tuple-element.159), channel_id=1, source_target_pairs={{1,2},{2,1},{3,4},{4,3},{5,6},{6,5},{7,8},{8,7},{9,10},{10,9},{11,... | collective-permute-start | bytes 393224 | tf_op jit(solution)/shard_map/ppermute | solution.py:349
  2.3 10.3 %collective-permute-start.1 = (f32[256,128]{1,0:T(8,128)S(1)}, f32[256,128]{1,0:T(8,128)S(1)}, u32[]{:S(2)}, u32[]{:S(2)}) collective-permute-start(f32[256,128]{1,0:T(8,128)S(1)} %get-tuple-element.158), channel_id=1, source_target_pairs={{0,1},{1,0},{2,3},{3,2},{4,5},{5,4},{6,7},{7,6},{8,9},{9,8},{10,11... | collective-permute-start | bytes 393224 | tf_op jit(solution)/shard_map/ppermute | solution.py:349
  7.6 0.7 copy-start
  7.6 0.7 copy-start.1
  12.7 5.8 %collective-permute-start.2 = (f32[256,128]{1,0:T(8,128)S(1)}, f32[256,128]{1,0:T(8,128)S(1)}, u32[]{:S(2)}, u32[]{:S(2)}) collective-permute-start(f32[256,128]{1,0:T(8,128)S(1)} %collective-permute-done.refs_1_), channel_id=1, source_target_pairs={{0,16},{16,0},{1,17},{17,1},{2,18},{18,2},{3,19},{19,3},{4,20},{20... | collective-permute-start | bytes 393224 | tf_op jit(solution)/shard_map/ppermute | solution.py:399
  14.1 4.4 %collective-permute-start.3 = (f32[256,128]{1,0:T(8,128)S(1)}, f32[256,128]{1,0:T(8,128)S(1)}, u32[]{:S(2)}, u32[]{:S(2)}) collective-permute-start(f32[256,128]{1,0:T(8,128)S(1)} %collective-permute-done.1.refs_2_), channel_id=1, source_target_pairs={{0,16},{16,0},{1,17},{17,1},{2,18},{18,2},{3,19},{19,3},{4,20},{20... | collective-permute-start | bytes 393224 | tf_op jit(solution)/shard_map/ppermute | solution.py:399
  14.1 10.4 %collective-permute-start.6 = (f32[512,128]{1,0:T(8,128)S(1)}, f32[512,128]{1,0:T(8,128)S(1)}, u32[]{:S(2)}, u32[]{:S(2)}) collective-permute-start(f32[512,128]{1,0:T(8,128)S(1)} %get-tuple-element.90.refs_2_), channel_id=1, source_target_pairs={{1,2},{2,1},{3,4},{4,3},{5,6},{6,5},{7,8},{8,7},{9,10},{10,9},{11,... | collective-permute-start | bytes 786440 | tf_op jit(solution)/shard_map/ppermute | solution.py:349
  14.7 20.5 %collective-permute-start.7 = (f32[512,128]{1,0:T(8,128)S(1)}, f32[512,128]{1,0:T(8,128)S(1)}, u32[]{:S(2)}, u32[]{:S(2)}) collective-permute-start(f32[512,128]{1,0:T(8,128)S(1)} %get-tuple-element.91.refs_3_), channel_id=1, source_target_pairs={{0,1},{1,0},{2,3},{3,2},{4,5},{5,4},{6,7},{7,6},{8,9},{9,8},{10,11... | collective-permute-start | bytes 786440 | tf_op jit(solution)/shard_map/ppermute | solution.py:349
  19.4 15.9 %collective-permute-start.4 = (f32[512,128]{1,0:T(8,128)S(1)}, f32[512,128]{1,0:T(8,128)S(1)}, u32[]{:S(2)}, u32[]{:S(2)}) collective-permute-start(f32[512,128]{1,0:T(8,128)S(1)} %get-tuple-element.113.refs_0_.refs_2_.refs_6_), channel_id=1, source_target_pairs={{1,2},{2,1},{3,4},{4,3},{5,6},{6,5},{7,8},{8,7},{9,10},{10,9},{11,... | collective-permute-start | bytes 786440 | tf_op jit(solution)/shard_map/ppermute | solution.py:349
  20.1 21.1 %collective-permute-start.5 = (f32[512,128]{1,0:T(8,128)S(1)}, f32[512,128]{1,0:T(8,128)S(1)}, u32[]{:S(2)}, u32[]{:S(2)}) collective-permute-start(f32[512,128]{1,0:T(8,128)S(1)} %get-tuple-element.114.refs_1_.refs_3_.refs_7_), channel_id=1, source_target_pairs={{0,1},{1,0},{2,3},{3,2},{4,5},{5,4},{6,7},{7,6},{8,9},{9,8},{10,11... | collective-permute-start | bytes 786440 | tf_op jit(solution)/shard_map/ppermute | solution.py:349
  41.4 4.5 %collective-permute-start.8 = (f32[512,128]{1,0:T(8,128)S(1)}, f32[512,128]{1,0:T(8,128)S(1)}, u32[]{:S(2)}, u32[]{:S(2)}) collective-permute-start(f32[512,128]{1,0:T(8,128)S(1)} %get-tuple-element.123.refs_0_.refs_2_.refs_12_.refs_4_), channel_id=1, source_target_pairs={{1,2},{2,1},{3,4},{4,3},{5,6},{6,5},{7,8},{8,7},{9,10},{10,9},{11,... | collective-permute-start | bytes 786440 | tf_op jit(solution)/shard_map/ppermute | solution.py:349
  42.1 14.9 %collective-permute-start.9 = (f32[512,128]{1,0:T(8,128)S(1)}, f32[512,128]{1,0:T(8,128)S(1)}, u32[]{:S(2)}, u32[]{:S(2)}) collective-permute-start(f32[512,128]{1,0:T(8,128)S(1)} %get-tuple-element.124.refs_1_.refs_3_.refs_13_.refs_5_), channel_id=1, source_target_pairs={{0,1},{1,0},{2,3},{3,2},{4,5},{5,4},{6,7},{7,6},{8,9},{9,8},{10,11... | collective-permute-start | bytes 786440 | tf_op jit(solution)/shard_map/ppermute | solution.py:349
  57.2 4.6 %collective-permute-start.10 = (f32[512,128]{1,0:T(8,128)S(1)}, f32[512,128]{1,0:T(8,128)S(1)}, u32[]{:S(2)}, u32[]{:S(2)}) collective-permute-start(f32[512,128]{1,0:T(8,128)S(1)} %get-tuple-element.127.refs_0_.refs_2_.refs_6_), channel_id=1, source_target_pairs={{1,2},{2,1},{3,4},{4,3},{5,6},{6,5},{7,8},{8,7},{9,10},{10,9},{11,... | collective-permute-start | bytes 786440 | tf_op jit(solution)/shard_map/ppermute | solution.py:349
  57.9 14.1 %collective-permute-start.11 = (f32[512,128]{1,0:T(8,128)S(1)}, f32[512,128]{1,0:T(8,128)S(1)}, u32[]{:S(2)}, u32[]{:S(2)}) collective-permute-start(f32[512,128]{1,0:T(8,128)S(1)} %get-tuple-element.128.refs_1_.refs_3_.refs_7_), channel_id=1, source_target_pairs={{0,1},{1,0},{2,3},{3,2},{4,5},{5,4},{6,7},{7,6},{8,9},{9,8},{10,11... | collective-permute-start | bytes 786440 | tf_op jit(solution)/shard_map/ppermute | solution.py:349
  87.5 3.8 %collective-permute-start.12 = (f32[2,512,128]{2,1,0:T(8,128)S(1)}, f32[2,512,128]{2,1,0:T(8,128)S(1)}, u32[]{:S(2)}, u32[]{:S(2)}) collective-permute-start(f32[2,512,128]{2,1,0:T(8,128)S(1)} %get-tuple-element.157), channel_id=1, source_target_pairs={{0,16},{16,0},{1,17},{17,1},{2,18},{18,2},{3,19},{19,3},{4,20},{20... | collective-permute-start | bytes 1572872 | tf_op jit(solution)/shard_map/ppermute | solution.py:459

commit v4 on v1

v4 whole, which is shorter than its diff:
```python
import jax
import jax.numpy as jnp
from jax import lax
from jax.experimental import pallas as pl
from jax.experimental.pallas import tpu as pltpu
from jax.sharding import PartitionSpec as P

WELL_TERM = 4.0
CHUNK = 64
COST = 1024
HEADS_STEP = 0
VMEM = pltpu.VMEM
SMEM = pltpu.SMEM


def row_before(ref, start, count):
    if start == 0:
        return pltpu.roll(ref[0:count], 1, 0)
    return ref[start - 1 : start + count - 1]


def row_after(ref, start, count):
    if start + count == ref.shape[0]:
        return pltpu.roll(ref[start : start + count], count - 1, 0)
    return ref[start + 1 : start + count + 1]


def lane_before(v):
    return pltpu.roll(v, 1, 1)


def lane_after(v):
    return pltpu.roll(v, v.shape[1] - 1, 1)


def chunks_of(rows):
    count = min(CHUNK, rows)
    return [(start, count) for start in range(0, rows, count)]


def fold(v):
    return jnp.sum(v.reshape(v.shape[0] // 8, 8, v.shape[1]), axis=0)


def call(kernel, ins, outs, scalars=0, space=VMEM, stored=0, scratch=(), cost=COST):
    out_shape = [VMEM(o, jnp.float32) if isinstance(o, tuple) else o for o in outs]
    if space is not None:
        ins = [
            x if x.size == 1 or (i < scalars and space is VMEM) else pltpu.with_memory_space_constraint(x, space) for i, x in enumerate(ins)
        ]
    return pl.pallas_call(
        kernel,
        out_shape=out_shape,
        in_specs=[
            pl.BlockSpec(memory_space=SMEM if i < scalars else VMEM if i < len(ins) - stored else pl.ANY) for i in range(len(ins))
        ],
        out_specs=[pl.BlockSpec(memory_space=VMEM)] * len(outs),
        scratch_shapes=scratch,
        cost_estimate=pl.CostEstimate(flops=COST, bytes_accessed=cost, transcendentals=0),
        compiler_params=pltpu.CompilerParams(vmem_limit_bytes=16 * 1024 * 1024),
    )(*ins)


def plane_at(i, width, flip):
    return i + flip * (width - 1 - 2 * i)


SIDES = 4


def around(ref, part, start, count):
    here = ref[part]
    return row_before(ref, start, count), row_after(ref, start, count), lane_before(here), lane_after(here)


def native_kernel(width, place, pump_ref, obs_ref, data_ref, storage_ref, mask_ref, head_ref, later_ref, far_ref, near_ref):
    rows, depth = storage_ref.shape[1:]
    lane = lax.broadcasted_iota(jnp.int32, (min(CHUNK, rows), depth), 1)
    row = lax.broadcasted_iota(jnp.int32, (min(CHUNK, rows), depth), 0)
    outs = [(far_ref, 0)] + [(near_ref, 2 * i) for i in range(width - 1)]
    places = [plane_at(i, width, place[7]) for i in range(width)]
    for at, (out_ref, k) in zip(places, outs):
        for r, n in chunks_of(rows):
            part = slice(r, r + n)
            active = mask_ref[at, part] > 0
            store = storage_ref[at, part]
            well = jnp.where(row * depth + lane + (at * rows + r) * depth == pump_ref[0] - place[0], WELL_TERM, 0.0)
            out_ref[k, part] = jnp.where(active, store + well, 0.0)
            out_ref[k + 1, part] = jnp.where(active, store * later_ref[0, at, part], 0.0)
    lanes = lax.broadcasted_iota(jnp.int32, (1, depth), 1)

    def observe(o, _):
        cell = obs_ref[o] - place[0]

        @pl.when((cell >= 0) & (cell < width * rows * depth))
        def _():
            for at, (out_ref, k) in zip(places, outs):
                local = cell - at * rows * depth

                @pl.when((local >= 0) & (local < rows * depth))
                def _():
                    line = pl.ds(local // depth, 1)
                    here = (lanes == local % depth) & (mask_ref[at, line] > 0)
                    out_ref[k + 1, line] += jnp.where(here, head_ref[0, at, line] - data_ref[o], 0.0)

        return 0

    lax.fori_loop(0, obs_ref.shape[0], observe, 0)


def pick(place, kept, moved):
    return jnp.where(place[4], moved, kept)


def cond_kernel(width, place, log_ref, log_moved, log_halo, *outs):
    cond, halo = outs[:width], outs[width]
    for r, n in chunks_of(halo.shape[0]):
        halo[r : r + n] = jnp.exp(log_halo[r : r + n])
    for i in range(width):
        at = plane_at(i, width, place[3])
        for r, n in chunks_of(cond[0].shape[0]):
            part = slice(r, r + n)
            cond[i][part] = jnp.exp(pick(place, log_ref[at, part], log_moved[at, part]))


def face_kernel(width, *refs):
    cond, total, refs = refs[:width], refs[width : 2 * width], refs[2 * width :]
    faces, fx = [refs[k * width : (k + 1) * width] for k in range(SIDES)], refs[SIDES * width :]
    rows, depth = cond[0].shape
    lane = lax.broadcasted_iota(jnp.int32, (min(CHUNK, rows), depth), 1)
    row = lax.broadcasted_iota(jnp.int32, (min(CHUNK, rows), depth), 0)
    for i in range(width):
        for r, n in chunks_of(rows):
            part = slice(r, r + n)
            c = cond[i][part]
            inside = (
                None if r else row > 0,
                None if r + n < rows else row < n - 1,
                lane > 0,
                lane < depth - 1,
            )
            amount = fx[i - 1][part] if i > 0 else jnp.zeros_like(c)
            for k, other in enumerate(around(cond[i], part, r, n)):
                face = 2.0 * c * other / (c + other)
                if inside[k] is not None:
                    face = jnp.where(inside[k], face, 0.0)
                faces[k][i][part] = face
                amount = amount + face
            if i < width - 1:
                other = cond[i + 1][part]
                face = 2.0 * c * other / (c + other)
                fx[i][part] = face
                amount = amount + face
            total[i][part] = amount


def start_kernel(count, ends, place, pack_ref, pack_moved, *refs):
    halo, cond, total = refs[: len(ends)], refs[len(ends) :][:count], refs[len(ends) + count :][:count]
    refs = refs[len(ends) + 2 * count :]
    field, inverse, own = (refs[k * count : (k + 1) * count] for k in range(3))
    outer, refs = refs[3 * count :][: len(ends)], refs[3 * count + len(ends) :]
    sums_ref, least_ref = refs[:2]
    rows, depth = cond[0].shape
    sums = jnp.zeros((8, depth), jnp.float32)
    least = jnp.ones((8, depth), jnp.float32)
    for r, n in chunks_of(rows):
        part = slice(r, r + n)
        for i in range(count):
            c, amount = cond[i][part], total[i][part]
            for k, (end, side) in enumerate(ends):
                if i == end:
                    other = halo[k][part]
                    face = jnp.where(place[1 + side], 2.0 * c * other / (c + other), 0.0)
                    outer[k][part] = face
                    amount = amount + face
            own_here = pick(place, pack_ref[2 * i, part], pack_moved[2 * i, part])
            right = pick(place, pack_ref[2 * i + 1, part], pack_moved[2 * i + 1, part])
            active = own_here > 0.0
            inv = 1.0 / (own_here + amount)
            least_here = jnp.where(active, own_here * inv, 1.0)
            inv = jnp.where(active, inv, 0.0)
            v = right * inv
            own[i][part] = own_here
            field[i][part] = v
            inverse[i][part] = inv
            sums = sums + fold(v * right)
            least = jnp.minimum(least, jnp.min(least_here.reshape(n // 8, 8, depth), axis=0))
    sums_ref[...] = sums
    least_ref[...] = least


def inner_kernel(width, *refs):
    v, own, *faces = (refs[k * width : (k + 1) * width] for k in range(2 + SIDES))
    fx, image = refs[(2 + SIDES) * width : -width], refs[-width:]
    for i in range(width):
        for r, n in chunks_of(v[0].shape[0]):
            part = slice(r, r + n)
            here = v[i][part]
            result = own[i][part] * here
            for k, other in enumerate(around(v[i], part, r, n)):
                result = result + faces[k][i][part] * (here - other)
            if i > 0:
                result = result + fx[i - 1][part] * (here - v[i - 1][part])
            if i < width - 1:
                result = result + fx[i][part] * (here - v[i + 1][part])
            image[i][part] = result


def flat(ref):
    return ref.at[0] if len(ref.shape) == 3 else ref


def outer_image(width, refs, part):
    inner, v, outer, halo = refs
    result = []
    for i in range(width):
        w, here = inner[i][part], v[i][part]
        for k, end in enumerate((0, width - 1)):
            if i == end:
                w = w + outer[k][part] * (here - flat(halo[k])[part])
        result.append((here, w))
    return result


def finish_kernel(width, *refs):
    inner, v, inverse = (refs[k * width : (k + 1) * width] for k in range(3))
    outer, halo = refs[3 * width : 3 * width + 2], refs[3 * width + 2 : 3 * width + 4]
    following = refs[3 * width + 4 : 4 * width + 4]
    odd_ref, even_ref = refs[4 * width + 4 :]
    rows, depth = v[0].shape
    odd = jnp.zeros((8, depth), jnp.float32)
    even = jnp.zeros((8, depth), jnp.float32)
    for r, n in chunks_of(rows):
        part = slice(r, r + n)
        for i, (here, w) in enumerate(outer_image(width, (inner, v, outer, halo), part)):
            new = w * inverse[i][part]
            following[i][part] = new
            odd = odd + fold(here * w)
            even = even + fold(new * w)
    odd_ref[...] = odd
    even_ref[...] = even


def head_kernel(width, place, head_ref, head_moved, *head):
    for i in range(width):
        at = plane_at(i, width, place[3])
        for r, n in chunks_of(head[0].shape[0]):
            part = slice(r, r + n)
            head[i][part] = pick(place, head_ref[0, at, part], head_moved[0, at, part])


def gradient_kernel(width, *refs):
    cond, head, *faces = (refs[k * width : (k + 1) * width] for k in range(2 + SIDES))
    refs = refs[(2 + SIDES) * width :]
    fx, refs = refs[: width - 1], refs[width - 1 :]
    outer, heads_halo, refs = refs[:2], refs[2:4], refs[4:]
    v, refs = [refs[k * width : (k + 1) * width] for k in range(3)], refs[3 * width :]
    halos, refs = [refs[:2], refs[2:4]], refs[4:]
    terms, weight = [refs[k * width : (k + 1) * width] for k in range(3)], refs[3 * width :]
    for i in range(width):
        for r, n in chunks_of(cond[0].shape[0]):
            part = slice(r, r + n)
            h = head[i][part]
            here = [f[i][part] for f in v]
            sums = [jnp.zeros_like(h)] * 3
            others = [around(f[i], part, r, n) for f in v]
            for k, head_n in enumerate(around(head[i], part, r, n)):
                face = faces[k][i][part]
                scale = face * face * (h - head_n)
                sums = [s + scale * (a - b[k]) for s, a, b in zip(sums, here, others)]
            for other, face_ref in ((i - 1, fx[i - 1] if i > 0 else None), (i + 1, fx[i] if i < width - 1 else None)):
                if face_ref is not None:
                    face = face_ref[part]
                    scale = face * face * (h - head[other][part])
                    sums = [s + scale * (a - f[other][part]) for s, a, f in zip(sums, here, v)]
            inverse = 0.5 / cond[i][part]
            for k, end in enumerate((0, width - 1)):
                if i == end:
                    face = outer[k][part]
                    scale = face * face * (h - heads_halo[k][part])
                    weight[k][part] = scale * inverse
                    for j in range(2):
                        sums[j] = sums[j] + scale * (here[j] - flat(halos[j][k])[part])
            for t, s in zip(terms, sums):
                t[i][part] = s * inverse


def last_kernel(width, *refs):
    inner, v, terms = (refs[k * width : (k + 1) * width] for k in range(3))
    outer, halo, weight = (refs[3 * width + 2 * k : 3 * width + 2 * k + 2] for k in range(3))
    refs = refs[3 * width + 6 :]
    first, earlier, leasts, out_ref, whole_terms = refs[:2], refs[2:6], refs[6:8], refs[8], refs[9:]
    rows, depth = v[0].shape
    odd = jnp.zeros((8, depth), jnp.float32)
    for r, n in chunks_of(rows):
        part = slice(r, r + n)
        for i, (here, w) in enumerate(outer_image(width, (inner, v, outer, halo), part)):
            odd = odd + fold(here * w)
            term = terms[i][part]
            for k, end in enumerate((0, width - 1)):
                if i == end:
                    term = term + weight[k][part] * (here - flat(halo[k])[part])
            whole_terms[i][part] = term
    every = (first[0][...] + first[1][...], *(e[...] for e in earlier), odd)
    sums = [jnp.sum(x, axis=0, keepdims=True) for x in every]
    least = jnp.min(jnp.minimum(leasts[0][...], leasts[1][...]), axis=0, keepdims=True)
    told = jnp.concatenate([*sums, least, least], axis=0)
    for k in range(out_ref.shape[0]):
        out_ref[k] = told


def combine(moments, least):
    m0, m1, m2, m3, m4, m5 = moments
    most = 2.0 - least
    alpha_low, alpha_high = 1.0 / most, 1.0 / least
    beta_high = (1.0 - least) * (1.0 - least) / (least * most)

    def alpha_of(rz, curve):
        return jnp.clip(jnp.where(curve > 0.0, rz / curve, alpha_low), alpha_low, alpha_high)

    def beta_of(rz_new, rz):
        return jnp.clip(jnp.where(rz > 0.0, rz_new / rz, 0.0), 0.0, beta_high)

    a0 = alpha_of(m0, m1)
    rz1 = m0 - 2.0 * a0 * m1 + a0 * a0 * m2
    b0 = beta_of(rz1, m0)
    u = 1.0 + b0
    curve1 = u * u * m1 - 2.0 * a0 * u * m2 + a0 * a0 * m3
    a1 = alpha_of(rz1, curve1)
    c1 = -a0 - a1 * u
    c2 = a0 * a1
    rz2 = m0 + 2.0 * c1 * m1 + (2.0 * c2 + c1 * c1) * m2 + 2.0 * c1 * c2 * m3 + c2 * c2 * m4
    b1 = beta_of(rz2, rz1)
    q0 = 1.0 + b1 * u
    q1 = c1 - b1 * a0
    q2 = c2
    curve2 = q0 * q0 * m1 + 2.0 * q0 * q1 * m2 + (2.0 * q0 * q2 + q1 * q1) * m3 + 2.0 * q1 * q2 * m4 + q2 * q2 * m5
    a2 = alpha_of(rz2, curve2)
    return a0 + a1 * u + a2 * q0, a2 * q1 - a1 * a0, a2 * q2


def result_kernel(width, groups, place, told_ref, *refs):
    stored, (gradient_ref, adjoint_ref), (fetched, arrived) = refs[: 6 * width], refs[6 * width : -2], refs[-2:]
    fetches = [pltpu.make_async_copy(x, fetched.at[k], arrived.at[k]) for k, x in enumerate(stored)]
    for fetch in fetches:
        fetch.start()
    terms, fields = (
        [[fetched.at[k * width + i] for i in range(width)] for k in range(first, first + 3)] for first in (0, 3)
    )
    found = []
    for g in range(groups):
        sums = least = told_ref[g]
        for k in range(g + groups, told_ref.shape[0], groups):
            sums = sums + told_ref[k]
            least = jnp.minimum(least, told_ref[k])
        sums = jnp.sum(sums, axis=1, keepdims=True)
        least = jnp.min(least, axis=1, keepdims=True)
        found.append(combine([sums[i : i + 1] for i in range(6)], least[6:7]))
    coefs = [jnp.where(place[5] > 0, b, a) for a, b in zip(found[0], found[-1])]
    rows, depth = fetched.shape[1:]
    wide = [jnp.broadcast_to(c, (8, depth)) for c in coefs]
    for fetch in fetches:
        fetch.wait()
    for r, n in chunks_of(rows):
        part = slice(r, r + n)
        scale = [jnp.concatenate([c] * (n // 8), axis=0) for c in wide]
        for i in range(width):
            at = plane_at(i, width, place[3])
            gradient_ref[at, part] = -sum(c * t[i][part] for c, t in zip(scale, terms))
            adjoint_ref[0, at, part] = sum(c * f[i][part] for c, f in zip(scale, fields))


def adjoint_kernel(place, kept, moved, out_ref):
    for i in range(out_ref.shape[1]):
        for r, n in chunks_of(out_ref.shape[2]):
            part = slice(r, r + n)
            out_ref[0, i, part] = pick(place, kept[0, i, part], moved[0, i, part])


def add_kernel(place, own_ref, beside_ref, other_ref, handed_ref, out_ref):
    for i in range(out_ref.shape[0]):
        for r, n in chunks_of(out_ref.shape[1]):
            part = slice(r, r + n)
            here = pick(place, own_ref[i, part], beside_ref[i, part])
            out_ref[i, part] = here + pick(place, handed_ref[i, part], other_ref[i, part])


BOTH = ("test", "slab")


def on_device(
    log_conductivity, storage, active_mask, heads, adjoint_next, pump_cells, obs_cells, obs_data
):
    width, rows, depth = log_conductivity.shape
    plane, stack = (rows, depth), (width, rows, depth)
    slabs = lax.axis_size("slab")
    cells_here = width * rows * depth
    turned = lax.axis_size("test") == 2 and slabs % 2 == 0
    if turned:
        pairs = [(slabs + 2 * j, 2 * j + 1) for j in range(slabs // 2)]
        far_pairs = [(slabs + i, i + 2) for i in range(slabs - 2)]
        near_axis, near = "test", [(0, 1), (1, 0)]
        far_axis, groups = BOTH, 2
        at = lambda t, i: t * slabs + i
        first_far = [
            way
            for j in range(0, slabs - 2, 2)
            for way in (
                (at(0, j + 2), at(1, j)),
                (at(1, j + 2), at(1, j + 1)),
                (at(0, j + 1), at(0, j + 2)),
                (at(1, j + 1), at(0, j + 3)),
            )
        ]
    else:
        pairs = []
        far_pairs = [(i, i + 1) for i in range(1, slabs - 1, 2)]
        near_axis, near = "slab", [(i, i ^ 1) for i in range(slabs) if i ^ 1 < slabs]
        far_axis, groups = "slab", 1
    both_ways = lambda links: [way for a, b in links for way in ((a, b), (b, a))]
    if not turned:
        first_far = both_ways(far_pairs)

    def position():
        place, test = lax.axis_index("slab"), lax.axis_index("test")
        parity = lax.rem(place, 2)
        flip, mine = (test, place - parity + test) if turned else (parity, place)
        far_partner, near_partner = mine - 1 + 2 * flip, mine + 1 - 2 * flip
        return [
            place * cells_here,
            (far_partner >= 0) & (far_partner < slabs),
            near_partner < slabs,
            flip,
            mine != place,
            parity if turned else 0,
            test if turned else 0,
            parity,
        ]

    def move(x):
        return lax.ppermute(x, BOTH, both_ways(pairs)) if turned else x

    def swap_near(x):
        return lax.ppermute(x, near_axis, near)

    def swap_far(x):
        return lax.ppermute(x, far_axis, both_ways(far_pairs))

    def after(x, *others):
        return lax.optimization_barrier((x, others))[0]

    hbm = lambda *shape: pltpu.HBM(shape, jnp.float32)
    planes = [plane] * width

    far_at = plane_at(0, width, position()[7])
    far_plane = lambda x: lax.dynamic_slice(x, (far_at, 0, 0), (1, rows, depth))[0]
    log_moved = move(log_conductivity)
    far_pack, near_pack = call(
        lambda *refs: native_kernel(width, position(), *refs),
        [pump_cells, obs_cells, obs_data[0], storage, active_mask, heads, adjoint_next],
        [(2, rows, depth), (2 * (width - 1), rows, depth)],
        scalars=3,
        space=pltpu.HBM,
    )
    far_moved = move(far_pack)
    log_halo = lax.ppermute(after(far_plane(log_conductivity), far_pack), far_axis, first_far)
    head_far = lax.ppermute(after(far_plane(heads[0]), far_pack), far_axis, first_far)
    *cond, cond_far = call(
        lambda *refs: cond_kernel(width, position(), *refs),
        [log_conductivity, log_moved, log_halo],
        [*planes, plane],
        space=None,
    )
    cond_halo = [cond_far, swap_near(cond[-1])]
    near_moved = move(after(near_pack, *cond))
    near_moved, head_far = lax.optimization_barrier((near_moved, head_far))
    total, faces = (lambda x: (x[:width], x[width:]))(
        call(lambda *refs: face_kernel(width, *refs), cond, planes * (1 + SIDES) + [plane] * (width - 1))
    )
    def start(first, count, ends, pack, pack_moved):
        started = call(
            lambda *refs: start_kernel(count, ends, position(), *refs),
            [pack, pack_moved, *(cond_halo[side] for _, side in ends), *cond[first:][:count], *total[first:][:count]],
            [plane] * (3 * count + len(ends)) + [(8, depth)] * 2,
        )
        return [*(started[k * count : (k + 1) * count] for k in range(3)), started[3 * count :]]

    field, inverse, own, (outer_far, sum_far, least_far) = start(0, 1, [(0, 0)], far_pack, far_moved)
    v_halo = swap_far(field[0])
    field_near, inverse_near, own_near, (outer_near, sum_near, least_near) = start(
        1, width - 1, [(width - 2, 1)], near_pack, near_moved
    )
    field, inverse, own = [*field, *field_near], [*inverse, *inverse_near], [*own, *own_near]
    outer = [outer_far, outer_near]

    sums, fields, halos = [sum_far, sum_near], [], []
    for step in range(3):
        halo = [swap_far(field[0]) if step else v_halo, swap_near(field[-1])]
        fields += field
        image = call(lambda *refs: inner_kernel(width, *refs), [*field, *own, *faces], planes)
        if step == HEADS_STEP:
            heads_moved = move(after(heads, *image))
        if step == 2:
            head = call(lambda *refs: head_kernel(width, position(), *refs), [heads, heads_moved], planes, space=None)
            head_near = swap_near(head[-1])
        if step < 2:
            halos += halo
            made = call(
                lambda *refs: finish_kernel(width, *refs),
                [*image, *field, *inverse, *outer, *halo],
                planes + [(8, depth)] * 2,
            )
            field, (odd, even) = made[:width], made[width:]
            sums += [odd, even]
    *terms, weight_0, weight_1 = call(
        lambda *refs: gradient_kernel(width, *refs),
        [*cond, *head, *faces, *outer, head_far, head_near, *fields, *halos],
        [hbm(*plane)] * (2 * width) + planes + [plane] * 2,
    )
    told, *last_terms = call(
        lambda *refs: last_kernel(width, *refs),
        [*image, *field, *terms[2 * width :], *outer, *halo, weight_0, weight_1, *sums, least_far, least_near],
        [hbm(groups * slabs, 8, depth)] + [hbm(*plane)] * width,
        cost=1 << 24,
    )
    told = lax.all_to_all(told, BOTH if turned else "slab", 0, 0, tiled=True)
    gradient, adjoint = call(
        lambda *refs: result_kernel(width, groups, position(), *refs),
        [told, *(pltpu.with_memory_space_constraint(x, pltpu.HBM) for x in (*terms[: 2 * width], *last_terms)), *fields],
        [stack, (1, *stack) if turned else jax.ShapeDtypeStruct((1, *stack), jnp.float32)],
        space=None,
        stored=6 * width,
        scratch=[VMEM((6 * width, rows, depth), jnp.float32), pltpu.SemaphoreType.DMA((6 * width,))],
    )
    if turned:
        other = move(gradient)
        beside = lax.ppermute(gradient, "test", near)
        handed = lax.ppermute(other, "test", near)
        (gradient,) = call(
            lambda *refs: add_kernel(position(), *refs),
            [gradient, beside, other, handed],
            [jax.ShapeDtypeStruct(stack, jnp.float32)],
        )
        (adjoint,) = call(
            lambda *refs: adjoint_kernel(position(), *refs),
            [adjoint, move(adjoint)],
            [jax.ShapeDtypeStruct((1, *stack), jnp.float32)],
        )
    else:
        gradient = lax.psum(gradient, "test")
    return adjoint, gradient


def solution(mesh):
    return jax.shard_map(
        on_device,
        mesh=mesh,
        in_specs=(
            P("slab", None, None),
            P("slab", None, None),
            P("slab", None, None),
            P("test", "slab", None, None),
            P("test", "slab", None, None),
            P("test"),
            P(),
            P("test", None),
        ),
        out_specs=(P("test", "slab", None, None), P("slab", None, None)),
        check_vma=False,
    )
```

time: 106 us -> 91.2 us (0.86)
  between operations: 17 us -> 1.57 us
  blocking collectives: 0 us -> 14.1 us
  other arithmetic: 12.9 us -> 0 us
  Pallas kernels: 0 us -> 12.1 us
  local copies, waits for them, and re-layouts: 9.66 us -> 0.06 us
  starting transfers between devices: 45.4 us -> 41.5 us
  waiting for transfers between devices: 20.2 us -> 21.4 us
    all_to_all x0 -> x1, blocking collectives: none -> 14.1 us  [on_device(): told = lax.all_to_all(told, BOTH if turned else 'slab', 0, 0, tiled=True)]
    pallas_call x0 -> x16, Pallas kernels: none -> 12.1 us  [call(): pl.pallas_call(kernel, out_shape=out_shape, in_specs=[pl.BlockSpec(memory...]
    all_to_all x1 -> x0, starting transfers between devices: 9.41 us -> none  [on_device(): lax.all_to_all(jnp.broadcast_to(payload[None], (slabs, *payload.shape)),...]
    ppermute x11 -> x18, starting transfers between devices: 36 us -> 41.5 us  [the longest x6 22.6 us: move(): return lax.ppermute(x, BOTH, both_ways(pairs)) if turned else x]
    unnamed x50 -> x4, local copies, waits for them, and re-layouts: 4.94 us -> 0.01 us
    another operation x2 -> x0, other arithmetic: 4.33 us -> none  [on_device(): terms = -jnp.stack(terms)]
    div x6 -> x0, other arithmetic: 2.66 us -> none  [the longest x2 1.66 us: on_device(): field = [rhs[i] / diag[i] for i in range(width)]]
    squeeze x2, local copies, waits for them, and re-layouts: 2.56 us -> 0.05 us  [on_device(): lax.dynamic_slice(x, (far_at, 0, 0), (1, rows, depth))[0]]
  transfers between devices with their start and end apart: 12 -> 18, of which waited for: 8 -> 8; matrix products, arithmetic and copies ran while one was open for 10% -> 0% of each run, Pallas kernels for 0% -> 9%
where the time goes in v4:
time: 91.2 us; the launch traced here: 90.7 us
  starting transfers between devices  41.5 us (46%)
  waiting for transfers between devices  21.4 us (23%)
  blocking collectives  14.1 us (15%)
  Pallas kernels  12.1 us (13%)
  between operations  1.57 us (2%)
    ppermute x6, starting transfers between devices, move(): return lax.ppermute(x, BOTH, both_ways(pairs)) if turned else x  22.6 us
    ppermute x3, starting transfers between devices, swap_far(): return lax.ppermute(x, far_axis, both_ways(far_pairs))  15.5 us
    all_to_all x1, blocking collectives, on_device(): told = lax.all_to_all(told, BOTH if turned else 'slab', 0, 0, tiled=True)  14.1 us
    pallas_call x16, Pallas kernels, call(): pl.pallas_call(kernel, out_shape=out_shape, in_specs=[pl.BlockSpec(memory...  12.1 us
    ppermute x6, waiting for transfers between devices, move(): return lax.ppermute(x, BOTH, both_ways(pairs)) if turned else x  11 us
    ppermute x3, waiting for transfers between devices, swap_far(): return lax.ppermute(x, far_axis, both_ways(far_pairs))  6.71 us
    ppermute x1, waiting for transfers between devices, on_device(): lax.ppermute(after(far_plane(log_conductivity), far_pack), far_axis, firs...  3.6 us
  transfers between devices with their start and end apart: 18, of which 8 were waited for; matrix products, arithmetic and copies ran while one was open for 0% of the time, Pallas kernels for 9%

profile of v4, /device:TPU:1, one launch (start us, length us, event | category | flops | bytes accessed | tf_op | source)
XLA Modules:
  0.0 90.7 jit_solution(5746891489730454635)
XLA Ops:
  0.6 4.5 %collective-permute-start.1 = (f32[2,512,128]{2,1,0:T(8,128)}, f32[2,512,128]{2,1,0:T(8,128)S(1)}, u32[]{:S(2)}, u32[]{:S(2)}) collective-permute-start(f32[2,512,128]{2,1,0:T(8,128)} %refs_0_.3), channel_id=1, source_target_pairs={{16,1},{1,16},{18,3},{3,18},{20,5},{5,20},{22,7},{7,22},{24,9},{9,... | collective-permute-start | bytes 1572872 | tf_op jit(solution)/shard_map/ppermute | solution.py:441
  5.8 2.8 %shard_map.95 = (f32[2,512,128]{2,1,0:T(8,128)S(1)}, f32[2,512,128]{2,1,0:T(8,128)S(1)}) custom-call(s32[1]{0:T(128)S(6)} %copy.10.refs_0_, s32[64]{0:T(128)} %refs_1_.1, f32[64]{0:T(128)} %bitcast.5, f32[2,512,128]{2,1,0:T(8,128)} %refs_3_.1, s32[2,512,128]{2,1,0:T(8,128)} %refs_4_.1, f32[1,2,512,128]{3,2,1,0:T(8,128)} %refs_0_.4, f32[1,2,512,128]{3,2,1,0:T(8,128)} %refs_6_.1), custom_call_target="tpu_custom_call" | custom-call | flops 1024 | bytes 1024 | tf_op jit(solution)/shard_map/pallas_call | solution.py:51
  8.6 1.4 %collective-permute-start.2 = (f32[512,128]{1,0:T(8,128)S(1)}, f32[512,128]{1,0:T(8,128)S(1)}, u32[]{:S(2)}, u32[]{:S(2)}) collective-permute-start(f32[512,128]{1,0:T(8,128)S(1)} %dynamic-slice_bitcast_fusion.1), channel_id=1, source_target_pairs={{2,16},{18,17},{1,2},{17,3},{4,18},{20,19},{3,4},{19,5},{6,20},{22... | collective-permute-start | bytes 786440 | tf_op jit(solution)/shard_map/ppermute | solution.py:466
  10.1 2.8 %collective-permute-start = (f32[2,512,128]{2,1,0:T(8,128)S(1)}, f32[2,512,128]{2,1,0:T(8,128)S(1)}, u32[]{:S(2)}, u32[]{:S(2)}) collective-permute-start(f32[2,512,128]{2,1,0:T(8,128)S(1)} %get-tuple-element.65.refs_0_), channel_id=1, source_target_pairs={{16,1},{1,16},{18,3},{3,18},{20,5},{5,20},{22,7},{7,22},{24,9},{9,... | collective-permute-start | bytes 1572872 | tf_op jit(solution)/shard_map/ppermute | solution.py:441
  12.9 3.6 %collective-permute-done.2.refs_2_ = f32[512,128]{1,0:T(8,128)S(1)} collective-permute-done((f32[512,128]{1,0:T(8,128)S(1)}, f32[512,128]{1,0:T(8,128)S(1)}, u32[]{:S(2)}, u32[]{:S(2)}) %collective-permute-start.2) | collective-permute-done | bytes 262176 | tf_op jit(solution)/shard_map/ppermute | solution.py:466
  16.6 1.9 %collective-permute-start.3 = (f32[2,512,128]{2,1,0:T(8,128)S(1)}, f32[2,512,128]{2,1,0:T(8,128)S(1)}, u32[]{:S(2)}, u32[]{:S(2)}) collective-permute-start(f32[2,512,128]{2,1,0:T(8,128)S(1)} %get-tuple-element.73.refs_0_), channel_id=1, source_target_pairs={{16,1},{1,16},{18,3},{3,18},{20,5},{5,20},{22,7},{7,22},{24,9},{9,... | collective-permute-start | bytes 1572872 | tf_op jit(solution)/shard_map/ppermute | solution.py:441
  18.6 1.3 %collective-permute-start.4 = (f32[512,128]{1,0:T(8,128)S(1)}, f32[512,128]{1,0:T(8,128)S(1)}, u32[]{:S(2)}, u32[]{:S(2)}) collective-permute-start(f32[512,128]{1,0:T(8,128)S(1)} %dynamic-slice_bitcast_fusion), channel_id=1, source_target_pairs={{2,16},{18,17},{1,2},{17,3},{4,18},{20,19},{3,4},{19,5},{6,20},{22... | collective-permute-start | bytes 786440 | tf_op jit(solution)/shard_map/ppermute | solution.py:467
  19.9 0.5 shard_map.97
  20.4 0.2 collective-permute-done.refs_1_
  20.8 6.7 %collective-permute-start.6 = (f32[512,128]{1,0:T(8,128)S(1)}, f32[512,128]{1,0:T(8,128)S(1)}, u32[]{:S(2)}, u32[]{:S(2)}) collective-permute-start(f32[512,128]{1,0:T(8,128)S(1)} %get-tuple-element.71.refs_0_.refs_2_.refs_17_.refs_7_), channel_id=1, source_target_pairs={{16,2},{2,16},{17,3},{3,17},{18,4},{4,18},{19,5},{5,19},{20,6},{6,... | collective-permute-start | bytes 786440 | tf_op jit(solution)/shard_map/ppermute | solution.py:447
  27.9 0.4 shard_map.100
  28.2 7.9 %collective-permute-start.10 = (f32[1,2,512,128]{3,2,1,0:T(8,128)S(1)}, f32[1,2,512,128]{3,2,1,0:T(8,128)S(1)}, u32[]{:S(2)}, u32[]{:S(2)}) collective-permute-start(f32[1,2,512,128]{3,2,1,0:T(8,128)S(1)} %copy-done), channel_id=1, source_target_pairs={{16,1},{1,16},{18,3},{3,18},{20,5},{5,20},{22,7},{7,22},{24,9},{9,... | collective-permute-start | bytes 1572872 | tf_op jit(solution)/shard_map/ppermute | solution.py:441
  36.1 1.5 %collective-permute-done.6.refs_8_.refs_23_ = f32[512,128]{1,0:T(8,128)S(1)} collective-permute-done((f32[512,128]{1,0:T(8,128)S(1)}, f32[512,128]{1,0:T(8,128)S(1)}, u32[]{:S(2)}, u32[]{:S(2)}) %collective-permute-start.6) | collective-permute-done | bytes 262176 | tf_op jit(solution)/shard_map/ppermute | solution.py:447
  37.8 4.4 %collective-permute-start.8 = (f32[512,128]{1,0:T(8,128)S(1)}, f32[512,128]{1,0:T(8,128)S(1)}, u32[]{:S(2)}, u32[]{:S(2)}) collective-permute-start(f32[512,128]{1,0:T(8,128)S(1)} %get-tuple-element.95.refs_0_.refs_2_.refs_19_.refs_9_), channel_id=1, source_target_pairs={{16,2},{2,16},{17,3},{3,17},{18,4},{4,18},{19,5},{5,19},{20,6},{6,... | collective-permute-start | bytes 786440 | tf_op jit(solution)/shard_map/ppermute | solution.py:447
  42.2 0.4 shard_map.102
  42.6 0.4 collective-permute-done.10.refs_1_
  43.0 0.2 collective-permute-start.11
  43.2 3.5 %collective-permute-done.8.refs_8_.refs_25_ = f32[512,128]{1,0:T(8,128)S(1)} collective-permute-done((f32[512,128]{1,0:T(8,128)S(1)}, f32[512,128]{1,0:T(8,128)S(1)}, u32[]{:S(2)}, u32[]{:S(2)}) %collective-permute-start.8) | collective-permute-done | bytes 262176 | tf_op jit(solution)/shard_map/ppermute | solution.py:447
  46.8 0.2 shard_map.103
  46.9 4.4 %collective-permute-start.12 = (f32[512,128]{1,0:T(8,128)S(1)}, f32[512,128]{1,0:T(8,128)S(1)}, u32[]{:S(2)}, u32[]{:S(2)}) collective-permute-start(f32[512,128]{1,0:T(8,128)S(1)} %get-tuple-element.99.refs_0_.refs_21_.refs_2_.refs_11_), channel_id=1, source_target_pairs={{16,2},{2,16},{17,3},{3,17},{18,4},{4,18},{19,5},{5,19},{20,6},{6,... | collective-permute-start | bytes 786440 | tf_op jit(solution)/shard_map/ppermute | solution.py:447
  51.4 0.4 shard_map.104
  51.8 2.5 %shard_map.106 = (f32[512,128]{1,0:T(8,128)}, f32[512,128]{1,0:T(8,128)}, f32[512,128]{1,0:T(8,128)}, f32[512,128]{1,0:T(8,128)}, f32[512,128]{1,0:T(8,128)S(1)}...) custom-call(f32[512,128]{1,0:T(8,128)S(1)} %get-tuple-element.68.refs_0_.refs_3_, ...), custom_call_target="tpu_custom_call" | custom-call | flops 1024 | bytes 1024 | tf_op jit(solution)/shard_map/pallas_call | solution.py:51
  54.3 1.7 %collective-permute-done.12.refs_8_ = f32[512,128]{1,0:T(8,128)S(1)} collective-permute-done((f32[512,128]{1,0:T(8,128)S(1)}, f32[512,128]{1,0:T(8,128)S(1)}, u32[]{:S(2)}, u32[]{:S(2)}) %collective-permute-start.12) | collective-permute-done | bytes 262176 | tf_op jit(solution)/shard_map/ppermute | solution.py:447
  56.0 1.0 %shard_map.107 = (f32[32,8,128]{2,1,0:T(8,128)}, f32[512,128]{1,0:T(8,128)}, f32[512,128]{1,0:T(8,128)}) custom-call(f32[512,128]{1,0:T(8,128)S(1)} %get-tuple-element.101.refs_0_, f32[512,128]{1,0:T(8,128)S(1)} %get-tuple-element.102.refs_1_, f32[512,128]{1,0:T(8,128)S(1)} %get-tuple-element.99.refs_0_.refs_21_.refs_2_.refs_11_, ...), custom_call_target="tpu_custom_call" | custom-call | flops 1024 | bytes 16777216 | tf_op jit(solution)/shard_map/pallas_call | solution.py:51
  57.0 14.1 %all_to_all.5.refs_0_ = f32[32,8,128]{2,1,0:T(8,128)S(1)} all-to-all(f32[32,8,128]{2,1,0:T(8,128)} %get-tuple-element.119), channel_id=1, replica_groups=mesh['test'=2,'slab'=16] {'test','slab'}, dimensions={0} | all-to-all | bytes 262144 | tf_op jit(solution)/shard_map/all_to_all | solution.py:526
  71.1 1.6 %shard_map.108 = (f32[2,512,128]{2,1,0:T(8,128)S(1)}, f32[1,2,512,128]{3,2,1,0:T(8,128)S(1)}) custom-call(f32[32,8,128]{2,1,0:T(8,128)S(1)} %all_to_all.5.refs_0_, f32[512,128]{1,0:T(8,128)} %get-tuple-element.120.refs_1_, f32[512,128]{1,0:T(8,128)} %get-tuple-element.121.refs_2_, f32[512,128]{1,0:T(8,128)} %get-tuple-element.122.refs_3_, ...), custom_call_target="tpu_custom_call" | custom-call | flops 1024 | bytes 1024 | tf_op jit(solution)/shard_map/pallas_call | solution.py:51
  72.8 3.2 %collective-permute-start.16 = (f32[2,512,128]{2,1,0:T(8,128)S(1)}, f32[2,512,128]{2,1,0:T(8,128)S(1)}, u32[]{:S(2)}, u32[]{:S(2)}) collective-permute-start(f32[2,512,128]{2,1,0:T(8,128)S(1)} %get-tuple-element.127.refs_0_), channel_id=1, source_target_pairs={{16,1},{1,16},{18,3},{3,18},{20,5},{5,20},{22,7},{7,22},{24,9},{9,... | collective-permute-start | bytes 1572872 | tf_op jit(solution)/shard_map/ppermute | solution.py:441
  76.0 2.3 %collective-permute-start.14 = (f32[1,2,512,128]{3,2,1,0:T(8,128)S(1)}, f32[1,2,512,128]{3,2,1,0:T(8,128)S(1)}, u32[]{:S(2)}, u32[]{:S(2)}) collective-permute-start(f32[1,2,512,128]{3,2,1,0:T(8,128)S(1)} %get-tuple-element.126.refs_0_), channel_id=1, source_target_pairs={{16,1},{1,16},{18,3},{3,18},{20,5},{5,20},{22,7},{7,22},{24,9},{9,... | collective-permute-start | bytes 1572872 | tf_op jit(solution)/shard_map/ppermute | solution.py:441
  78.5 4.8 %collective-permute-done.16.refs_2_ = f32[2,512,128]{2,1,0:T(8,128)S(1)} collective-permute-done((f32[2,512,128]{2,1,0:T(8,128)S(1)}, f32[2,512,128]{2,1,0:T(8,128)S(1)}, u32[]{:S(2)}, u32[]{:S(2)}) %collective-permute-start.16) | collective-permute-done | bytes 524320 | tf_op jit(solution)/shard_map/ppermute | solution.py:441
  83.3 5.6 %collective-permute-done.14.refs_1_ = f32[1,2,512,128]{3,2,1,0:T(8,128)S(1)} collective-permute-done((f32[1,2,512,128]{3,2,1,0:T(8,128)S(1)}, f32[1,2,512,128]{3,2,1,0:T(8,128)S(1)}, u32[]{:S(2)}, u32[]{:S(2)}) %collective-permute-start.14) | collective-permute-done | bytes 524320 | tf_op jit(solution)/shard_map/ppermute | solution.py:441
  88.9 0.8 shard_map.109
  89.8 0.9 shard_map.110
  (27 shorter events, 1.1 us)
Async XLA Ops:
  0.6 15.8 %collective-permute-start.1 = (f32[2,512,128]{2,1,0:T(8,128)}, f32[2,512,128]{2,1,0:T(8,128)S(1)}, u32[]{:S(2)}, u32[]{:S(2)}) collective-permute-start(f32[2,512,128]{2,1,0:T(8,128)} %refs_0_.3), channel_id=1, source_target_pairs={{16,1},{1,16},{18,3},{3,18},{20,5},{5,20},{22,7},{7,22},{24,9},{9,... | collective-permute-start | bytes 1572872 | tf_op jit(solution)/shard_map/ppermute | solution.py:441
  5.8 2.8 %copy-start.1 = (f32[2,512,128]{2,1,0:T(8,128)S(1)}, f32[2,512,128]{2,1,0:T(8,128)}, u32[]{:S(2)}) copy-start(f32[2,512,128]{2,1,0:T(8,128)} %refs_0_.3) | copy-start | bytes 1572868
  8.6 9.9 %copy-start = (f32[1,2,512,128]{3,2,1,0:T(8,128)S(1)}, f32[1,2,512,128]{3,2,1,0:T(8,128)}, u32[]{:S(2)}) copy-start(f32[1,2,512,128]{3,2,1,0:T(8,128)} %refs_0_.4) | copy-start | bytes 1572868
  8.6 7.8 %collective-permute-start.2 = (f32[512,128]{1,0:T(8,128)S(1)}, f32[512,128]{1,0:T(8,128)S(1)}, u32[]{:S(2)}, u32[]{:S(2)}) collective-permute-start(f32[512,128]{1,0:T(8,128)S(1)} %dynamic-slice_bitcast_fusion.1), channel_id=1, source_target_pairs={{2,16},{18,17},{1,2},{17,3},{4,18},{20,19},{3,4},{19,5},{6,20},{22... | collective-permute-start | bytes 786440 | tf_op jit(solution)/shard_map/ppermute | solution.py:466
  10.1 10.6 %collective-permute-start = (f32[2,512,128]{2,1,0:T(8,128)S(1)}, f32[2,512,128]{2,1,0:T(8,128)S(1)}, u32[]{:S(2)}, u32[]{:S(2)}) collective-permute-start(f32[2,512,128]{2,1,0:T(8,128)S(1)} %get-tuple-element.65.refs_0_), channel_id=1, source_target_pairs={{16,1},{1,16},{18,3},{3,18},{20,5},{5,20},{22,7},{7,22},{24,9},{9,... | collective-permute-start | bytes 1572872 | tf_op jit(solution)/shard_map/ppermute | solution.py:441
  16.6 11.0 %collective-permute-start.3 = (f32[2,512,128]{2,1,0:T(8,128)S(1)}, f32[2,512,128]{2,1,0:T(8,128)S(1)}, u32[]{:S(2)}, u32[]{:S(2)}) collective-permute-start(f32[2,512,128]{2,1,0:T(8,128)S(1)} %get-tuple-element.73.refs_0_), channel_id=1, source_target_pairs={{16,1},{1,16},{18,3},{3,18},{20,5},{5,20},{22,7},{7,22},{24,9},{9,... | collective-permute-start | bytes 1572872 | tf_op jit(solution)/shard_map/ppermute | solution.py:441
  18.6 9.0 %collective-permute-start.4 = (f32[512,128]{1,0:T(8,128)S(1)}, f32[512,128]{1,0:T(8,128)S(1)}, u32[]{:S(2)}, u32[]{:S(2)}) collective-permute-start(f32[512,128]{1,0:T(8,128)S(1)} %dynamic-slice_bitcast_fusion), channel_id=1, source_target_pairs={{2,16},{18,17},{1,2},{17,3},{4,18},{20,19},{3,4},{19,5},{6,20},{22... | collective-permute-start | bytes 786440 | tf_op jit(solution)/shard_map/ppermute | solution.py:467
  19.9 7.7 %collective-permute-start.5 = (f32[512,128]{1,0:T(8,128)S(1)}, f32[512,128]{1,0:T(8,128)S(1)}, u32[]{:S(2)}, u32[]{:S(2)}) collective-permute-start(f32[512,128]{1,0:T(8,128)S(1)} %get-tuple-element.69.refs_1_.refs_3_), channel_id=1, source_target_pairs={{0,16},{16,0},{1,17},{17,1},{2,18},{18,2},{3,19},{19,3},{4,20},{20... | collective-permute-start | bytes 786440 | tf_op jit(solution)/shard_map/ppermute | solution.py:444
  20.8 16.8 %collective-permute-start.6 = (f32[512,128]{1,0:T(8,128)S(1)}, f32[512,128]{1,0:T(8,128)S(1)}, u32[]{:S(2)}, u32[]{:S(2)}) collective-permute-start(f32[512,128]{1,0:T(8,128)S(1)} %get-tuple-element.71.refs_0_.refs_2_.refs_17_.refs_7_), channel_id=1, source_target_pairs={{16,2},{2,16},{17,3},{3,17},{18,4},{4,18},{19,5},{5,19},{20,6},{6,... | collective-permute-start | bytes 786440 | tf_op jit(solution)/shard_map/ppermute | solution.py:447
  27.8 9.8 %collective-permute-start.7 = (f32[512,128]{1,0:T(8,128)S(1)}, f32[512,128]{1,0:T(8,128)S(1)}, u32[]{:S(2)}, u32[]{:S(2)}) collective-permute-start(f32[512,128]{1,0:T(8,128)S(1)} %get-tuple-element.77.refs_1_.refs_3_.refs_18_.refs_8_), channel_id=1, source_target_pairs={{0,16},{16,0},{1,17},{17,1},{2,18},{18,2},{3,19},{19,3},{4,20},{20... | collective-permute-start | bytes 786440 | tf_op jit(solution)/shard_map/ppermute | solution.py:444
  28.2 14.7 %collective-permute-start.10 = (f32[1,2,512,128]{3,2,1,0:T(8,128)S(1)}, f32[1,2,512,128]{3,2,1,0:T(8,128)S(1)}, u32[]{:S(2)}, u32[]{:S(2)}) collective-permute-start(f32[1,2,512,128]{3,2,1,0:T(8,128)S(1)} %copy-done), channel_id=1, source_target_pairs={{16,1},{1,16},{18,3},{3,18},{20,5},{5,20},{22,7},{7,22},{24,9},{9,... | collective-permute-start | bytes 1572872 | tf_op jit(solution)/shard_map/ppermute | solution.py:441
  37.8 9.0 %collective-permute-start.8 = (f32[512,128]{1,0:T(8,128)S(1)}, f32[512,128]{1,0:T(8,128)S(1)}, u32[]{:S(2)}, u32[]{:S(2)}) collective-permute-start(f32[512,128]{1,0:T(8,128)S(1)} %get-tuple-element.95.refs_0_.refs_2_.refs_19_.refs_9_), channel_id=1, source_target_pairs={{16,2},{2,16},{17,3},{3,17},{18,4},{4,18},{19,5},{5,19},{20,6},{6,... | collective-permute-start | bytes 786440 | tf_op jit(solution)/shard_map/ppermute | solution.py:447
  42.2 4.6 %collective-permute-start.9 = (f32[512,128]{1,0:T(8,128)S(1)}, f32[512,128]{1,0:T(8,128)S(1)}, u32[]{:S(2)}, u32[]{:S(2)}) collective-permute-start(f32[512,128]{1,0:T(8,128)S(1)} %get-tuple-element.96.refs_1_.refs_3_.refs_20_.refs_10_), channel_id=1, source_target_pairs={{0,16},{16,0},{1,17},{17,1},{2,18},{18,2},{3,19},{19,3},{4,20},{20... | collective-permute-start | bytes 786440 | tf_op jit(solution)/shard_map/ppermute | solution.py:444
  43.0 8.8 %collective-permute-start.11 = (f32[512,128]{1,0:T(8,128)S(1)}, f32[512,128]{1,0:T(8,128)S(1)}, u32[]{:S(2)}, u32[]{:S(2)}) collective-permute-start(f32[512,128]{1,0:T(8,128)S(1)} %get-tuple-element.105.refs_3_), channel_id=1, source_target_pairs={{0,16},{16,0},{1,17},{17,1},{2,18},{18,2},{3,19},{19,3},{4,20},{20... | collective-permute-start | bytes 786440 | tf_op jit(solution)/shard_map/ppermute | solution.py:444
  46.9 9.1 %collective-permute-start.12 = (f32[512,128]{1,0:T(8,128)S(1)}, f32[512,128]{1,0:T(8,128)S(1)}, u32[]{:S(2)}, u32[]{:S(2)}) collective-permute-start(f32[512,128]{1,0:T(8,128)S(1)} %get-tuple-element.99.refs_0_.refs_21_.refs_2_.refs_11_), channel_id=1, source_target_pairs={{16,2},{2,16},{17,3},{3,17},{18,4},{4,18},{19,5},{5,19},{20,6},{6,... | collective-permute-start | bytes 786440 | tf_op jit(solution)/shard_map/ppermute | solution.py:447
  51.3 4.7 %collective-permute-start.13 = (f32[512,128]{1,0:T(8,128)S(1)}, f32[512,128]{1,0:T(8,128)S(1)}, u32[]{:S(2)}, u32[]{:S(2)}) collective-permute-start(f32[512,128]{1,0:T(8,128)S(1)} %get-tuple-element.100.refs_1_.refs_22_.refs_3_.refs_12_), channel_id=1, source_target_pairs={{0,16},{16,0},{1,17},{17,1},{2,18},{18,2},{3,19},{19,3},{4,20},{20... | collective-permute-start | bytes 786440 | tf_op jit(solution)/shard_map/ppermute | solution.py:444
  72.8 10.5 %collective-permute-start.16 = (f32[2,512,128]{2,1,0:T(8,128)S(1)}, f32[2,512,128]{2,1,0:T(8,128)S(1)}, u32[]{:S(2)}, u32[]{:S(2)}) collective-permute-start(f32[2,512,128]{2,1,0:T(8,128)S(1)} %get-tuple-element.127.refs_0_), channel_id=1, source_target_pairs={{16,1},{1,16},{18,3},{3,18},{20,5},{5,20},{22,7},{7,22},{24,9},{9,... | collective-permute-start | bytes 1572872 | tf_op jit(solution)/shard_map/ppermute | solution.py:441
  76.0 12.9 %collective-permute-start.14 = (f32[1,2,512,128]{3,2,1,0:T(8,128)S(1)}, f32[1,2,512,128]{3,2,1,0:T(8,128)S(1)}, u32[]{:S(2)}, u32[]{:S(2)}) collective-permute-start(f32[1,2,512,128]{3,2,1,0:T(8,128)S(1)} %get-tuple-element.126.refs_0_), channel_id=1, source_target_pairs={{16,1},{1,16},{18,3},{3,18},{20,5},{5,20},{22,7},{7,22},{24,9},{9,... | collective-permute-start | bytes 1572872 | tf_op jit(solution)/shard_map/ppermute | solution.py:441
  78.4 11.4 %collective-permute-start.15 = (f32[2,512,128]{2,1,0:T(8,128)S(1)}, f32[2,512,128]{2,1,0:T(8,128)S(1)}, u32[]{:S(2)}, u32[]{:S(2)}) collective-permute-start(f32[2,512,128]{2,1,0:T(8,128)S(1)} %get-tuple-element.127.refs_0_), channel_id=1, source_target_pairs={{0,16},{16,0},{1,17},{17,1},{2,18},{18,2},{3,19},{19,3},{4,20},{20... | collective-permute-start | bytes 1572872 | tf_op jit(solution)/shard_map/ppermute | solution.py:537
  83.3 6.5 %collective-permute-start.17 = (f32[2,512,128]{2,1,0:T(8,128)S(1)}, f32[2,512,128]{2,1,0:T(8,128)S(1)}, u32[]{:S(2)}, u32[]{:S(2)}) collective-permute-start(f32[2,512,128]{2,1,0:T(8,128)S(1)} %collective-permute-done.16.refs_2_), channel_id=1, source_target_pairs={{0,16},{16,0},{1,17},{17,1},{2,18},{18,2},{3,19},{19,3},{4,20},{20... | collective-permute-start | bytes 1572872 | tf_op jit(solution)/shard_map/ppermute | solution.py:538

commit v5 on v4

--- a/solution.py
+++ b/solution.py
@@ -9,6 +9,7 @@
 CHUNK = 64
 COST = 1024
 HEADS_STEP = 0
+SPARE = 8
 VMEM = pltpu.VMEM
 SMEM = pltpu.SMEM
 
@@ -73,12 +74,12 @@
     return row_before(ref, start, count), row_after(ref, start, count), lane_before(here), lane_after(here)
 
 
-def native_kernel(width, place, pump_ref, obs_ref, data_ref, storage_ref, mask_ref, head_ref, later_ref, far_ref, near_ref):
+def native_kernel(width, first, count, place, pump_ref, obs_ref, data_ref, storage_ref, mask_ref, head_ref, later_ref, pack_ref):
     rows, depth = storage_ref.shape[1:]
     lane = lax.broadcasted_iota(jnp.int32, (min(CHUNK, rows), depth), 1)
     row = lax.broadcasted_iota(jnp.int32, (min(CHUNK, rows), depth), 0)
-    outs = [(far_ref, 0)] + [(near_ref, 2 * i) for i in range(width - 1)]
-    places = [plane_at(i, width, place[7]) for i in range(width)]
+    places = [plane_at(first + i, width, place[7]) for i in range(count)]
+    outs = [(pack_ref, 2 * i) for i in range(count)]
     for at, (out_ref, k) in zip(places, outs):
         for r, n in chunks_of(rows):
             part = slice(r, r + n)
@@ -89,7 +90,7 @@
             out_ref[k + 1, part] = jnp.where(active, store * later_ref[0, at, part], 0.0)
     lanes = lax.broadcasted_iota(jnp.int32, (1, depth), 1)
 
-    def observe(o, _):
+    def observe(o):
         cell = obs_ref[o] - place[0]
 
         @pl.when((cell >= 0) & (cell < width * rows * depth))
@@ -103,19 +104,15 @@
                     here = (lanes == local % depth) & (mask_ref[at, line] > 0)
                     out_ref[k + 1, line] += jnp.where(here, head_ref[0, at, line] - data_ref[o], 0.0)
 
-        return 0
-
-    lax.fori_loop(0, obs_ref.shape[0], observe, 0)
+    for o in range(obs_ref.shape[0]):
+        observe(o)
 
 
 def pick(place, kept, moved):
     return jnp.where(place[4], moved, kept)
 
 
-def cond_kernel(width, place, log_ref, log_moved, log_halo, *outs):
-    cond, halo = outs[:width], outs[width]
-    for r, n in chunks_of(halo.shape[0]):
-        halo[r : r + n] = jnp.exp(log_halo[r : r + n])
+def cond_kernel(width, place, log_ref, log_moved, *cond):
     for i in range(width):
         at = plane_at(i, width, place[3])
         for r, n in chunks_of(cond[0].shape[0]):
@@ -159,7 +156,7 @@
     refs = refs[len(ends) + 2 * count :]
     field, inverse, own = (refs[k * count : (k + 1) * count] for k in range(3))
     outer, refs = refs[3 * count :][: len(ends)], refs[3 * count + len(ends) :]
-    sums_ref, least_ref = refs[:2]
+    sums_ref, least_ref, *sends = refs
     rows, depth = cond[0].shape
     sums = jnp.zeros((8, depth), jnp.float32)
     least = jnp.ones((8, depth), jnp.float32)
@@ -169,7 +166,7 @@
             c, amount = cond[i][part], total[i][part]
             for k, (end, side) in enumerate(ends):
                 if i == end:
-                    other = halo[k][part]
+                    other = halo[k][part] if side else jnp.exp(halo[k][part])
                     face = jnp.where(place[1 + side], 2.0 * c * other / (c + other), 0.0)
                     outer[k][part] = face
                     amount = amount + face
@@ -183,8 +180,12 @@
             own[i][part] = own_here
             field[i][part] = v
             inverse[i][part] = inv
+            if sends and i == 0:
+                sends[0][part] = v
             sums = sums + fold(v * right)
             least = jnp.minimum(least, jnp.min(least_here.reshape(n // 8, 8, depth), axis=0))
+    for send in sends:
+        send[rows:] = jnp.zeros((send.shape[0] - rows, depth), jnp.float32)
     sums_ref[...] = sums
     least_ref[...] = least
 
@@ -339,35 +340,53 @@
     return a0 + a1 * u + a2 * q0, a2 * q1 - a1 * a0, a2 * q2
 
 
-def result_kernel(width, groups, place, told_ref, *refs):
-    stored, (gradient_ref, adjoint_ref), (fetched, arrived) = refs[: 6 * width], refs[6 * width : -2], refs[-2:]
-    fetches = [pltpu.make_async_copy(x, fetched.at[k], arrived.at[k]) for k, x in enumerate(stored)]
-    for fetch in fetches:
-        fetch.start()
-    terms, fields = (
-        [[fetched.at[k * width + i] for i in range(width)] for k in range(first, first + 3)] for first in (0, 3)
-    )
-    found = []
-    for g in range(groups):
-        sums = least = told_ref[g]
-        for k in range(g + groups, told_ref.shape[0], groups):
-            sums = sums + told_ref[k]
-            least = jnp.minimum(least, told_ref[k])
-        sums = jnp.sum(sums, axis=1, keepdims=True)
-        least = jnp.min(least, axis=1, keepdims=True)
-        found.append(combine([sums[i : i + 1] for i in range(6)], least[6:7]))
-    coefs = [jnp.where(place[5] > 0, b, a) for a, b in zip(found[0], found[-1])]
-    rows, depth = fetched.shape[1:]
-    wide = [jnp.broadcast_to(c, (8, depth)) for c in coefs]
-    for fetch in fetches:
-        fetch.wait()
-    for r, n in chunks_of(rows):
+def weigh(places, coefs, arrays, store):
+    for r, n in chunks_of(arrays[0][0].shape[0]):
         part = slice(r, r + n)
-        scale = [jnp.concatenate([c] * (n // 8), axis=0) for c in wide]
-        for i in range(width):
-            at = plane_at(i, width, place[3])
-            gradient_ref[at, part] = -sum(c * t[i][part] for c, t in zip(scale, terms))
-            adjoint_ref[0, at, part] = sum(c * f[i][part] for c, f in zip(scale, fields))
+        scale = [jnp.concatenate([c] * (n // 8), axis=0) for c in coefs]
+        for i, at in enumerate(places):
+            store(at, part, sum(c * a[i][part] for c, a in zip(scale, arrays)))
+
+
+def fetch_all(stored, fetched, arrived, width):
+    copies = [pltpu.make_async_copy(x, fetched.at[k], arrived.at[k]) for k, x in enumerate(stored)]
+    for copy in copies:
+        copy.start()
+    return copies, [[fetched.at[k * width + i] for i in range(width)] for k in range(3)]
+
+
+def gradient_sum_kernel(width, place, told_ref, *refs):
+    stored, (gradient_ref, coef_ref, fetched, arrived) = refs[: 3 * width], refs[3 * width :]
+    copies, terms = fetch_all(stored, fetched, arrived, width)
+    sums = least = told_ref[0]
+    for k in range(1, told_ref.shape[0]):
+        sums = sums + told_ref[k]
+        least = jnp.minimum(least, told_ref[k])
+    sums = jnp.sum(sums, axis=1, keepdims=True)
+    least = jnp.min(least, axis=1, keepdims=True)
+    coefs = combine([sums[i : i + 1] for i in range(6)], least[6:7])
+    depth = coef_ref.shape[1]
+    for k, c in enumerate(coefs):
+        coef_ref[8 * k : 8 * k + 8] = jnp.broadcast_to(c, (8, depth))
+    for copy in copies:
+        copy.wait()
+
+    def store(at, part, value):
+        gradient_ref[at, part] = value
+
+    weigh([plane_at(i, width, place[3]) for i in range(width)], [jnp.broadcast_to(-c, (8, depth)) for c in coefs], terms, store)
+
+
+def lambda_kernel(width, place, coef_ref, *refs):
+    stored, (adjoint_ref, fetched, arrived) = refs[: 3 * width], refs[3 * width :]
+    copies, fields = fetch_all(stored, fetched, arrived, width)
+    for copy in copies:
+        copy.wait()
+
+    def store(at, part, value):
+        adjoint_ref[0, at, part] = value
+
+    weigh([plane_at(i, width, place[3]) for i in range(width)], [coef_ref[8 * k : 8 * k + 8] for k in range(3)], fields, store)
 
 
 def adjoint_kernel(place, kept, moved, out_ref):
@@ -400,7 +419,8 @@
         pairs = [(slabs + 2 * j, 2 * j + 1) for j in range(slabs // 2)]
         far_pairs = [(slabs + i, i + 2) for i in range(slabs - 2)]
         near_axis, near = "test", [(0, 1), (1, 0)]
-        far_axis, groups = BOTH, 2
+        far_axis = BOTH
+        same_test = [[t * slabs + i for t in range(2) for i in range(x, slabs, 2)] for x in range(2)]
         at = lambda t, i: t * slabs + i
         first_far = [
             way
@@ -416,7 +436,7 @@
         pairs = []
         far_pairs = [(i, i + 1) for i in range(1, slabs - 1, 2)]
         near_axis, near = "slab", [(i, i ^ 1) for i in range(slabs) if i ^ 1 < slabs]
-        far_axis, groups = "slab", 1
+        far_axis, same_test = "slab", None
     both_ways = lambda links: [way for a, b in links for way in ((a, b), (b, a))]
     if not turned:
         first_far = both_ways(far_pairs)
@@ -455,25 +475,27 @@
     far_at = plane_at(0, width, position()[7])
     far_plane = lambda x: lax.dynamic_slice(x, (far_at, 0, 0), (1, rows, depth))[0]
     log_moved = move(log_conductivity)
-    far_pack, near_pack = call(
-        lambda *refs: native_kernel(width, position(), *refs),
-        [pump_cells, obs_cells, obs_data[0], storage, active_mask, heads, adjoint_next],
-        [(2, rows, depth), (2 * (width - 1), rows, depth)],
-        scalars=3,
-        space=pltpu.HBM,
-    )
+    def native(first, count):
+        (pack,) = call(
+            lambda *refs: native_kernel(width, first, count, position(), *refs),
+            [pump_cells, obs_cells, obs_data[0], storage, active_mask, heads, adjoint_next],
+            [(2 * count, rows, depth)],
+            scalars=3,
+            space=pltpu.HBM,
+        )
+        return pack
+
+    far_pack, near_pack = native(0, 1), native(1, width - 1)
     far_moved = move(far_pack)
     log_halo = lax.ppermute(after(far_plane(log_conductivity), far_pack), far_axis, first_far)
-    head_far = lax.ppermute(after(far_plane(heads[0]), far_pack), far_axis, first_far)
-    *cond, cond_far = call(
+    cond = call(
         lambda *refs: cond_kernel(width, position(), *refs),
-        [log_conductivity, log_moved, log_halo],
-        [*planes, plane],
+        [log_conductivity, log_moved],
+        planes,
         space=None,
     )
-    cond_halo = [cond_far, swap_near(cond[-1])]
-    near_moved = move(after(near_pack, *cond))
-    near_moved, head_far = lax.optimization_barrier((near_moved, head_far))
+    cond_halo = [log_halo, swap_near(cond[-1])]
+    near_moved = move(after(near_pack, *cond, log_halo))
     total, faces = (lambda x: (x[:width], x[width:]))(
         call(lambda *refs: face_kernel(width, *refs), cond, planes * (1 + SIDES) + [plane] * (width - 1))
     )
@@ -481,12 +503,12 @@
         started = call(
             lambda *refs: start_kernel(count, ends, position(), *refs),
             [pack, pack_moved, *(cond_halo[side] for _, side in ends), *cond[first:][:count], *total[first:][:count]],
-            [plane] * (3 * count + len(ends)) + [(8, depth)] * 2,
+            [plane] * (3 * count + len(ends)) + [(8, depth)] * 2 + [(rows + SPARE, depth)] * (not first),
         )
         return [*(started[k * count : (k + 1) * count] for k in range(3)), started[3 * count :]]
 
-    field, inverse, own, (outer_far, sum_far, least_far) = start(0, 1, [(0, 0)], far_pack, far_moved)
-    v_halo = swap_far(field[0])
+    field, inverse, own, (outer_far, sum_far, least_far, send) = start(0, 1, [(0, 0)], far_pack, far_moved)
+    v_halo = swap_far(send)
     field_near, inverse_near, own_near, (outer_near, sum_near, least_near) = start(
         1, width - 1, [(width - 2, 1)], near_pack, near_moved
     )
@@ -497,12 +519,13 @@
     for step in range(3):
         halo = [swap_far(field[0]) if step else v_halo, swap_near(field[-1])]
         fields += field
-        image = call(lambda *refs: inner_kernel(width, *refs), [*field, *own, *faces], planes)
+        image = call(lambda *refs: inner_kernel(width, *refs), [*field, *own, *faces], planes, cost=(1 << 23) if step == 1 else COST)
         if step == HEADS_STEP:
             heads_moved = move(after(heads, *image))
-        if step == 2:
+        if step == 1:
+            heads_moved = after(heads_moved, *image)
             head = call(lambda *refs: head_kernel(width, position(), *refs), [heads, heads_moved], planes, space=None)
-            head_near = swap_near(head[-1])
+            head_far, head_near = swap_far(head[0]), swap_near(head[-1])
         if step < 2:
             halos += halo
             made = call(
@@ -520,17 +543,26 @@
     told, *last_terms = call(
         lambda *refs: last_kernel(width, *refs),
         [*image, *field, *terms[2 * width :], *outer, *halo, weight_0, weight_1, *sums, least_far, least_near],
-        [hbm(groups * slabs, 8, depth)] + [hbm(*plane)] * width,
+        [hbm(slabs, 8, depth)] + [hbm(*plane)] * width,
         cost=1 << 24,
     )
-    told = lax.all_to_all(told, BOTH if turned else "slab", 0, 0, tiled=True)
-    gradient, adjoint = call(
-        lambda *refs: result_kernel(width, groups, position(), *refs),
-        [told, *(pltpu.with_memory_space_constraint(x, pltpu.HBM) for x in (*terms[: 2 * width], *last_terms)), *fields],
-        [stack, (1, *stack) if turned else jax.ShapeDtypeStruct((1, *stack), jnp.float32)],
+    told = lax.all_to_all(told, far_axis, 0, 0, axis_index_groups=same_test, tiled=True)
+    fetching = dict(
         space=None,
-        stored=6 * width,
-        scratch=[VMEM((6 * width, rows, depth), jnp.float32), pltpu.SemaphoreType.DMA((6 * width,))],
+        stored=3 * width,
+        scratch=[VMEM((3 * width, rows, depth), jnp.float32), pltpu.SemaphoreType.DMA((3 * width,))],
+    )
+    gradient, coefs = call(
+        lambda *refs: gradient_sum_kernel(width, position(), *refs),
+        [told, *(pltpu.with_memory_space_constraint(x, pltpu.HBM) for x in (*terms[: 2 * width], *last_terms))],
+        [stack, (24, depth)],
+        **fetching,
+    )
+    (adjoint,) = call(
+        lambda *refs: lambda_kernel(width, position(), *refs),
+        [coefs, *fields],
+        [(1, *stack) if turned else jax.ShapeDtypeStruct((1, *stack), jnp.float32)],
+        **fetching,
     )
     if turned:
         other = move(gradient)

time: 91.2 us -> 89.2 us (0.978)
  starting transfers between devices: 41.5 us -> 37.3 us
  Pallas kernels: 12.1 us -> 14.5 us
    ppermute x6, starting transfers between devices: 22.6 us -> 18.5 us  [move(): return lax.ppermute(x, BOTH, both_ways(pairs)) if turned else x]
    ppermute x6, waiting for transfers between devices: 11 us -> 14.3 us  [move(): return lax.ppermute(x, BOTH, both_ways(pairs)) if turned else x]
    ppermute x3 -> x4, waiting for transfers between devices: 6.71 us -> 3.88 us  [swap_far(): return lax.ppermute(x, far_axis, both_ways(far_pairs))]
    pallas_call x16 -> x18, Pallas kernels: 12.1 us -> 14.5 us  [call(): pl.pallas_call(kernel, out_shape=out_shape, in_specs=[pl.BlockSpec(memory...]
    ppermute x1, waiting for transfers between devices: 3.6 us -> 1.23 us  [on_device(): lax.ppermute(after(far_plane(log_conductivity), far_pack), far_axis, firs...]
    ppermute x3 -> x4, starting transfers between devices: 15.5 us -> 17.1 us  [swap_far(): return lax.ppermute(x, far_axis, both_ways(far_pairs))]
    ppermute x5, waiting for transfers between devices: 0.01 us -> 1.52 us  [swap_near(): return lax.ppermute(x, near_axis, near)]
    ppermute x1 -> x0, starting transfers between devices: 1.29 us -> none  [on_device(): lax.ppermute(after(far_plane(heads[0]), far_pack), far_axis, first_far)]
  transfers between devices with their start and end apart: 18 -> 18, of which waited for: 8 -> 9; matrix products, arithmetic and copies ran while one was open for 0% -> 0% of each run, Pallas kernels for 9% -> 12%
where the time goes in v5:
time: 89.2 us; the launch traced here: 88.6 us
  starting transfers between devices  37.3 us (42%)
  waiting for transfers between devices  21 us (24%)
  Pallas kernels  14.5 us (16%)
  blocking collectives  13.6 us (15%)
  between operations  1.58 us (2%)
    ppermute x6, starting transfers between devices, move(): return lax.ppermute(x, BOTH, both_ways(pairs)) if turned else x  18.5 us
    ppermute x4, starting transfers between devices, swap_far(): return lax.ppermute(x, far_axis, both_ways(far_pairs))  17.1 us
    pallas_call x18, Pallas kernels, call(): pl.pallas_call(kernel, out_shape=out_shape, in_specs=[pl.BlockSpec(memory...  14.5 us
    ppermute x6, waiting for transfers between devices, move(): return lax.ppermute(x, BOTH, both_ways(pairs)) if turned else x  14.3 us
    all_to_all x1, blocking collectives, on_device(): lax.all_to_all(told, far_axis, 0, 0, axis_index_groups=same_test, tiled=T...  13.6 us
    ppermute x4, waiting for transfers between devices, swap_far(): return lax.ppermute(x, far_axis, both_ways(far_pairs))  3.88 us
  transfers between devices with their start and end apart: 18, of which 9 were waited for; matrix products, arithmetic and copies ran while one was open for 0% of the time, Pallas kernels for 12%

profile of v5, /device:TPU:1, one launch (start us, length us, event | category | flops | bytes accessed | tf_op | source)
XLA Modules:
  0.0 88.6 jit_solution(1014760049927012735)
XLA Ops:
  0.6 4.5 %collective-permute-start.2 = (f32[2,512,128]{2,1,0:T(8,128)}, f32[2,512,128]{2,1,0:T(8,128)S(1)}, u32[]{:S(2)}, u32[]{:S(2)}) collective-permute-start(f32[2,512,128]{2,1,0:T(8,128)} %refs_0_.4), channel_id=1, source_target_pairs={{16,1},{1,16},{18,3},{3,18},{20,5},{5,20},{22,7},{7,22},{24,9},{9,... | collective-permute-start | bytes 1572872 | tf_op jit(solution)/shard_map/ppermute | solution.py:461
  5.8 2.3 %shard_map.95.refs_0_ = f32[2,512,128]{2,1,0:T(8,128)S(1)} custom-call(s32[1]{0:T(128)S(6)} %copy.10.refs_0_, s32[64]{0:T(128)} %refs_1_.3, f32[64]{0:T(128)} %bitcast.3, f32[2,512,128]{2,1,0:T(8,128)} %refs_3_.3, s32[2,512,128]{2,1,0:T(8,128)} %refs_4_.3, f32[1,2,512,128]{3,2,1,0:T(8,128)} %refs_0_.5, f32[1,2,512,128]{3,2,1,0:T(8,128)} %refs_6_.3), custom_call_target="tpu_custom_call" | custom-call | flops 1024 | bytes 1024 | tf_op jit(solution)/shard_map/pallas_call | solution.py:52
  8.1 1.3 %collective-permute-start.1 = (f32[512,128]{1,0:T(8,128)S(1)}, f32[512,128]{1,0:T(8,128)S(1)}, u32[]{:S(2)}, u32[]{:S(2)}) collective-permute-start(f32[512,128]{1,0:T(8,128)S(1)} %dynamic-slice_bitcast_fusion), channel_id=1, source_target_pairs={{2,16},{18,17},{1,2},{17,3},{4,18},{20,19},{3,4},{19,5},{6,20},{22... | collective-permute-start | bytes 786440 | tf_op jit(solution)/shard_map/ppermute | solution.py:490
  9.4 2.8 %collective-permute-start = (f32[2,512,128]{2,1,0:T(8,128)S(1)}, f32[2,512,128]{2,1,0:T(8,128)S(1)}, u32[]{:S(2)}, u32[]{:S(2)}) collective-permute-start(f32[2,512,128]{2,1,0:T(8,128)S(1)} %shard_map.95.refs_0_), channel_id=1, source_target_pairs={{16,1},{1,16},{18,3},{3,18},{20,5},{5,20},{22,7},{7,22},{24,9},{9,... | collective-permute-start | bytes 1572872 | tf_op jit(solution)/shard_map/ppermute | solution.py:461
  12.3 2.2 %shard_map.99.refs_0_ = f32[2,512,128]{2,1,0:T(8,128)S(1)} custom-call(s32[1]{0:T(128)S(6)} %copy.10.refs_0_, s32[64]{0:T(128)} %refs_1_.3, f32[64]{0:T(128)} %bitcast.4, f32[2,512,128]{2,1,0:T(8,128)} %refs_3_.3, s32[2,512,128]{2,1,0:T(8,128)} %refs_4_.3, f32[1,2,512,128]{3,2,1,0:T(8,128)} %refs_0_.5, f32[1,2,512,128]{3,2,1,0:T(8,128)} %refs_6_.3), custom_call_target="tpu_custom_call" | custom-call | flops 1024 | bytes 1024 | tf_op jit(solution)/shard_map/pallas_call | solution.py:52
  14.6 1.2 %collective-permute-done.1.refs_2_ = f32[512,128]{1,0:T(8,128)S(1)} collective-permute-done((f32[512,128]{1,0:T(8,128)S(1)}, f32[512,128]{1,0:T(8,128)S(1)}, u32[]{:S(2)}, u32[]{:S(2)}) %collective-permute-start.1) | collective-permute-done | bytes 262176 | tf_op jit(solution)/shard_map/ppermute | solution.py:490
  15.8 1.9 %collective-permute-start.3 = (f32[2,512,128]{2,1,0:T(8,128)S(1)}, f32[2,512,128]{2,1,0:T(8,128)S(1)}, u32[]{:S(2)}, u32[]{:S(2)}) collective-permute-start(f32[2,512,128]{2,1,0:T(8,128)S(1)} %shard_map.99.refs_0_), channel_id=1, source_target_pairs={{16,1},{1,16},{18,3},{3,18},{20,5},{5,20},{22,7},{7,22},{24,9},{9,... | collective-permute-start | bytes 1572872 | tf_op jit(solution)/shard_map/ppermute | solution.py:461
  17.8 0.5 shard_map.97
  18.3 2.3 %collective-permute-done.refs_1_ = f32[2,512,128]{2,1,0:T(8,128)S(1)} collective-permute-done((f32[2,512,128]{2,1,0:T(8,128)S(1)}, f32[2,512,128]{2,1,0:T(8,128)S(1)}, u32[]{:S(2)}, u32[]{:S(2)}) %collective-permute-start) | collective-permute-done | bytes 524320 | tf_op jit(solution)/shard_map/ppermute | solution.py:461
  20.8 4.0 %collective-permute-start.5 = (f32[520,128]{1,0:T(8,128)S(1)}, f32[520,128]{1,0:T(8,128)S(1)}, u32[]{:S(2)}, u32[]{:S(2)}) collective-permute-start(f32[520,128]{1,0:T(8,128)S(1)} %get-tuple-element.86), channel_id=1, source_target_pairs={{16,2},{2,16},{17,3},{3,17},{18,4},{4,18},{19,5},{5,19},{20,6},{6,... | collective-permute-start | bytes 798728 | tf_op jit(solution)/shard_map/ppermute | solution.py:467
  24.9 1.4 %collective-permute-done.3.refs_1_ = f32[2,512,128]{2,1,0:T(8,128)S(1)} collective-permute-done((f32[2,512,128]{2,1,0:T(8,128)S(1)}, f32[2,512,128]{2,1,0:T(8,128)S(1)}, u32[]{:S(2)}, u32[]{:S(2)}) %collective-permute-start.3) | collective-permute-done | bytes 524320 | tf_op jit(solution)/shard_map/ppermute | solution.py:461
  26.5 0.4 shard_map.101
  26.9 0.6 copy-done
  27.6 3.7 %collective-permute-start.9 = (f32[1,2,512,128]{3,2,1,0:T(8,128)S(1)}, f32[1,2,512,128]{3,2,1,0:T(8,128)S(1)}, u32[]{:S(2)}, u32[]{:S(2)}) collective-permute-start(f32[1,2,512,128]{3,2,1,0:T(8,128)S(1)} %copy-done), channel_id=1, source_target_pairs={{16,1},{1,16},{18,3},{3,18},{20,5},{5,20},{22,7},{7,22},{24,9},{9,... | collective-permute-start | bytes 1572872 | tf_op jit(solution)/shard_map/ppermute | solution.py:461
  31.4 1.5 %collective-permute-done.6.refs_9_.refs_24_ = f32[512,128]{1,0:T(8,128)S(1)} collective-permute-done((f32[512,128]{1,0:T(8,128)S(1)}, f32[512,128]{1,0:T(8,128)S(1)}, u32[]{:S(2)}, u32[]{:S(2)}) %collective-permute-start.6) | collective-permute-done | bytes 262176 | tf_op jit(solution)/shard_map/ppermute | solution.py:464
  33.1 4.2 %collective-permute-start.7 = (f32[512,128]{1,0:T(8,128)S(1)}, f32[512,128]{1,0:T(8,128)S(1)}, u32[]{:S(2)}, u32[]{:S(2)}) collective-permute-start(f32[512,128]{1,0:T(8,128)S(1)} %get-tuple-element.87.refs_0_.refs_2_.refs_19_.refs_3_), channel_id=1, source_target_pairs={{16,2},{2,16},{17,3},{3,17},{18,4},{4,18},{19,5},{5,19},{20,6},{6,... | collective-permute-start | bytes 786440 | tf_op jit(solution)/shard_map/ppermute | solution.py:467
  37.3 0.4 shard_map.103
  37.7 0.4 collective-permute-done.9.refs_1_
  38.2 4.5 %collective-permute-start.10 = (f32[512,128]{1,0:T(8,128)S(1)}, f32[512,128]{1,0:T(8,128)S(1)}, u32[]{:S(2)}, u32[]{:S(2)}) collective-permute-start(f32[512,128]{1,0:T(8,128)S(1)} %get-tuple-element.97.refs_2_), channel_id=1, source_target_pairs={{16,2},{2,16},{17,3},{3,17},{18,4},{4,18},{19,5},{5,19},{20,6},{6,... | collective-permute-start | bytes 786440 | tf_op jit(solution)/shard_map/ppermute | solution.py:467
  42.8 0.6 collective-permute-done.7.refs_8_.refs_25_
  43.6 4.4 %collective-permute-start.12 = (f32[512,128]{1,0:T(8,128)S(1)}, f32[512,128]{1,0:T(8,128)S(1)}, u32[]{:S(2)}, u32[]{:S(2)}) collective-permute-start(f32[512,128]{1,0:T(8,128)S(1)} %get-tuple-element.91.refs_0_.refs_21_.refs_2_.refs_5_), channel_id=1, source_target_pairs={{16,2},{2,16},{17,3},{3,17},{18,4},{4,18},{19,5},{5,19},{20,6},{6,... | collective-permute-start | bytes 786440 | tf_op jit(solution)/shard_map/ppermute | solution.py:467
  48.5 2.8 %shard_map.107 = (f32[512,128]{1,0:T(8,128)}, f32[512,128]{1,0:T(8,128)}, f32[512,128]{1,0:T(8,128)}, f32[512,128]{1,0:T(8,128)}, f32[512,128]{1,0:T(8,128)S(1)}...) custom-call(f32[512,128]{1,0:T(8,128)S(1)} %get-tuple-element.62.refs_0_.refs_3_, ...), custom_call_target="tpu_custom_call" | custom-call | flops 1024 | bytes 1024 | tf_op jit(solution)/shard_map/pallas_call | solution.py:52
  51.3 3.3 %collective-permute-done.12.refs_8_ = f32[512,128]{1,0:T(8,128)S(1)} collective-permute-done((f32[512,128]{1,0:T(8,128)S(1)}, f32[512,128]{1,0:T(8,128)S(1)}, u32[]{:S(2)}, u32[]{:S(2)}) %collective-permute-start.12) | collective-permute-done | bytes 262176 | tf_op jit(solution)/shard_map/ppermute | solution.py:467
  54.6 1.0 %shard_map.108 = (f32[16,8,128]{2,1,0:T(8,128)}, f32[512,128]{1,0:T(8,128)}, f32[512,128]{1,0:T(8,128)}) custom-call(f32[512,128]{1,0:T(8,128)S(1)} %get-tuple-element.93.refs_0_, f32[512,128]{1,0:T(8,128)S(1)} %get-tuple-element.94.refs_1_, f32[512,128]{1,0:T(8,128)S(1)} %get-tuple-element.91.refs_0_.refs_21_.refs_2_.refs_5_, ...), custom_call_target="tpu_custom_call" | custom-call | flops 1024 | bytes 16777216 | tf_op jit(solution)/shard_map/pallas_call | solution.py:52
  55.6 13.6 %all_to_all.5.refs_0_ = f32[16,8,128]{2,1,0:T(8,128)S(1)} all-to-all(f32[16,8,128]{2,1,0:T(8,128)} %get-tuple-element.111), channel_id=1, replica_groups={{0,2,4,6,8,10,12,14,16,18,20,22,24,26,28,30},{1,3,5,7,9,11,13,15,17,19,..., dimensions={0} | all-to-all | bytes 131072 | tf_op jit(solution)/shard_map/all_to_all | solution.py:549
  69.2 1.5 %shard_map.109 = (f32[2,512,128]{2,1,0:T(8,128)S(1)}, f32[24,128]{1,0:T(8,128)S(1)}) custom-call(f32[16,8,128]{2,1,0:T(8,128)S(1)} %all_to_all.5.refs_0_, f32[512,128]{1,0:T(8,128)} %get-tuple-element.112.refs_1_, f32[512,128]{1,0:T(8,128)} %get-tuple-element.113.refs_2_, f32[512,128]{1,0:T(8,128)} %get-tuple-element.114.refs_3_, ...), custom_call_target="tpu_custom_call" | custom-call | flops 1024 | bytes 1024 | tf_op jit(solution)/shard_map/pallas_call | solution.py:52
  70.7 2.7 %collective-permute-start.16 = (f32[2,512,128]{2,1,0:T(8,128)S(1)}, f32[2,512,128]{2,1,0:T(8,128)S(1)}, u32[]{:S(2)}, u32[]{:S(2)}) collective-permute-start(f32[2,512,128]{2,1,0:T(8,128)S(1)} %get-tuple-element.119.refs_0_), channel_id=1, source_target_pairs={{16,1},{1,16},{18,3},{3,18},{20,5},{5,20},{22,7},{7,22},{24,9},{9,... | collective-permute-start | bytes 1572872 | tf_op jit(solution)/shard_map/ppermute | solution.py:461
  73.7 2.9 %collective-permute-start.14 = (f32[1,2,512,128]{3,2,1,0:T(8,128)S(1)}, f32[1,2,512,128]{3,2,1,0:T(8,128)S(1)}, u32[]{:S(2)}, u32[]{:S(2)}) collective-permute-start(f32[1,2,512,128]{3,2,1,0:T(8,128)S(1)} %shard_map.110.refs_0_), channel_id=1, source_target_pairs={{16,1},{1,16},{18,3},{3,18},{20,5},{5,20},{22,7},{7,22},{24,9},{9,... | collective-permute-start | bytes 1572872 | tf_op jit(solution)/shard_map/ppermute | solution.py:461
  76.7 4.6 %collective-permute-done.16.refs_2_ = f32[2,512,128]{2,1,0:T(8,128)S(1)} collective-permute-done((f32[2,512,128]{2,1,0:T(8,128)S(1)}, f32[2,512,128]{2,1,0:T(8,128)S(1)}, u32[]{:S(2)}, u32[]{:S(2)}) %collective-permute-start.16) | collective-permute-done | bytes 524320 | tf_op jit(solution)/shard_map/ppermute | solution.py:461
  81.2 5.6 %collective-permute-done.14.refs_1_ = f32[1,2,512,128]{3,2,1,0:T(8,128)S(1)} collective-permute-done((f32[1,2,512,128]{3,2,1,0:T(8,128)S(1)}, f32[1,2,512,128]{3,2,1,0:T(8,128)S(1)}, u32[]{:S(2)}, u32[]{:S(2)}) %collective-permute-start.14) | collective-permute-done | bytes 524320 | tf_op jit(solution)/shard_map/ppermute | solution.py:461
  86.8 0.8 shard_map.111
  87.7 0.9 %shard_map.112 = f32[2,512,128]{2,1,0:T(8,128)} custom-call(f32[2,512,128]{2,1,0:T(8,128)S(1)} %get-tuple-element.119.refs_0_, f32[2,512,128]{2,1,0:T(8,128)S(1)} %collective-permute-done.15.refs_1_, f32[2,512,128]{2,1,0:T(8,128)S(1)} %collective-permute-done.16.refs_2_, f32[2,512,128]{2,1,0:T(8,128)S(1)} %collective-permute-done.17.refs_3_), custom_call_target="tpu_custom_call" | custom-call | flops 1024 | bytes 1024 | tf_op jit(solution)/shard_map/pallas_call | solution.py:52
  (28 shorter events, 2.1 us)
Async XLA Ops:
  0.6 13.9 %collective-permute-start.2 = (f32[2,512,128]{2,1,0:T(8,128)}, f32[2,512,128]{2,1,0:T(8,128)S(1)}, u32[]{:S(2)}, u32[]{:S(2)}) collective-permute-start(f32[2,512,128]{2,1,0:T(8,128)} %refs_0_.4), channel_id=1, source_target_pairs={{16,1},{1,16},{18,3},{3,18},{20,5},{5,20},{22,7},{7,22},{24,9},{9,... | collective-permute-start | bytes 1572872 | tf_op jit(solution)/shard_map/ppermute | solution.py:461
  5.8 2.3 %copy-start.1 = (f32[2,512,128]{2,1,0:T(8,128)S(1)}, f32[2,512,128]{2,1,0:T(8,128)}, u32[]{:S(2)}) copy-start(f32[2,512,128]{2,1,0:T(8,128)} %refs_0_.4) | copy-start | bytes 1572868
  8.1 7.7 %collective-permute-start.1 = (f32[512,128]{1,0:T(8,128)S(1)}, f32[512,128]{1,0:T(8,128)S(1)}, u32[]{:S(2)}, u32[]{:S(2)}) collective-permute-start(f32[512,128]{1,0:T(8,128)S(1)} %dynamic-slice_bitcast_fusion), channel_id=1, source_target_pairs={{2,16},{18,17},{1,2},{17,3},{4,18},{20,19},{3,4},{19,5},{6,20},{22... | collective-permute-start | bytes 786440 | tf_op jit(solution)/shard_map/ppermute | solution.py:490
  9.4 11.2 %collective-permute-start = (f32[2,512,128]{2,1,0:T(8,128)S(1)}, f32[2,512,128]{2,1,0:T(8,128)S(1)}, u32[]{:S(2)}, u32[]{:S(2)}) collective-permute-start(f32[2,512,128]{2,1,0:T(8,128)S(1)} %shard_map.95.refs_0_), channel_id=1, source_target_pairs={{16,1},{1,16},{18,3},{3,18},{20,5},{5,20},{22,7},{7,22},{24,9},{9,... | collective-permute-start | bytes 1572872 | tf_op jit(solution)/shard_map/ppermute | solution.py:461
  15.8 10.5 %collective-permute-start.3 = (f32[2,512,128]{2,1,0:T(8,128)S(1)}, f32[2,512,128]{2,1,0:T(8,128)S(1)}, u32[]{:S(2)}, u32[]{:S(2)}) collective-permute-start(f32[2,512,128]{2,1,0:T(8,128)S(1)} %shard_map.99.refs_0_), channel_id=1, source_target_pairs={{16,1},{1,16},{18,3},{3,18},{20,5},{5,20},{22,7},{7,22},{24,9},{9,... | collective-permute-start | bytes 1572872 | tf_op jit(solution)/shard_map/ppermute | solution.py:461
  17.8 7.1 %collective-permute-start.4 = (f32[512,128]{1,0:T(8,128)S(1)}, f32[512,128]{1,0:T(8,128)S(1)}, u32[]{:S(2)}, u32[]{:S(2)}) collective-permute-start(f32[512,128]{1,0:T(8,128)S(1)} %get-tuple-element.63.refs_1_.refs_3_), channel_id=1, source_target_pairs={{0,16},{16,0},{1,17},{17,1},{2,18},{18,2},{3,19},{19,3},{4,20},{20... | collective-permute-start | bytes 786440 | tf_op jit(solution)/shard_map/ppermute | solution.py:464
  20.8 10.5 %collective-permute-start.5 = (f32[520,128]{1,0:T(8,128)S(1)}, f32[520,128]{1,0:T(8,128)S(1)}, u32[]{:S(2)}, u32[]{:S(2)}) collective-permute-start(f32[520,128]{1,0:T(8,128)S(1)} %get-tuple-element.86), channel_id=1, source_target_pairs={{16,2},{2,16},{17,3},{3,17},{18,4},{4,18},{19,5},{5,19},{20,6},{6,... | collective-permute-start | bytes 798728 | tf_op jit(solution)/shard_map/ppermute | solution.py:467
  26.5 1.0 %copy-start = (f32[1,2,512,128]{3,2,1,0:T(8,128)S(1)}, f32[1,2,512,128]{3,2,1,0:T(8,128)}, u32[]{:S(2)}) copy-start(f32[1,2,512,128]{3,2,1,0:T(8,128)} %refs_0_.5) | copy-start | bytes 1572868
  27.6 10.6 %collective-permute-start.9 = (f32[1,2,512,128]{3,2,1,0:T(8,128)S(1)}, f32[1,2,512,128]{3,2,1,0:T(8,128)S(1)}, u32[]{:S(2)}, u32[]{:S(2)}) collective-permute-start(f32[1,2,512,128]{3,2,1,0:T(8,128)S(1)} %copy-done), channel_id=1, source_target_pairs={{16,1},{1,16},{18,3},{3,18},{20,5},{5,20},{22,7},{7,22},{24,9},{9,... | collective-permute-start | bytes 1572872 | tf_op jit(solution)/shard_map/ppermute | solution.py:461
  31.3 1.6 %collective-permute-start.6 = (f32[512,128]{1,0:T(8,128)S(1)}, f32[512,128]{1,0:T(8,128)S(1)}, u32[]{:S(2)}, u32[]{:S(2)}) collective-permute-start(f32[512,128]{1,0:T(8,128)S(1)} %get-tuple-element.68.refs_1_.refs_3_.refs_18_.refs_2_), channel_id=1, source_target_pairs={{0,16},{16,0},{1,17},{17,1},{2,18},{18,2},{3,19},{19,3},{4,20},{20... | collective-permute-start | bytes 786440 | tf_op jit(solution)/shard_map/ppermute | solution.py:464
  33.1 10.3 %collective-permute-start.7 = (f32[512,128]{1,0:T(8,128)S(1)}, f32[512,128]{1,0:T(8,128)S(1)}, u32[]{:S(2)}, u32[]{:S(2)}) collective-permute-start(f32[512,128]{1,0:T(8,128)S(1)} %get-tuple-element.87.refs_0_.refs_2_.refs_19_.refs_3_), channel_id=1, source_target_pairs={{16,2},{2,16},{17,3},{3,17},{18,4},{4,18},{19,5},{5,19},{20,6},{6,... | collective-permute-start | bytes 786440 | tf_op jit(solution)/shard_map/ppermute | solution.py:467
  37.2 6.1 %collective-permute-start.8 = (f32[512,128]{1,0:T(8,128)S(1)}, f32[512,128]{1,0:T(8,128)S(1)}, u32[]{:S(2)}, u32[]{:S(2)}) collective-permute-start(f32[512,128]{1,0:T(8,128)S(1)} %get-tuple-element.88.refs_1_.refs_3_.refs_20_.refs_4_), channel_id=1, source_target_pairs={{0,16},{16,0},{1,17},{17,1},{2,18},{18,2},{3,19},{19,3},{4,20},{20... | collective-permute-start | bytes 786440 | tf_op jit(solution)/shard_map/ppermute | solution.py:464
  38.2 10.2 %collective-permute-start.10 = (f32[512,128]{1,0:T(8,128)S(1)}, f32[512,128]{1,0:T(8,128)S(1)}, u32[]{:S(2)}, u32[]{:S(2)}) collective-permute-start(f32[512,128]{1,0:T(8,128)S(1)} %get-tuple-element.97.refs_2_), channel_id=1, source_target_pairs={{16,2},{2,16},{17,3},{3,17},{18,4},{4,18},{19,5},{5,19},{20,6},{6,... | collective-permute-start | bytes 786440 | tf_op jit(solution)/shard_map/ppermute | solution.py:467
  42.7 5.8 %collective-permute-start.11 = (f32[512,128]{1,0:T(8,128)S(1)}, f32[512,128]{1,0:T(8,128)S(1)}, u32[]{:S(2)}, u32[]{:S(2)}) collective-permute-start(f32[512,128]{1,0:T(8,128)S(1)} %get-tuple-element.98.refs_3_), channel_id=1, source_target_pairs={{0,16},{16,0},{1,17},{17,1},{2,18},{18,2},{3,19},{19,3},{4,20},{20... | collective-permute-start | bytes 786440 | tf_op jit(solution)/shard_map/ppermute | solution.py:464
  43.6 11.0 %collective-permute-start.12 = (f32[512,128]{1,0:T(8,128)S(1)}, f32[512,128]{1,0:T(8,128)S(1)}, u32[]{:S(2)}, u32[]{:S(2)}) collective-permute-start(f32[512,128]{1,0:T(8,128)S(1)} %get-tuple-element.91.refs_0_.refs_21_.refs_2_.refs_5_), channel_id=1, source_target_pairs={{16,2},{2,16},{17,3},{3,17},{18,4},{4,18},{19,5},{5,19},{20,6},{6,... | collective-permute-start | bytes 786440 | tf_op jit(solution)/shard_map/ppermute | solution.py:467
  47.9 6.6 %collective-permute-start.13 = (f32[512,128]{1,0:T(8,128)S(1)}, f32[512,128]{1,0:T(8,128)S(1)}, u32[]{:S(2)}, u32[]{:S(2)}) collective-permute-start(f32[512,128]{1,0:T(8,128)S(1)} %get-tuple-element.92.refs_1_.refs_22_.refs_3_.refs_6_), channel_id=1, source_target_pairs={{0,16},{16,0},{1,17},{17,1},{2,18},{18,2},{3,19},{19,3},{4,20},{20... | collective-permute-start | bytes 786440 | tf_op jit(solution)/shard_map/ppermute | solution.py:464
  70.7 10.5 %collective-permute-start.16 = (f32[2,512,128]{2,1,0:T(8,128)S(1)}, f32[2,512,128]{2,1,0:T(8,128)S(1)}, u32[]{:S(2)}, u32[]{:S(2)}) collective-permute-start(f32[2,512,128]{2,1,0:T(8,128)S(1)} %get-tuple-element.119.refs_0_), channel_id=1, source_target_pairs={{16,1},{1,16},{18,3},{3,18},{20,5},{5,20},{22,7},{7,22},{24,9},{9,... | collective-permute-start | bytes 1572872 | tf_op jit(solution)/shard_map/ppermute | solution.py:461
  73.7 13.2 %collective-permute-start.14 = (f32[1,2,512,128]{3,2,1,0:T(8,128)S(1)}, f32[1,2,512,128]{3,2,1,0:T(8,128)S(1)}, u32[]{:S(2)}, u32[]{:S(2)}) collective-permute-start(f32[1,2,512,128]{3,2,1,0:T(8,128)S(1)} %shard_map.110.refs_0_), channel_id=1, source_target_pairs={{16,1},{1,16},{18,3},{3,18},{20,5},{5,20},{22,7},{7,22},{24,9},{9,... | collective-permute-start | bytes 1572872 | tf_op jit(solution)/shard_map/ppermute | solution.py:461
  76.6 11.1 %collective-permute-start.15 = (f32[2,512,128]{2,1,0:T(8,128)S(1)}, f32[2,512,128]{2,1,0:T(8,128)S(1)}, u32[]{:S(2)}, u32[]{:S(2)}) collective-permute-start(f32[2,512,128]{2,1,0:T(8,128)S(1)} %get-tuple-element.119.refs_0_), channel_id=1, source_target_pairs={{0,16},{16,0},{1,17},{17,1},{2,18},{18,2},{3,19},{19,3},{4,20},{20... | collective-permute-start | bytes 1572872 | tf_op jit(solution)/shard_map/ppermute | solution.py:569
  81.2 6.5 %collective-permute-start.17 = (f32[2,512,128]{2,1,0:T(8,128)S(1)}, f32[2,512,128]{2,1,0:T(8,128)S(1)}, u32[]{:S(2)}, u32[]{:S(2)}) collective-permute-start(f32[2,512,128]{2,1,0:T(8,128)S(1)} %collective-permute-done.16.refs_2_), channel_id=1, source_target_pairs={{0,16},{16,0},{1,17},{17,1},{2,18},{18,2},{3,19},{19,3},{4,20},{20... | collective-permute-start | bytes 1572872 | tf_op jit(solution)/shard_map/ppermute | solution.py:570

commit v6 on v5

--- a/solution.py
+++ b/solution.py
@@ -74,7 +74,7 @@
     return row_before(ref, start, count), row_after(ref, start, count), lane_before(here), lane_after(here)
 
 
-def native_kernel(width, first, count, place, pump_ref, obs_ref, data_ref, storage_ref, mask_ref, head_ref, later_ref, pack_ref):
+def native_kernel(width, first, count, place, pump_ref, obs_ref, data_ref, storage_ref, mask_ref, head_ref, later_ref, pack_ref, *copies):
     rows, depth = storage_ref.shape[1:]
     lane = lax.broadcasted_iota(jnp.int32, (min(CHUNK, rows), depth), 1)
     row = lax.broadcasted_iota(jnp.int32, (min(CHUNK, rows), depth), 0)
@@ -88,6 +88,10 @@
             well = jnp.where(row * depth + lane + (at * rows + r) * depth == pump_ref[0] - place[0], WELL_TERM, 0.0)
             out_ref[k, part] = jnp.where(active, store + well, 0.0)
             out_ref[k + 1, part] = jnp.where(active, store * later_ref[0, at, part], 0.0)
+    for copy in copies:
+        for i in range(copy.shape[1]):
+            for r, n in chunks_of(rows):
+                copy[0, i, r : r + n] = head_ref[0, i, r : r + n]
     lanes = lax.broadcasted_iota(jnp.int32, (1, depth), 1)
 
     def observe(o):
@@ -389,19 +393,13 @@
     weigh([plane_at(i, width, place[3]) for i in range(width)], [coef_ref[8 * k : 8 * k + 8] for k in range(3)], fields, store)
 
 
-def adjoint_kernel(place, kept, moved, out_ref):
-    for i in range(out_ref.shape[1]):
-        for r, n in chunks_of(out_ref.shape[2]):
-            part = slice(r, r + n)
-            out_ref[0, i, part] = pick(place, kept[0, i, part], moved[0, i, part])
-
-
-def add_kernel(place, own_ref, beside_ref, other_ref, handed_ref, out_ref):
-    for i in range(out_ref.shape[0]):
-        for r, n in chunks_of(out_ref.shape[1]):
+def deliver_kernel(place, own_ref, beside_ref, other_ref, handed_ref, kept_ref, moved_ref, gradient_ref, adjoint_ref):
+    for i in range(gradient_ref.shape[0]):
+        for r, n in chunks_of(gradient_ref.shape[1]):
             part = slice(r, r + n)
             here = pick(place, own_ref[i, part], beside_ref[i, part])
-            out_ref[i, part] = here + pick(place, handed_ref[i, part], other_ref[i, part])
+            gradient_ref[i, part] = here + pick(place, handed_ref[i, part], other_ref[i, part])
+            adjoint_ref[0, i, part] = pick(place, kept_ref[0, i, part], moved_ref[0, i, part])
 
 
 BOTH = ("test", "slab")
@@ -476,16 +474,15 @@
     far_plane = lambda x: lax.dynamic_slice(x, (far_at, 0, 0), (1, rows, depth))[0]
     log_moved = move(log_conductivity)
     def native(first, count):
-        (pack,) = call(
+        return call(
             lambda *refs: native_kernel(width, first, count, position(), *refs),
             [pump_cells, obs_cells, obs_data[0], storage, active_mask, heads, adjoint_next],
-            [(2 * count, rows, depth)],
+            [(2 * count, rows, depth)] + [(1, *stack)] * (first > 0),
             scalars=3,
             space=pltpu.HBM,
         )
-        return pack
-
-    far_pack, near_pack = native(0, 1), native(1, width - 1)
+
+    (far_pack,), (near_pack, heads_here) = native(0, 1), native(1, width - 1)
     far_moved = move(far_pack)
     log_halo = lax.ppermute(after(far_plane(log_conductivity), far_pack), far_axis, first_far)
     cond = call(
@@ -521,10 +518,10 @@
         fields += field
         image = call(lambda *refs: inner_kernel(width, *refs), [*field, *own, *faces], planes, cost=(1 << 23) if step == 1 else COST)
         if step == HEADS_STEP:
-            heads_moved = move(after(heads, *image))
+            heads_moved = move(after(heads_here, *image))
         if step == 1:
             heads_moved = after(heads_moved, *image)
-            head = call(lambda *refs: head_kernel(width, position(), *refs), [heads, heads_moved], planes, space=None)
+            head = call(lambda *refs: head_kernel(width, position(), *refs), [heads_here, heads_moved], planes, space=None)
             head_far, head_near = swap_far(head[0]), swap_near(head[-1])
         if step < 2:
             halos += halo
@@ -568,15 +565,10 @@
         other = move(gradient)
         beside = lax.ppermute(gradient, "test", near)
         handed = lax.ppermute(other, "test", near)
-        (gradient,) = call(
-            lambda *refs: add_kernel(position(), *refs),
-            [gradient, beside, other, handed],
-            [jax.ShapeDtypeStruct(stack, jnp.float32)],
-        )
-        (adjoint,) = call(
-            lambda *refs: adjoint_kernel(position(), *refs),
-            [adjoint, move(adjoint)],
-            [jax.ShapeDtypeStruct((1, *stack), jnp.float32)],
+        gradient, adjoint = call(
+            lambda *refs: deliver_kernel(position(), *refs),
+            [gradient, beside, other, handed, adjoint, move(adjoint)],
+            [jax.ShapeDtypeStruct(shape, jnp.float32) for shape in (stack, (1, *stack))],
         )
     else:
         gradient = lax.psum(gradient, "test")

time: 89.2 us -> 87.9 us (0.985)
    pallas_call x18 -> x17, Pallas kernels: 14.5 us -> 13.9 us  [call(): pl.pallas_call(kernel, out_shape=out_shape, in_specs=[pl.BlockSpec(memory...]
  transfers between devices with their start and end apart: 18 -> 18, of which waited for: 9 -> 11; matrix products, arithmetic and copies ran while one was open for 0% -> 0% of each run, Pallas kernels for 12% -> 12%
where the time goes in v6:
time: 87.9 us; the launch traced here: 87.4 us
  starting transfers between devices  37.3 us (42%)
  waiting for transfers between devices  21 us (24%)
  Pallas kernels  13.9 us (16%)
  blocking collectives  13.6 us (15%)
  between operations  1.55 us (2%)
    ppermute x6, starting transfers between devices, move(): return lax.ppermute(x, BOTH, both_ways(pairs)) if turned else x  18.4 us
    ppermute x4, starting transfers between devices, swap_far(): return lax.ppermute(x, far_axis, both_ways(far_pairs))  17.1 us
    ppermute x6, waiting for transfers between devices, move(): return lax.ppermute(x, BOTH, both_ways(pairs)) if turned else x  14.3 us
    pallas_call x17, Pallas kernels, call(): pl.pallas_call(kernel, out_shape=out_shape, in_specs=[pl.BlockSpec(memory...  13.9 us
    all_to_all x1, blocking collectives, on_device(): lax.all_to_all(told, far_axis, 0, 0, axis_index_groups=same_test, tiled=T...  13.6 us
    ppermute x4, waiting for transfers between devices, swap_far(): return lax.ppermute(x, far_axis, both_ways(far_pairs))  4.32 us
  transfers between devices with their start and end apart: 18, of which 11 were waited for; matrix products, arithmetic and copies ran while one was open for 0% of the time, Pallas kernels for 12%

profile of v6, /device:TPU:1, one launch (start us, length us, event | category | flops | bytes accessed | tf_op | source)
XLA Modules:
  0.0 87.4 jit_solution(5874647143705921969)
XLA Ops:
  0.6 4.5 %collective-permute-start.2 = (f32[2,512,128]{2,1,0:T(8,128)}, f32[2,512,128]{2,1,0:T(8,128)S(1)}, u32[]{:S(2)}, u32[]{:S(2)}) collective-permute-start(f32[2,512,128]{2,1,0:T(8,128)} %refs_0_.3), channel_id=1, source_target_pairs={{16,1},{1,16},{18,3},{3,18},{20,5},{5,20},{22,7},{7,22},{24,9},{9,... | collective-permute-start | bytes 1572872 | tf_op jit(solution)/shard_map/ppermute | solution.py:459
  5.8 2.3 %shard_map.95.refs_0_ = f32[2,512,128]{2,1,0:T(8,128)S(1)} custom-call(s32[1]{0:T(128)S(6)} %copy.10.refs_0_, s32[64]{0:T(128)} %refs_1_.3, f32[64]{0:T(128)} %bitcast.3, f32[2,512,128]{2,1,0:T(8,128)} %refs_3_.3, s32[2,512,128]{2,1,0:T(8,128)} %refs_4_.3, f32[1,2,512,128]{3,2,1,0:T(8,128)} %refs_5_.3, f32[1,2,512,128]{3,2,1,0:T(8,128)} %refs_6_.3), custom_call_target="tpu_custom_call" | custom-call | flops 1024 | bytes 1024 | tf_op jit(solution)/shard_map/pallas_call | solution.py:52
  8.2 1.3 %collective-permute-start.1 = (f32[512,128]{1,0:T(8,128)S(1)}, f32[512,128]{1,0:T(8,128)S(1)}, u32[]{:S(2)}, u32[]{:S(2)}) collective-permute-start(f32[512,128]{1,0:T(8,128)S(1)} %dynamic-slice_bitcast_fusion), channel_id=1, source_target_pairs={{2,16},{18,17},{1,2},{17,3},{4,18},{20,19},{3,4},{19,5},{6,20},{22... | collective-permute-start | bytes 786440 | tf_op jit(solution)/shard_map/ppermute | solution.py:487
  9.5 2.8 %collective-permute-start = (f32[2,512,128]{2,1,0:T(8,128)S(1)}, f32[2,512,128]{2,1,0:T(8,128)S(1)}, u32[]{:S(2)}, u32[]{:S(2)}) collective-permute-start(f32[2,512,128]{2,1,0:T(8,128)S(1)} %shard_map.95.refs_0_), channel_id=1, source_target_pairs={{16,1},{1,16},{18,3},{3,18},{20,5},{5,20},{22,7},{7,22},{24,9},{9,... | collective-permute-start | bytes 1572872 | tf_op jit(solution)/shard_map/ppermute | solution.py:459
  12.3 2.3 %shard_map.99 = (f32[2,512,128]{2,1,0:T(8,128)S(1)}, f32[1,2,512,128]{3,2,1,0:T(8,128)S(1)}) custom-call(s32[1]{0:T(128)S(6)} %copy.10.refs_0_, s32[64]{0:T(128)} %refs_1_.3, f32[64]{0:T(128)} %bitcast.4, f32[2,512,128]{2,1,0:T(8,128)} %refs_3_.3, s32[2,512,128]{2,1,0:T(8,128)} %refs_4_.3, f32[1,2,512,128]{3,2,1,0:T(8,128)} %refs_5_.3, ...), custom_call_target="tpu_custom_call" | custom-call | flops 1024 | bytes 1024 | tf_op jit(solution)/shard_map/pallas_call | solution.py:52
  14.7 1.2 %collective-permute-done.1.refs_2_ = f32[512,128]{1,0:T(8,128)S(1)} collective-permute-done((f32[512,128]{1,0:T(8,128)S(1)}, f32[512,128]{1,0:T(8,128)S(1)}, u32[]{:S(2)}, u32[]{:S(2)}) %collective-permute-start.1) | collective-permute-done | bytes 262176 | tf_op jit(solution)/shard_map/ppermute | solution.py:487
  15.9 1.9 %collective-permute-start.3 = (f32[2,512,128]{2,1,0:T(8,128)S(1)}, f32[2,512,128]{2,1,0:T(8,128)S(1)}, u32[]{:S(2)}, u32[]{:S(2)}) collective-permute-start(f32[2,512,128]{2,1,0:T(8,128)S(1)} %get-tuple-element.71.refs_0_), channel_id=1, source_target_pairs={{16,1},{1,16},{18,3},{3,18},{20,5},{5,20},{22,7},{7,22},{24,9},{9,... | collective-permute-start | bytes 1572872 | tf_op jit(solution)/shard_map/ppermute | solution.py:459
  17.9 0.5 shard_map.97
  18.4 2.3 %collective-permute-done.refs_1_ = f32[2,512,128]{2,1,0:T(8,128)S(1)} collective-permute-done((f32[2,512,128]{2,1,0:T(8,128)S(1)}, f32[2,512,128]{2,1,0:T(8,128)S(1)}, u32[]{:S(2)}, u32[]{:S(2)}) %collective-permute-start) | collective-permute-done | bytes 524320 | tf_op jit(solution)/shard_map/ppermute | solution.py:459
  20.8 4.1 %collective-permute-start.5 = (f32[520,128]{1,0:T(8,128)S(1)}, f32[520,128]{1,0:T(8,128)S(1)}, u32[]{:S(2)}, u32[]{:S(2)}) collective-permute-start(f32[520,128]{1,0:T(8,128)S(1)} %get-tuple-element.91), channel_id=1, source_target_pairs={{16,2},{2,16},{17,3},{3,17},{18,4},{4,18},{19,5},{5,19},{20,6},{6,... | collective-permute-start | bytes 798728 | tf_op jit(solution)/shard_map/ppermute | solution.py:465
  24.9 1.5 %collective-permute-done.3.refs_1_ = f32[2,512,128]{2,1,0:T(8,128)S(1)} collective-permute-done((f32[2,512,128]{2,1,0:T(8,128)S(1)}, f32[2,512,128]{2,1,0:T(8,128)S(1)}, u32[]{:S(2)}, u32[]{:S(2)}) %collective-permute-start.3) | collective-permute-done | bytes 524320 | tf_op jit(solution)/shard_map/ppermute | solution.py:459
  26.6 0.4 shard_map.101
  27.0 3.7 %collective-permute-start.9 = (f32[1,2,512,128]{3,2,1,0:T(8,128)S(1)}, f32[1,2,512,128]{3,2,1,0:T(8,128)S(1)}, u32[]{:S(2)}, u32[]{:S(2)}) collective-permute-start(f32[1,2,512,128]{3,2,1,0:T(8,128)S(1)} %get-tuple-element.101.refs_0_), channel_id=1, source_target_pairs={{16,1},{1,16},{18,3},{3,18},{20,5},{5,20},{22,7},{7,22},{24,9},{9,... | collective-permute-start | bytes 1572872 | tf_op jit(solution)/shard_map/ppermute | solution.py:459
  30.7 0.4 collective-permute-done.5.refs_8_.refs_23_
  31.1 1.2 %collective-permute-done.6.refs_9_.refs_24_ = f32[512,128]{1,0:T(8,128)S(1)} collective-permute-done((f32[512,128]{1,0:T(8,128)S(1)}, f32[512,128]{1,0:T(8,128)S(1)}, u32[]{:S(2)}, u32[]{:S(2)}) %collective-permute-start.6) | collective-permute-done | bytes 262176 | tf_op jit(solution)/shard_map/ppermute | solution.py:462
  32.4 4.2 %collective-permute-start.7 = (f32[512,128]{1,0:T(8,128)S(1)}, f32[512,128]{1,0:T(8,128)S(1)}, u32[]{:S(2)}, u32[]{:S(2)}) collective-permute-start(f32[512,128]{1,0:T(8,128)S(1)} %get-tuple-element.92.refs_0_.refs_2_.refs_19_.refs_3_), channel_id=1, source_target_pairs={{16,2},{2,16},{17,3},{3,17},{18,4},{4,18},{19,5},{5,19},{20,6},{6,... | collective-permute-start | bytes 786440 | tf_op jit(solution)/shard_map/ppermute | solution.py:465
  36.7 0.4 shard_map.103
  37.1 0.4 collective-permute-done.9.refs_1_
  37.6 4.5 %collective-permute-start.10 = (f32[512,128]{1,0:T(8,128)S(1)}, f32[512,128]{1,0:T(8,128)S(1)}, u32[]{:S(2)}, u32[]{:S(2)}) collective-permute-start(f32[512,128]{1,0:T(8,128)S(1)} %get-tuple-element.103.refs_2_), channel_id=1, source_target_pairs={{16,2},{2,16},{17,3},{3,17},{18,4},{4,18},{19,5},{5,19},{20,6},{6,... | collective-permute-start | bytes 786440 | tf_op jit(solution)/shard_map/ppermute | solution.py:465
  42.2 0.6 collective-permute-done.7.refs_8_.refs_25_
  43.0 4.4 %collective-permute-start.12 = (f32[512,128]{1,0:T(8,128)S(1)}, f32[512,128]{1,0:T(8,128)S(1)}, u32[]{:S(2)}, u32[]{:S(2)}) collective-permute-start(f32[512,128]{1,0:T(8,128)S(1)} %get-tuple-element.96.refs_0_.refs_21_.refs_2_.refs_5_), channel_id=1, source_target_pairs={{16,2},{2,16},{17,3},{3,17},{18,4},{4,18},{19,5},{5,19},{20,6},{6,... | collective-permute-start | bytes 786440 | tf_op jit(solution)/shard_map/ppermute | solution.py:465
  47.4 0.4 shard_map.105
  47.8 3.3 %collective-permute-done.10.refs_15_ = f32[512,128]{1,0:T(8,128)S(1)} collective-permute-done((f32[512,128]{1,0:T(8,128)S(1)}, f32[512,128]{1,0:T(8,128)S(1)}, u32[]{:S(2)}, u32[]{:S(2)}) %collective-permute-start.10) | collective-permute-done | bytes 262176 | tf_op jit(solution)/shard_map/ppermute | solution.py:465
  51.2 2.8 %shard_map.107 = (f32[512,128]{1,0:T(8,128)}, f32[512,128]{1,0:T(8,128)}, f32[512,128]{1,0:T(8,128)}, f32[512,128]{1,0:T(8,128)}, f32[512,128]{1,0:T(8,128)S(1)}...) custom-call(f32[512,128]{1,0:T(8,128)S(1)} %get-tuple-element.66.refs_0_.refs_3_, ...), custom_call_target="tpu_custom_call" | custom-call | flops 1024 | bytes 1024 | tf_op jit(solution)/shard_map/pallas_call | solution.py:52
  54.0 1.0 %shard_map.108 = (f32[16,8,128]{2,1,0:T(8,128)}, f32[512,128]{1,0:T(8,128)}, f32[512,128]{1,0:T(8,128)}) custom-call(f32[512,128]{1,0:T(8,128)S(1)} %get-tuple-element.98.refs_0_, f32[512,128]{1,0:T(8,128)S(1)} %get-tuple-element.99.refs_1_, f32[512,128]{1,0:T(8,128)S(1)} %get-tuple-element.96.refs_0_.refs_21_.refs_2_.refs_5_, ...), custom_call_target="tpu_custom_call" | custom-call | flops 1024 | bytes 16777216 | tf_op jit(solution)/shard_map/pallas_call | solution.py:52
  55.0 13.6 %all_to_all.5.refs_0_ = f32[16,8,128]{2,1,0:T(8,128)S(1)} all-to-all(f32[16,8,128]{2,1,0:T(8,128)} %get-tuple-element.117), channel_id=1, replica_groups={{0,2,4,6,8,10,12,14,16,18,20,22,24,26,28,30},{1,3,5,7,9,11,13,15,17,19,..., dimensions={0} | all-to-all | bytes 131072 | tf_op jit(solution)/shard_map/all_to_all | solution.py:546
  68.6 1.5 %shard_map.109 = (f32[2,512,128]{2,1,0:T(8,128)S(1)}, f32[24,128]{1,0:T(8,128)S(1)}) custom-call(f32[16,8,128]{2,1,0:T(8,128)S(1)} %all_to_all.5.refs_0_, f32[512,128]{1,0:T(8,128)} %get-tuple-element.118.refs_1_, f32[512,128]{1,0:T(8,128)} %get-tuple-element.119.refs_2_, f32[512,128]{1,0:T(8,128)} %get-tuple-element.120.refs_3_, ...), custom_call_target="tpu_custom_call" | custom-call | flops 1024 | bytes 1024 | tf_op jit(solution)/shard_map/pallas_call | solution.py:52
  70.1 2.7 %collective-permute-start.15 = (f32[2,512,128]{2,1,0:T(8,128)S(1)}, f32[2,512,128]{2,1,0:T(8,128)S(1)}, u32[]{:S(2)}, u32[]{:S(2)}) collective-permute-start(f32[2,512,128]{2,1,0:T(8,128)S(1)} %get-tuple-element.124.refs_0_), channel_id=1, source_target_pairs={{16,1},{1,16},{18,3},{3,18},{20,5},{5,20},{22,7},{7,22},{24,9},{9,... | collective-permute-start | bytes 1572872 | tf_op jit(solution)/shard_map/ppermute | solution.py:459
  73.2 2.9 %collective-permute-start.17 = (f32[1,2,512,128]{3,2,1,0:T(8,128)S(1)}, f32[1,2,512,128]{3,2,1,0:T(8,128)S(1)}, u32[]{:S(2)}, u32[]{:S(2)}) collective-permute-start(f32[1,2,512,128]{3,2,1,0:T(8,128)S(1)} %shard_map.110.refs_4_), channel_id=1, source_target_pairs={{16,1},{1,16},{18,3},{3,18},{20,5},{5,20},{22,7},{7,22},{24,9},{9,... | collective-permute-start | bytes 1572872 | tf_op jit(solution)/shard_map/ppermute | solution.py:459
  76.1 4.6 %collective-permute-done.15.refs_2_ = f32[2,512,128]{2,1,0:T(8,128)S(1)} collective-permute-done((f32[2,512,128]{2,1,0:T(8,128)S(1)}, f32[2,512,128]{2,1,0:T(8,128)S(1)}, u32[]{:S(2)}, u32[]{:S(2)}) %collective-permute-start.15) | collective-permute-done | bytes 524320 | tf_op jit(solution)/shard_map/ppermute | solution.py:459
  80.6 5.6 %collective-permute-done.17.refs_5_ = f32[1,2,512,128]{3,2,1,0:T(8,128)S(1)} collective-permute-done((f32[1,2,512,128]{3,2,1,0:T(8,128)S(1)}, f32[1,2,512,128]{3,2,1,0:T(8,128)S(1)}, u32[]{:S(2)}, u32[]{:S(2)}) %collective-permute-start.17) | collective-permute-done | bytes 524320 | tf_op jit(solution)/shard_map/ppermute | solution.py:459
  86.2 1.1 %shard_map.111 = (f32[2,512,128]{2,1,0:T(8,128)}, f32[1,2,512,128]{3,2,1,0:T(8,128)}) custom-call(f32[2,512,128]{2,1,0:T(8,128)S(1)} %get-tuple-element.124.refs_0_, f32[2,512,128]{2,1,0:T(8,128)S(1)} %collective-permute-done.14.refs_1_, f32[2,512,128]{2,1,0:T(8,128)S(1)} %collective-permute-done.15.refs_2_, ...), custom_call_target="tpu_custom_call" | custom-call | flops 1024 | bytes 1024 | tf_op jit(solution)/shard_map/pallas_call | solution.py:52
  (25 shorter events, 1.7 us)
Async XLA Ops:
  0.6 13.9 %collective-permute-start.2 = (f32[2,512,128]{2,1,0:T(8,128)}, f32[2,512,128]{2,1,0:T(8,128)S(1)}, u32[]{:S(2)}, u32[]{:S(2)}) collective-permute-start(f32[2,512,128]{2,1,0:T(8,128)} %refs_0_.3), channel_id=1, source_target_pairs={{16,1},{1,16},{18,3},{3,18},{20,5},{5,20},{22,7},{7,22},{24,9},{9,... | collective-permute-start | bytes 1572872 | tf_op jit(solution)/shard_map/ppermute | solution.py:459
  5.8 2.4 %copy-start = (f32[2,512,128]{2,1,0:T(8,128)S(1)}, f32[2,512,128]{2,1,0:T(8,128)}, u32[]{:S(2)}) copy-start(f32[2,512,128]{2,1,0:T(8,128)} %refs_0_.3) | copy-start | bytes 1572868
  8.2 7.7 %collective-permute-start.1 = (f32[512,128]{1,0:T(8,128)S(1)}, f32[512,128]{1,0:T(8,128)S(1)}, u32[]{:S(2)}, u32[]{:S(2)}) collective-permute-start(f32[512,128]{1,0:T(8,128)S(1)} %dynamic-slice_bitcast_fusion), channel_id=1, source_target_pairs={{2,16},{18,17},{1,2},{17,3},{4,18},{20,19},{3,4},{19,5},{6,20},{22... | collective-permute-start | bytes 786440 | tf_op jit(solution)/shard_map/ppermute | solution.py:487
  9.5 11.1 %collective-permute-start = (f32[2,512,128]{2,1,0:T(8,128)S(1)}, f32[2,512,128]{2,1,0:T(8,128)S(1)}, u32[]{:S(2)}, u32[]{:S(2)}) collective-permute-start(f32[2,512,128]{2,1,0:T(8,128)S(1)} %shard_map.95.refs_0_), channel_id=1, source_target_pairs={{16,1},{1,16},{18,3},{3,18},{20,5},{5,20},{22,7},{7,22},{24,9},{9,... | collective-permute-start | bytes 1572872 | tf_op jit(solution)/shard_map/ppermute | solution.py:459
  15.9 10.5 %collective-permute-start.3 = (f32[2,512,128]{2,1,0:T(8,128)S(1)}, f32[2,512,128]{2,1,0:T(8,128)S(1)}, u32[]{:S(2)}, u32[]{:S(2)}) collective-permute-start(f32[2,512,128]{2,1,0:T(8,128)S(1)} %get-tuple-element.71.refs_0_), channel_id=1, source_target_pairs={{16,1},{1,16},{18,3},{3,18},{20,5},{5,20},{22,7},{7,22},{24,9},{9,... | collective-permute-start | bytes 1572872 | tf_op jit(solution)/shard_map/ppermute | solution.py:459
  17.8 7.1 %collective-permute-start.4 = (f32[512,128]{1,0:T(8,128)S(1)}, f32[512,128]{1,0:T(8,128)S(1)}, u32[]{:S(2)}, u32[]{:S(2)}) collective-permute-start(f32[512,128]{1,0:T(8,128)S(1)} %get-tuple-element.67.refs_1_.refs_3_), channel_id=1, source_target_pairs={{0,16},{16,0},{1,17},{17,1},{2,18},{18,2},{3,19},{19,3},{4,20},{20... | collective-permute-start | bytes 786440 | tf_op jit(solution)/shard_map/ppermute | solution.py:462
  20.8 10.3 %collective-permute-start.5 = (f32[520,128]{1,0:T(8,128)S(1)}, f32[520,128]{1,0:T(8,128)S(1)}, u32[]{:S(2)}, u32[]{:S(2)}) collective-permute-start(f32[520,128]{1,0:T(8,128)S(1)} %get-tuple-element.91), channel_id=1, source_target_pairs={{16,2},{2,16},{17,3},{3,17},{18,4},{4,18},{19,5},{5,19},{20,6},{6,... | collective-permute-start | bytes 798728 | tf_op jit(solution)/shard_map/ppermute | solution.py:465
  27.0 10.5 %collective-permute-start.9 = (f32[1,2,512,128]{3,2,1,0:T(8,128)S(1)}, f32[1,2,512,128]{3,2,1,0:T(8,128)S(1)}, u32[]{:S(2)}, u32[]{:S(2)}) collective-permute-start(f32[1,2,512,128]{3,2,1,0:T(8,128)S(1)} %get-tuple-element.101.refs_0_), channel_id=1, source_target_pairs={{16,1},{1,16},{18,3},{3,18},{20,5},{5,20},{22,7},{7,22},{24,9},{9,... | collective-permute-start | bytes 1572872 | tf_op jit(solution)/shard_map/ppermute | solution.py:459
  30.7 1.6 %collective-permute-start.6 = (f32[512,128]{1,0:T(8,128)S(1)}, f32[512,128]{1,0:T(8,128)S(1)}, u32[]{:S(2)}, u32[]{:S(2)}) collective-permute-start(f32[512,128]{1,0:T(8,128)S(1)} %get-tuple-element.73.refs_1_.refs_3_.refs_18_.refs_2_), channel_id=1, source_target_pairs={{0,16},{16,0},{1,17},{17,1},{2,18},{18,2},{3,19},{19,3},{4,20},{20... | collective-permute-start | bytes 786440 | tf_op jit(solution)/shard_map/ppermute | solution.py:462
  32.4 10.3 %collective-permute-start.7 = (f32[512,128]{1,0:T(8,128)S(1)}, f32[512,128]{1,0:T(8,128)S(1)}, u32[]{:S(2)}, u32[]{:S(2)}) collective-permute-start(f32[512,128]{1,0:T(8,128)S(1)} %get-tuple-element.92.refs_0_.refs_2_.refs_19_.refs_3_), channel_id=1, source_target_pairs={{16,2},{2,16},{17,3},{3,17},{18,4},{4,18},{19,5},{5,19},{20,6},{6,... | collective-permute-start | bytes 786440 | tf_op jit(solution)/shard_map/ppermute | solution.py:465
  36.6 6.1 %collective-permute-start.8 = (f32[512,128]{1,0:T(8,128)S(1)}, f32[512,128]{1,0:T(8,128)S(1)}, u32[]{:S(2)}, u32[]{:S(2)}) collective-permute-start(f32[512,128]{1,0:T(8,128)S(1)} %get-tuple-element.93.refs_1_.refs_3_.refs_20_.refs_4_), channel_id=1, source_target_pairs={{0,16},{16,0},{1,17},{17,1},{2,18},{18,2},{3,19},{19,3},{4,20},{20... | collective-permute-start | bytes 786440 | tf_op jit(solution)/shard_map/ppermute | solution.py:462
  37.6 13.6 %collective-permute-start.10 = (f32[512,128]{1,0:T(8,128)S(1)}, f32[512,128]{1,0:T(8,128)S(1)}, u32[]{:S(2)}, u32[]{:S(2)}) collective-permute-start(f32[512,128]{1,0:T(8,128)S(1)} %get-tuple-element.103.refs_2_), channel_id=1, source_target_pairs={{16,2},{2,16},{17,3},{3,17},{18,4},{4,18},{19,5},{5,19},{20,6},{6,... | collective-permute-start | bytes 786440 | tf_op jit(solution)/shard_map/ppermute | solution.py:465
  42.1 9.1 %collective-permute-start.11 = (f32[512,128]{1,0:T(8,128)S(1)}, f32[512,128]{1,0:T(8,128)S(1)}, u32[]{:S(2)}, u32[]{:S(2)}) collective-permute-start(f32[512,128]{1,0:T(8,128)S(1)} %get-tuple-element.104.refs_3_), channel_id=1, source_target_pairs={{0,16},{16,0},{1,17},{17,1},{2,18},{18,2},{3,19},{19,3},{4,20},{20... | collective-permute-start | bytes 786440 | tf_op jit(solution)/shard_map/ppermute | solution.py:462
  43.0 11.0 %collective-permute-start.12 = (f32[512,128]{1,0:T(8,128)S(1)}, f32[512,128]{1,0:T(8,128)S(1)}, u32[]{:S(2)}, u32[]{:S(2)}) collective-permute-start(f32[512,128]{1,0:T(8,128)S(1)} %get-tuple-element.96.refs_0_.refs_21_.refs_2_.refs_5_), channel_id=1, source_target_pairs={{16,2},{2,16},{17,3},{3,17},{18,4},{4,18},{19,5},{5,19},{20,6},{6,... | collective-permute-start | bytes 786440 | tf_op jit(solution)/shard_map/ppermute | solution.py:465
  47.4 6.6 %collective-permute-start.13 = (f32[512,128]{1,0:T(8,128)S(1)}, f32[512,128]{1,0:T(8,128)S(1)}, u32[]{:S(2)}, u32[]{:S(2)}) collective-permute-start(f32[512,128]{1,0:T(8,128)S(1)} %get-tuple-element.97.refs_1_.refs_22_.refs_3_.refs_6_), channel_id=1, source_target_pairs={{0,16},{16,0},{1,17},{17,1},{2,18},{18,2},{3,19},{19,3},{4,20},{20... | collective-permute-start | bytes 786440 | tf_op jit(solution)/shard_map/ppermute | solution.py:462
  70.1 10.5 %collective-permute-start.15 = (f32[2,512,128]{2,1,0:T(8,128)S(1)}, f32[2,512,128]{2,1,0:T(8,128)S(1)}, u32[]{:S(2)}, u32[]{:S(2)}) collective-permute-start(f32[2,512,128]{2,1,0:T(8,128)S(1)} %get-tuple-element.124.refs_0_), channel_id=1, source_target_pairs={{16,1},{1,16},{18,3},{3,18},{20,5},{5,20},{22,7},{7,22},{24,9},{9,... | collective-permute-start | bytes 1572872 | tf_op jit(solution)/shard_map/ppermute | solution.py:459
  72.8 13.5 %collective-permute-start.14 = (f32[2,512,128]{2,1,0:T(8,128)S(1)}, f32[2,512,128]{2,1,0:T(8,128)S(1)}, u32[]{:S(2)}, u32[]{:S(2)}) collective-permute-start(f32[2,512,128]{2,1,0:T(8,128)S(1)} %get-tuple-element.124.refs_0_), channel_id=1, source_target_pairs={{0,16},{16,0},{1,17},{17,1},{2,18},{18,2},{3,19},{19,3},{4,20},{20... | collective-permute-start | bytes 1572872 | tf_op jit(solution)/shard_map/ppermute | solution.py:566
  73.2 13.1 %collective-permute-start.17 = (f32[1,2,512,128]{3,2,1,0:T(8,128)S(1)}, f32[1,2,512,128]{3,2,1,0:T(8,128)S(1)}, u32[]{:S(2)}, u32[]{:S(2)}) collective-permute-start(f32[1,2,512,128]{3,2,1,0:T(8,128)S(1)} %shard_map.110.refs_4_), channel_id=1, source_target_pairs={{16,1},{1,16},{18,3},{3,18},{20,5},{5,20},{22,7},{7,22},{24,9},{9,... | collective-permute-start | bytes 1572872 | tf_op jit(solution)/shard_map/ppermute | solution.py:459
  80.6 5.6 %collective-permute-start.16 = (f32[2,512,128]{2,1,0:T(8,128)S(1)}, f32[2,512,128]{2,1,0:T(8,128)S(1)}, u32[]{:S(2)}, u32[]{:S(2)}) collective-permute-start(f32[2,512,128]{2,1,0:T(8,128)S(1)} %collective-permute-done.15.refs_2_), channel_id=1, source_target_pairs={{0,16},{16,0},{1,17},{17,1},{2,18},{18,2},{3,19},{19,3},{4,20},{20... | collective-permute-start | bytes 1572872 | tf_op jit(solution)/shard_map/ppermute | solution.py:567
